TPU v7x, 256 devices: a whole 4x4x8 slice. The times are simulated.
256 devices in a mesh: grp: 2 (over z_hi), tile: 32 (over x, y, core), lev: 4 (over z_lo).
Axes of the slice: x: 4, y: 4, z: 8 (z_hi: 2, z_lo: 4; z = z_hi * 4 + z_lo), core: 2. Of those that a mesh axis runs over, the one named last changes fastest.
Arguments:
- members: bfloat16 [16, 8, 1536, 3072], P('grp', 'lev', 'tile'), may hold values from -6 to 6
- obs_value: float32 [8, 1536, 3072], P('lev', 'tile'), may hold values from -6 to 6
- obs_count: int32 [1536, 3072], P('tile'), may hold values from 0 to 4
- variance: float32 [8, 768], P('lev'), may hold values from 0.1 to 4
- wave_order: int32 [768], replicated, may hold values from 0 to 767, each once
Outputs:
- recentered: bfloat16 [16, 8, 1536, 3072], P('grp', 'lev', 'tile')
- control: float32 [4, 2, 2, 768, 768], P('lev', 'grp', None, 'tile')
Inputs may be any that keep to these rules, and one draw needn't show every extreme that they name: `wave_order`: each wavenumber 0 to 767 stands in exactly one slot.
All inputs are finite; a program needn't handle non-finite values.
Results may differ from a plain program's by a relative error of at most 0.001.
Values sent between devices are 32-bit elements; how exact they have to be, the bound alone decides.
No kernel may reach another device: no remote copies, remote signals or barrier semaphores. Data moves between devices by JAX's collectives and lax.ppermute only.
A program may use at most 128 MiB of HBM per device.

v0:
```python
import math

import jax
import jax.numpy as jnp
from jax import lax
from jax.sharding import PartitionSpec as P

MEM = 16
ITERS = 2


SPREAD_FACTOR = 1.2
HIGH = lax.Precision.HIGHEST


def zonal_basis(wave_order, lon_count):
    positions = jnp.arange(lon_count, dtype=jnp.int32)
    turn_index = wave_order[:, None] * positions[None, :] % lon_count
    angles = turn_index.astype(jnp.float32) * (2.0 * math.pi / lon_count)
    factor = math.sqrt(2.0 / lon_count)
    return jnp.stack([jnp.cos(angles), jnp.sin(angles)]) * factor


def latitude_basis(degrees, lat_rows):
    degree_index = jnp.arange(degrees, dtype=jnp.int32)
    odd_rows = 2 * jnp.arange(lat_rows, dtype=jnp.int32) + 1
    turn_index = degree_index[:, None] * odd_rows[None, :] % (4 * lat_rows)
    angles = turn_index.astype(jnp.float32) * (math.pi / (2.0 * lat_rows))
    return jnp.cos(angles) * math.sqrt(2.0 / lat_rows)


def squares(vector):
    return lax.psum(jnp.sum(vector * vector), ("grp", "tile", "lev"))


def on_device(members, obs_value, obs_count, variance, wave_order):
    var_level = lax.axis_index("grp")
    tile_count = lax.axis_size("tile")
    lat_band = members.shape[2]
    lon_count = members.shape[3]
    slot_count = wave_order.shape[0]
    own_slots = slot_count // tile_count
    degrees = variance.shape[1]
    zonal_rows = zonal_basis(wave_order, lon_count)
    latitude = latitude_basis(degrees, lat_band * tile_count)
    own_waves = lax.dynamic_slice_in_dim(
        wave_order, lax.axis_index("tile") * own_slots, own_slots, 0
    )
    own_variance = lax.dynamic_index_in_dim(variance, var_level, 0, keepdims=False)
    live_mask = jnp.arange(degrees, dtype=jnp.int32)[None, :] >= own_waves[:, None]
    spec_scale = jnp.where(live_mask, jnp.sqrt(own_variance)[None, :], jnp.float32(0.0))
    member_sum = jnp.sum(members, axis=0, dtype=jnp.float32)
    paired_mean = lax.psum(member_sum, "grp") / MEM
    own_mean = lax.dynamic_index_in_dim(paired_mean, var_level, 0, keepdims=False)
    weights = obs_count.astype(jnp.float32) * 0.5
    own_obs = lax.dynamic_index_in_dim(obs_value, var_level, 0, keepdims=False)

    def project(arrived):
        values = jnp.einsum("csj,nj->csn", arrived, latitude, precision=HIGH)
        return values * spec_scale[None]

    def to_spectral(grid_field):
        coeffs = jnp.einsum("csi,ji->csj", zonal_rows, grid_field, precision=HIGH)
        return project(lax.all_to_all(coeffs, "tile", split_axis=1, concat_axis=2, tiled=True))

    rhs = to_spectral(weights * (own_obs - own_mean))
    control = jnp.zeros_like(rhs)
    analysis_increment = jnp.zeros_like(own_mean)
    residual = rhs
    direction = rhs
    norm_now = squares(residual)
    for solver_iteration in range(ITERS):
        lat_values = jnp.einsum(
            "csn,nj->csj", direction * spec_scale[None], latitude, precision=HIGH
        )
        band_values = lax.all_to_all(lat_values, "tile", split_axis=2, concat_axis=1, tiled=True)
        field_now = jnp.einsum("csj,csi->ji", band_values, zonal_rows, precision=HIGH)
        image_vec = direction + to_spectral(weights * field_now)
        curve = lax.psum(jnp.sum(direction * image_vec), ("grp", "tile", "lev"))
        step_len = norm_now / curve
        control = control + step_len * direction
        analysis_increment = analysis_increment + step_len * field_now
        residual = residual - step_len * image_vec
        norm_next = squares(residual)
        direction = residual + norm_next / norm_now * direction
        norm_now = norm_next
    paired_increment = lax.all_gather(analysis_increment[None], "grp", axis=0, tiled=True)
    member_offset = paired_mean + paired_increment - SPREAD_FACTOR * paired_mean
    recentered = (SPREAD_FACTOR * members.astype(jnp.float32) + member_offset[None]).astype(
        jnp.bfloat16
    )
    return (recentered, control[None, None])


def solution(mesh):
    placed = (
        P("grp", "lev", "tile", None),
        P("lev", "tile", None),
        P("tile", None),
        P("lev", None),
        P(),
    )
    return jax.shard_map(
        on_device,
        mesh=mesh,
        in_specs=placed,
        out_specs=(P("grp", "lev", "tile", None), P("lev", "grp", None, "tile", None)),
        check_vma=False,
    )
```

profile of v0, /device:TPU:32, one launch (start us, length us, event | category | flops | bytes accessed | tf_op | source)
XLA Modules:
  0.0 691.9 jit_solution(10514851538526068287)
XLA Ops:
  7.2 4.3 convert_reduce_fusion
  11.7 41.2 %fusion.7 = (f32[1,768,3072]{2,1,0:T(8,128)}, f32[1,768,3072]{2,1,0:T(8,128)}) fusion(s32[768]{0:T(1024)S(1)} %copy-done.10), kind=kLoop, calls=%fused_computation.12 | loop fusion | flops 21233664 | bytes 18877440 | tf_op jit(solution)/shard_map/cos | solution.py:21
  52.9 44.2 %all-reduce.3.cloned.1.call-done = f32[2,48,3072]{2,1,0:T(8,128)} async-done(((f32[2,48,3072]{2,1,0:T(8,128)}), f32[2,48,3072]{2,1,0:T(8,128)}) %all-reduce.3.cloned.1.call-update) | async-done | bytes 1179664 | tf_op jit(solution)/shard_map/psum | solution.py:53
  98.5 21.6 %fusion.72 = f32[2,768,48]{1,2,0:T(8,128)S(1)} fusion(f32[1,768,3072]{2,1,0:T(8,128)} %get-tuple-element.7, f32[1,768,3072]{2,1,0:T(8,128)} %get-tuple-element.6, f32[2,48,3072]{2,1,0:T(8,128)S(1)} %broadcast_multiply_fusion, s32[]{:T(128)S(6)} %select_n.51, f32[2,48,3072]{2,1,0:T(8,128)S(1)} %copy-done.7, s32[48,3072]{1,0:T(8,128)S(1)} %copy-done), kind=kOutput, calls=%fused_computation.60 | convolution fusion | flops 2727936000 | bytes 20938756 | tf_op jit(solution)/shard_map/csi,ji->csj/dot_general | solution.py:63
  122.7 7.1 %all-to-all-start = ((f32[32,1,2304]{2,1,0:T(1,128)}), f32[32,1,2304]{2,1,0:T(1,128)S(1)}, u32[]{:S(2)}, u32[]{:S(2)}) async-start(f32[32,1,2304]{2,1,0:T(1,128)} %reshape.132), calls=%async_computation | async-start | bytes 589824 | tf_op jit(solution)/shard_map/all_to_all | solution.py:64
  129.9 9.0 %all-to-all-done = f32[32,1,2304]{2,1,0:T(1,128)S(1)} async-done(((f32[32,1,2304]{2,1,0:T(1,128)}), f32[32,1,2304]{2,1,0:T(1,128)S(1)}, u32[]{:S(2)}, u32[]{:S(2)}) %all-to-all-start) | async-done | bytes 294944 | tf_op jit(solution)/shard_map/all_to_all | solution.py:64
  142.8 22.6 %fusion.52 = f32[2,24,768]{2,1,0:T(8,128)S(1)} fusion(f32[2,24,1536]{2,1,0:T(8,128)S(1)} %all_to_all.68, s32[1536]{0:T(1024)S(1)} %multiply_add_fusion.2, f32[24,768]{1,0:T(8,128)S(1)} %fusion.91), kind=kOutput, calls=%fused_computation.52 | convolution fusion | flops 691310592 | bytes 522240 | tf_op jit(solution)/shard_map/csj,nj->csn/dot_general | solution.py:59
  166.1 20.8 %fusion.22 = f32[2,24,1536]{2,1,0:T(8,128)S(1)} fusion(s32[1536]{0:T(1024)S(1)} %multiply_add_fusion.2, f32[2,24,768]{2,1,0:T(8,128)S(1)} %fusion.52, f32[24,768]{1,0:T(8,128)S(1)} %fusion.91), kind=kOutput, calls=%fused_computation.26 | convolution fusion | flops 691310592 | bytes 522240 | tf_op jit(solution)/shard_map/csn,nj->csj/dot_general | solution.py:73
  190.5 13.2 %all_to_all.90 = f32[32,1,2304]{2,1,0:T(1,128)S(1)} all-to-all(f32[32,1,2304]{2,1,0:T(1,128)S(1)} %reshape.134), channel_id=1, replica_groups=mesh['grp'=2,'tile'=32,'lev'=4] {'tile'}, dimensions={0} | all-to-all | bytes 589824 | tf_op jit(solution)/shard_map/all_to_all | solution.py:76
  210.0 15.5 %convolution_bitcast_fusion.1 = f32[48,3072]{1,0:T(8,128)S(1)} fusion(f32[2,768,48]{2,1,0:T(8,128)} %bitcast.90, f32[1,768,3072]{2,1,0:T(8,128)} %get-tuple-element.7, f32[1,768,3072]{2,1,0:T(8,128)} %get-tuple-element.6), kind=kOutput, calls=%fused_computation.30 | convolution fusion | flops 2727346176 | bytes 19759104 | tf_op jit(solution)/shard_map/csj,csi->ji/dot_general | solution.py:77
  225.5 20.9 %fusion.71 = f32[2,768,48]{1,2,0:T(8,128)S(1)} fusion(f32[1,768,3072]{2,1,0:T(8,128)} %get-tuple-element.7, f32[1,768,3072]{2,1,0:T(8,128)S(1)} %bitcast.83, f32[48,3072]{1,0:T(8,128)S(1)} %convolution_bitcast_fusion.1, s32[48,3072]{1,0:T(8,128)S(1)} %copy-done), kind=kOutput, calls=%fused_computation.59 | convolution fusion | flops 2727788544 | bytes 20348928 | tf_op jit(solution)/shard_map/csi,ji->csj/dot_general | solution.py:63
  248.4 12.7 %all_to_all.91 = f32[32,1,2304]{2,1,0:T(1,128)S(1)} all-to-all(f32[32,1,2304]{2,1,0:T(1,128)S(1)} %reshape.136), channel_id=1, replica_groups=mesh['grp'=2,'tile'=32,'lev'=4] {'tile'}, dimensions={0} | all-to-all | bytes 589824 | tf_op jit(solution)/shard_map/all_to_all | solution.py:64
  264.5 23.0 %multiply_reduce_fusion.1 = (f32[]{:T(128)}, f32[]{:T(128)}, f32[2,24,768]{2,1,0:T(8,128)S(1)}) fusion(f32[2,24,768]{2,1,0:T(8,128)S(1)} %copy-done.5, f32[24,768]{1,0:T(8,128)S(1)} %copy-done.9, f32[2,24,1536]{2,1,0:T(8,128)S(1)} %all_to_all.76, s32[1536]{0:T(1024)S(1)} %multiply_add_fusion.2), kind=kOutput, calls=%fused_computation.82 | convolution fusion | flops 691494912 | bytes 669704 | tf_op jit(solution)/shard_map/csj,nj->csn/dot_general | solution.py:59
  287.5 75.0 %all-reduce = (f32[]{:T(128)}, f32[]{:T(128)}) all-reduce(f32[]{:T(128)} %get-tuple-element.3, f32[]{:T(128)} %get-tuple-element.2), channel_id=1, replica_groups=mesh['grp'=2,'tile'=32,'lev'=4] {'grp','tile','lev'}, use_global_device_ids=true, to_apply=%region_3.4 | all-reduce | flops 2 | bytes 16 | tf_op jit(solution)/shard_map/psum | solution.py:33
  364.4 72.8 %psum.38 = f32[]{:T(128)} all-reduce(f32[]{:T(128)} %multiply_reduce_fusion), channel_id=1, replica_groups=mesh['grp'=2,'tile'=32,'lev'=4] {'grp','tile','lev'}, use_global_device_ids=true, to_apply=%region_7.8 | all-reduce | flops 1 | bytes 8 | tf_op jit(solution)/shard_map/psum | solution.py:33
  438.4 20.9 %fusion.18 = f32[2,24,1536]{2,1,0:T(8,128)S(1)} fusion(s32[1536]{0:T(1024)S(1)} %multiply_add_fusion.2, f32[24,768]{1,0:T(8,128)S(1)} %copy-done.9, f32[2,24,768]{2,1,0:T(8,128)S(1)} %copy-done.5, f32[2,24,768]{2,1,0:T(8,128)S(1)} %get-tuple-element.8, f32[]{:T(128)S(6)} %div.18, f32[]{:T(128)S(6)} %div.17), kind=kOutput, calls=%fused_computation.24 | convolution fusion | flops 691458048 | bytes 669704 | tf_op jit(solution)/shard_map/csn,nj->csj/dot_general | solution.py:73
  462.9 13.7 %all_to_all.92 = f32[32,1,2304]{2,1,0:T(1,128)S(1)} all-to-all(f32[32,1,2304]{2,1,0:T(1,128)S(1)} %reshape.138), channel_id=1, replica_groups=mesh['grp'=2,'tile'=32,'lev'=4] {'tile'}, dimensions={0} | all-to-all | bytes 589824 | tf_op jit(solution)/shard_map/all_to_all | solution.py:76
  483.0 15.5 %convolution_bitcast_fusion = f32[48,3072]{1,0:T(8,128)S(1)} fusion(f32[2,768,48]{2,1,0:T(8,128)} %bitcast.91, f32[1,768,3072]{2,1,0:T(8,128)} %get-tuple-element.7, f32[1,768,3072]{2,1,0:T(8,128)} %get-tuple-element.6), kind=kOutput, calls=%fused_computation.29 | convolution fusion | flops 2727346176 | bytes 19759104 | tf_op jit(solution)/shard_map/csj,csi->ji/dot_general | solution.py:77
  498.5 20.6 %fusion.70 = f32[2,768,48]{1,2,0:T(8,128)S(1)} fusion(f32[1,768,3072]{2,1,0:T(8,128)} %get-tuple-element.7, f32[1,768,3072]{2,1,0:T(8,128)S(1)} %bitcast.85, f32[48,3072]{1,0:T(8,128)S(1)} %convolution_bitcast_fusion, s32[48,3072]{1,0:T(8,128)S(1)} %copy-done), kind=kOutput, calls=%fused_computation.58 | convolution fusion | flops 2727788544 | bytes 20348928 | tf_op jit(solution)/shard_map/csi,ji->csj/dot_general | solution.py:63
  521.5 12.7 %all_to_all.93 = f32[32,1,2304]{2,1,0:T(1,128)S(1)} all-to-all(f32[32,1,2304]{2,1,0:T(1,128)S(1)} %reshape.140), channel_id=1, replica_groups=mesh['grp'=2,'tile'=32,'lev'=4] {'tile'}, dimensions={0} | all-to-all | bytes 589824 | tf_op jit(solution)/shard_map/all_to_all | solution.py:64
  537.5 25.0 %fusion.81 = f32[]{:T(128)} fusion(f32[2,24,1536]{2,1,0:T(8,128)S(1)} %all_to_all.84, s32[1536]{0:T(1024)S(1)} %multiply_add_fusion.2, f32[24,768]{1,0:T(8,128)S(1)} %copy-done.9, f32[2,24,768]{2,1,0:T(8,128)S(1)} %copy-done.6, f32[]{:T(128)S(6)} %div.18, f32[2,24,768]{2,1,0:T(8,128)S(1)} %get-tuple-element.8, f32[]{:T(128)S(6)} %div.17), kind=kOutput, calls=%fused_computation.73 | convolution fusion | flops 691568640 | bytes 669708 | tf_op jit(solution)/shard_map/csj,nj->csn/dot_general | solution.py:59
  562.5 74.2 %psum.39 = f32[]{:T(128)} all-reduce(f32[]{:T(128)} %fusion.81), channel_id=1, replica_groups=mesh['grp'=2,'tile'=32,'lev'=4] {'grp','tile','lev'}, use_global_device_ids=true, to_apply=%region_9.10 | all-reduce | flops 1 | bytes 8 | tf_op jit(solution)/shard_map/psum | solution.py:79
  639.6 38.0 %all-gather.3.cloned.1.call-done = f32[96,3072]{1,0:T(8,128)} async-done(((f32[48,3072]{1,0:T(8,128)}), f32[96,3072]{1,0:T(8,128)}) %all-gather.3.cloned.1.call-update) | async-done | bytes 1179664 | tf_op jit(solution)/shard_map/all_gather | solution.py:87
  679.0 5.8 fusion.1
  (83 shorter events, 42.9 us)
Async XLA Ops:
  7.2 4.4 copy-start.10
  7.2 4.5 copy-start.11
  7.2 89.9 %all-reduce.3.cloned.1.call-start = ((), (), s32[]{:S(2)}) async-start(), calls=%async_computation.5 | async-start | bytes 2359296 | tf_op jit(solution)/shard_map/psum | solution.py:53
  11.7 86.8 %copy-start = (s32[48,3072]{1,0:T(8,128)S(1)}, s32[48,3072]{1,0:T(8,128)}, u32[]{:S(2)}) copy-start(s32[48,3072]{1,0:T(8,128)} %param.7) | copy-start | bytes 1769476
  11.7 86.8 %copy-start.7 = (f32[2,48,3072]{2,1,0:T(8,128)S(1)}, f32[2,48,3072]{2,1,0:T(8,128)}, u32[]{:S(2)}) copy-start(f32[2,48,3072]{2,1,0:T(8,128)} %param.6) | copy-start | bytes 3538948
  122.7 16.3 %all-to-all-start = ((f32[32,1,2304]{2,1,0:T(1,128)}), f32[32,1,2304]{2,1,0:T(1,128)S(1)}, u32[]{:S(2)}, u32[]{:S(2)}) async-start(f32[32,1,2304]{2,1,0:T(1,128)} %reshape.132), calls=%async_computation | async-start | bytes 589824 | tf_op jit(solution)/shard_map/all_to_all | solution.py:64
  129.8 547.8 %all-gather.3.cloned.1.call-start = ((), (), s32[]{:S(2)}) async-start(), calls=%async_computation.6 | async-start | bytes 1769472 | tf_op jit(solution)/shard_map/all_gather | solution.py:87
  129.9 35.5 %copy-start.8 = (f32[24,768]{1,0:T(8,128)}, f32[24,768]{1,0:T(8,128)S(1)}, u32[]{:S(2)}) copy-start(f32[24,768]{1,0:T(8,128)S(1)} %fusion.91) | copy-start | bytes 221188
  165.4 0.7 copy-start.4
  207.5 17.9 %slice-start = ((s8[9437184]{0:T(1024)(128)(4,1)}), s8[1048576]{0:T(1024)(128)(4,1)S(1)}, s32[]{:S(2)}) async-start(s8[9437184]{0:T(1024)(128)(4,1)} %bitcast.82), calls=%async_computation.7 | async-start | bytes 2097152
  210.0 15.5 %slice-start.1 = ((s8[9437184]{0:T(1024)(128)(4,1)}), s8[4194304]{0:T(1024)(128)(4,1)S(1)}, s32[]{:S(2)}) async-start(s8[9437184]{0:T(1024)(128)(4,1)} %bitcast.82), calls=%async_computation.8 | async-start | bytes 8388608
  210.0 15.5 %slice-start.2 = ((s8[9437184]{0:T(1024)(128)(4,1)}), s8[4194304]{0:T(1024)(128)(4,1)S(1)}, s32[]{:S(2)}) async-start(s8[9437184]{0:T(1024)(128)(4,1)} %bitcast.82), calls=%async_computation.9 | async-start | bytes 8388608
  225.5 20.9 %copy-start.1 = (f32[48,3072]{1,0:T(8,128)}, f32[48,3072]{1,0:T(8,128)S(1)}, u32[]{:S(2)}) copy-start(f32[48,3072]{1,0:T(8,128)S(1)} %convolution_bitcast_fusion.1) | copy-start | bytes 1769476
  246.4 18.0 %copy-start.5 = (f32[2,24,768]{2,1,0:T(8,128)S(1)}, f32[2,24,768]{2,1,0:T(8,128)}, u32[]{:S(2)}) copy-start(f32[2,24,768]{2,1,0:T(8,128)} %copy-done.4) | copy-start | bytes 442372
  247.1 17.4 %copy-start.9 = (f32[24,768]{1,0:T(8,128)S(1)}, f32[24,768]{1,0:T(8,128)}, u32[]{:S(2)}) copy-start(f32[24,768]{1,0:T(8,128)} %copy-done.8) | copy-start | bytes 221188
  480.5 18.0 %slice-start.3 = ((s8[9437184]{0:T(1024)(128)(4,1)}), s8[1048576]{0:T(1024)(128)(4,1)S(1)}, s32[]{:S(2)}) async-start(s8[9437184]{0:T(1024)(128)(4,1)} %bitcast.84), calls=%async_computation.10 | async-start | bytes 2097152
  483.0 15.5 %slice-start.4 = ((s8[9437184]{0:T(1024)(128)(4,1)}), s8[4194304]{0:T(1024)(128)(4,1)S(1)}, s32[]{:S(2)}) async-start(s8[9437184]{0:T(1024)(128)(4,1)} %bitcast.84), calls=%async_computation.11 | async-start | bytes 8388608
  483.0 15.5 %slice-start.5 = ((s8[9437184]{0:T(1024)(128)(4,1)}), s8[4194304]{0:T(1024)(128)(4,1)S(1)}, s32[]{:S(2)}) async-start(s8[9437184]{0:T(1024)(128)(4,1)} %bitcast.84), calls=%async_computation.12 | async-start | bytes 8388608
  519.2 18.3 %copy-start.6 = (f32[2,24,768]{2,1,0:T(8,128)S(1)}, f32[2,24,768]{2,1,0:T(8,128)}, u32[]{:S(2)}) copy-start(f32[2,24,768]{2,1,0:T(8,128)} %copy-done.4) | copy-start | bytes 442372
  537.5 100.5 %copy-start.2 = (f32[48,3072]{1,0:T(8,128)S(1)}, f32[48,3072]{1,0:T(8,128)}, u32[]{:S(2)}) copy-start(f32[48,3072]{1,0:T(8,128)} %copy-done.1) | copy-start | bytes 1769476
  537.5 140.1 %copy-start.3 = (f32[2,48,3072]{2,1,0:T(8,128)S(1)}, f32[2,48,3072]{2,1,0:T(8,128)}, u32[]{:S(2)}) copy-start(f32[2,48,3072]{2,1,0:T(8,128)} %all-reduce.3.cloned.1.call-done) | copy-start | bytes 3538948
Sparse Core Ops, SparseCore 0:
  11.7 85.3 all-reduce.2
  639.0 38.5 all-gather.2
where the time goes:
time: 703 us; the launch traced here: 692 us
  blocking collectives  274 us (39%)
  matrix products  206 us (29%)
  waiting for transfers between devices  91.3 us (13%)
  other arithmetic  63.1 us (9%)
  local copies, waits for them, and re-layouts  31.1 us (4%)
  between operations  18.5 us (3%)
  starting transfers between devices  7.17 us (1%)
    psum x2, blocking collectives, squares(): return lax.psum(jnp.sum(vector * vector), ('grp', 'tile', 'lev'))  148 us
    psum x1, blocking collectives, on_device(): curve = lax.psum(jnp.sum(direction * image_vec), ('grp', 'tile', 'lev'))  74.2 us
    dot_general x3, matrix products, project(): values = jnp.einsum('csj,nj->csn', arrived, latitude, precision=HIGH)  70.6 us
    dot_general x3, matrix products, to_spectral(): coeffs = jnp.einsum('csi,ji->csj', zonal_rows, grid_field, precision=HIGH)  63.1 us
    psum x1, waiting for transfers between devices, on_device(): paired_mean = lax.psum(member_sum, 'grp') / MEM  44.2 us
    dot_general x2, matrix products, on_device(): jnp.einsum('csn,nj->csj', direction * spec_scale[None], latitude, precisi...  41.7 us
    cos x1, other arithmetic, zonal_basis(): return jnp.stack([jnp.cos(angles), jnp.sin(angles)]) * factor  41.2 us
    all_gather x1, waiting for transfers between devices, on_device(): lax.all_gather(analysis_increment[None], 'grp', axis=0, tiled=True)  38 us
  transfers between devices with their start and end apart: 3, of which 3 were waited for; matrix products, arithmetic and copies ran while one was open for 6% of the time, Pallas kernels for 0%

commit v1 on v0

v1 whole, which is shorter than its diff:
```python
import functools
import math
import numpy as np
import jax
import jax.numpy as jnp
import ml_dtypes
from jax import lax
from jax.experimental import pallas as pl
from jax.experimental.pallas import tpu as pltpu
from jax.sharding import PartitionSpec as P

BF = jnp.bfloat16
F32 = jnp.float32
MEM = 16
SPREAD_FACTOR = 1.2
PARAMS = pltpu.CompilerParams(vmem_limit_bytes=56 * 2**20)


def split_table(table):
    high = table.astype(ml_dtypes.bfloat16)
    low = (table - high.astype(np.float64)).astype(ml_dtypes.bfloat16)
    return np.stack([high, low])


def zonal_tables(waves, lon_count):
    quarter = lon_count // 4
    columns = quarter + 128
    place = np.arange(columns)
    parts = []
    for parity in (0, 1):
        m = np.arange(parity, waves, 2)
        turn = (m[:, None] * place[None, :]) % lon_count
        angle = turn * (2.0 * math.pi / lon_count)
        for wave in (np.cos(angle), np.sin(angle)):
            wave = wave * math.sqrt(2.0 / lon_count)
            wave[:, quarter + 1 :] = 0.0
            parts.append(split_table(wave))
    return np.stack(parts)


def latitude_table(degrees, bands, rows):
    lat_count = bands * rows
    n = np.arange(degrees)
    out = np.zeros((degrees, bands, 64))
    j = np.arange(lat_count)
    turn = (n[:, None] * (2 * j + 1)[None, :]) % (4 * lat_count)
    out[:, :, :rows] = (np.cos(turn * (math.pi / (2.0 * lat_count))) * math.sqrt(2.0 / lat_count)).reshape(degrees, bands, rows)
    return split_table(out.reshape(degrees, bands * 64))


def halves(x):
    high = x.astype(BF)
    return high, (x - high.astype(F32)).astype(BF)


def lanes_like(x):
    return lax.broadcasted_iota(jnp.int32, x.shape, x.ndim - 1)


def flip_shift(x):
    lanes = lanes_like(x)
    return jnp.take_along_axis(x, (128 - lanes) % 128, axis=-1)


def block(x, q):
    return x[:, 128 * q : 128 * (q + 1)]


def mirrored(x, top, count, keep_first):
    out = []
    for q in range(count):
        body = flip_shift(block(x, top - 1 - q))
        first = lanes_like(body) == 0
        if q == 0 and not keep_first:
            out.append(jnp.where(first, 0.0, body))
        else:
            out.append(jnp.where(first, block(x, top - q), body))
    return jnp.concatenate(out, axis=1)


NT = (((1,), (1,)), ((), ()))
NN = (((1,), (0,)), ((), ()))
TN = (((0,), (0,)), ((), ()))


def dot(a, b, dims=NN):
    return lax.dot_general(a, b, dims, preferred_element_type=F32)


def fold(grid):
    q = grid.shape[1] // 4
    blocks = q // 128
    rows = grid.shape[0]
    zero = jnp.zeros((rows, 128), F32)
    a = grid[:, : q + 128]
    c = grid[:, 2 * q : 3 * q + 128]
    b = jnp.concatenate([mirrored(grid, 2 * blocks, blocks, False), zero], axis=1)
    d = jnp.concatenate([mirrored(grid, 4 * blocks, blocks, False), zero], axis=1)
    ac, bd, amc, bmd = a + c, b + d, a - c, b - d
    return ac + bd, ac - bd, amc - bmd, amc + bmd


def analyse(grid, table_ref, perm):
    rows = grid.shape[0]
    pad = jnp.zeros((64 - rows, grid.shape[1] // 4 + 128), BF)
    parts = fold(grid)
    natural = []
    for parity in (0, 1):
        sums = []
        for c in (0, 1):
            high, low = halves(parts[2 * parity + c])
            both = jnp.concatenate([high, pad, low, pad], axis=0)
            if c == 1:
                both = jnp.concatenate([low, pad, high, pad], axis=0)
            acc = dot(table_ref[2 * parity + c, 0], both, NT) + dot(table_ref[2 * parity + c, 1], both, NT)
            sums.append(acc + pltpu.roll(acc, 64, 1))
        natural.append(jnp.where(lanes_like(sums[0]) < 64, sums[0], sums[1]))
    natural = jnp.concatenate(natural, axis=0)
    high, low = halves(natural)
    moved = dot(perm, jnp.concatenate([high, low], axis=1))
    return moved[:, :128] + moved[:, 128:]


def place_of(wave, waves):
    return wave // 2 + (wave % 2) * (waves // 2)


def one_hot(place, axis, waves):
    return (lax.broadcasted_iota(jnp.int32, (waves, waves), axis) == place).astype(F32).astype(BF)


def synthesise(band, table_ref, perm_t, rows, lon):
    q = lon // 4
    blocks = q // 128
    waves = band.shape[0]
    high, low = halves(band)
    moved = dot(perm_t, jnp.concatenate([high, low], axis=1))
    natural = moved[:, :128] + moved[:, 128:]
    parts = []
    for parity in (0, 1):
        flipped = natural[parity * (waves // 2) : (parity + 1) * (waves // 2)].T
        high, low = halves(flipped)
        for c in (0, 1):
            lhs = jnp.concatenate([high[64 * c : 64 * c + 64], low[64 * c : 64 * c + 64]], axis=0)
            acc = dot(lhs, table_ref[2 * parity + c, 0]) + dot(lhs, table_ref[2 * parity + c, 1])
            parts.append(acc[:rows] + acc[64 : 64 + rows])
    ce, se, co, so = parts
    f1 = (ce + co + se + so)[:, :q]
    a = ce - co - se + so
    f3 = (ce - co + se - so)[:, :q]
    b = ce + co - se - so
    f2 = mirrored(a, blocks, blocks, True)
    f4 = mirrored(b, blocks, blocks, True)
    return jnp.concatenate([f1, f2, f3, f4], axis=1)


def turn(x, by):
    return pltpu.roll(x, by % 128, 1)


def pack(x):
    lanes = lanes_like(x)
    y = jnp.where(lanes < 48, x, turn(x, -16))
    k = x.shape[0] // 4
    a, b, c, d = (y[i * k : (i + 1) * k] for i in range(4))
    lanes = lanes[:k]
    return jnp.concatenate(
        [
            jnp.where(lanes < 96, a, turn(b, 96)),
            jnp.where(lanes < 64, turn(b, -32), turn(c, 64)),
            jnp.where(lanes < 32, turn(c, -64), turn(d, 32)),
        ],
        axis=0,
    )


def unpack(p):
    k = p.shape[0] // 3
    p0, p1, p2 = (p[i * k : (i + 1) * k] for i in range(3))
    lanes = lanes_like(p0)
    y = jnp.concatenate(
        [
            p0,
            jnp.where(lanes < 32, turn(p0, 32), turn(p1, 32)),
            jnp.where(lanes < 64, turn(p1, 64), turn(p2, 64)),
            turn(p2, -32),
        ],
        axis=0,
    )
    lanes = lanes_like(y)
    x = jnp.where(lanes < 48, y, turn(y, 16))
    return jnp.where((lanes < 48) | ((lanes >= 64) & (lanes < 112)), x, 0.0)


def total(x):
    return jnp.sum(jnp.sum(x, axis=0, keepdims=True), axis=1, keepdims=True)


def mark(x, values):
    rows = lax.broadcasted_iota(jnp.int32, x.shape, x.ndim - 2)
    lanes = lanes_like(x)
    for i, value in enumerate(values):
        value = value.reshape((1,) * x.ndim)
        x = jnp.where((rows == 0) & (lanes == 48 + i), value, x)
    return x


def spread(values):
    lanes = lax.broadcasted_iota(jnp.int32, (8, 128), 1)
    out = jnp.zeros((8, 128), F32)
    for i, value in enumerate(values):
        out = jnp.where(lanes == i, value, out)
    return out


def level_sum(members_ref):
    acc = members_ref[0, 0].astype(F32)
    for k in range(1, members_ref.shape[0]):
        acc = acc + members_ref[k, 0].astype(F32)
    return acc


def other_kernel(grp_ref, members_ref, count_ref, order_ref, table_ref, sum_ref, out_ref):
    waves = order_ref.shape[0]
    acc = level_sum(members_ref)
    sum_ref[...] = acc
    weights = count_ref[...].astype(F32) * 0.5
    perm = one_hot(place_of(order_ref[...], waves), 1, waves)
    out_ref[...] = pack(analyse(-weights * (acc / MEM), table_ref, perm))


def own_kernel(grp_ref, members_ref, obs_ref, count_ref, order_ref, table_ref, sum_ref, out_ref):
    waves = order_ref.shape[0]
    acc = level_sum(members_ref)
    sum_ref[...] = acc
    weights = count_ref[...].astype(F32) * 0.5
    perm = one_hot(place_of(order_ref[...], waves), 1, waves)
    out_ref[...] = analyse(weights * (obs_ref[0] - acc / MEM), table_ref, perm)


def join_kernel(own_ref, packed_ref, out_ref):
    out_ref[...] = (own_ref[...] + unpack(packed_ref[...])).reshape(out_ref.shape)


def latitude_analysis(chunks_ref, lat_ref):
    bands, slots, _ = chunks_ref.shape
    cos, sin = [], []
    for p in range(bands // 2):
        x0, x1 = chunks_ref[2 * p], chunks_ref[2 * p + 1]
        lower = lanes_like(x0) < 64
        cos.append(jnp.where(lower, x0, turn(x1, 64)))
        sin.append(jnp.where(lower, turn(x0, 64), x1))
    x = jnp.concatenate([jnp.concatenate(cos, axis=1), jnp.concatenate(sin, axis=1)], axis=0)
    high, low = halves(x)
    lhs = jnp.concatenate([high, low], axis=0)
    acc = dot(lhs, lat_ref[0], NT) + dot(lhs, lat_ref[1], NT)
    return acc[: 2 * slots] + acc[2 * slots :]


def latitude_synthesis(vector, lat_ref, out_ref, values):
    bands, slots, _ = out_ref.shape
    high, low = halves(vector)
    lhs = jnp.concatenate([high, low], axis=0)
    acc = dot(lhs, lat_ref[0]) + dot(lhs, lat_ref[1])
    y = acc[: 2 * slots] + acc[2 * slots :]
    for p in range(bands // 2):
        y0, y1 = block(y[:slots], p), block(y[slots:], p)
        lower = lanes_like(y0) < 64
        out_ref[2 * p] = mark(jnp.where(lower, y0, turn(y1, 64)), values)
        out_ref[2 * p + 1] = mark(jnp.where(lower, turn(y0, 64), y1), values)


def scale_of(variance, waves_col, degrees):
    slots = waves_col.shape[0]
    degree = lax.broadcasted_iota(jnp.int32, (slots, degrees), 1)
    scale = jnp.where(degree >= waves_col, jnp.sqrt(variance), 0.0)
    return jnp.concatenate([scale, scale], axis=0)


def latitude_first_kernel(chunks_ref, variance_ref, waves_ref, lat_ref, rhs_ref, out_ref):
    scale = scale_of(variance_ref[...], waves_ref[...], variance_ref.shape[1])
    rhs = latitude_analysis(chunks_ref, lat_ref) * scale
    rhs_ref[...] = rhs
    latitude_synthesis(rhs * scale, lat_ref, out_ref, [total(rhs * rhs)])


def latitude_second_kernel(chunks_ref, variance_ref, waves_ref, rhs_ref, lat_ref, image_ref, out_ref):
    scale = scale_of(variance_ref[...], waves_ref[...], variance_ref.shape[1])
    image = rhs_ref[...] + latitude_analysis(chunks_ref, lat_ref) * scale
    image_ref[...] = image
    latitude_synthesis(image * scale, lat_ref, out_ref, [])


def grid_kernel(band_ref, count_ref, row_ref, order_ref, table_ref, field_ref, packed_ref, out_ref):
    bands, slots, _ = band_ref.shape
    waves = bands * slots
    rows, lon = count_ref.shape
    band = band_ref[...].reshape(waves, 128)
    packed_ref[...] = pack(band)
    perm_t = one_hot(place_of(row_ref[...], waves), 0, waves)
    field = synthesise(band, table_ref, perm_t, rows, lon)
    field_ref[...] = field
    weighted = count_ref[...].astype(F32) * 0.5 * field
    perm = one_hot(place_of(order_ref[...], waves), 1, waves)
    out = analyse(weighted, table_ref, perm)
    norm = jnp.zeros((1, 1), F32)
    for t in range(bands):
        norm = norm + band_ref[t, 0:1, 48:49]
    out_ref[...] = mark(out.reshape(bands, slots, 128), [total(weighted * field), norm])


def pack_kernel(band_ref, packed_ref):
    bands, slots, _ = band_ref.shape
    packed_ref[...] = pack(band_ref[...].reshape(bands * slots, 128))


def first_step(reduced):
    norm, curve = reduced[0:1, 0:1], reduced[0:1, 1:2]
    return norm / (norm + curve)


def last_kernel(band_ref, count_ref, row_ref, table_ref, field_ref, rhs_ref, image_ref, reduced_ref, next_ref, sums_ref):
    bands, slots, _ = band_ref.shape
    waves = bands * slots
    rows, lon = count_ref.shape
    perm_t = one_hot(place_of(row_ref[...], waves), 0, waves)
    field = synthesise(band_ref[...].reshape(waves, 128), table_ref, perm_t, rows, lon)
    step = first_step(reduced_ref[...])
    start = field_ref[...]
    following = start - step * field
    next_ref[...] = following
    weighted = count_ref[...].astype(F32) * 0.5 * following
    rhs = rhs_ref[...]
    residual = rhs - step * image_ref[...]
    sums_ref[...] = spread([total(residual * residual), total(residual * rhs), total(weighted * following), total(weighted * start)])


def partner_first_kernel(packed_ref, row_ref, table_ref, field_ref):
    waves = row_ref.shape[1]
    rows, lon = field_ref.shape
    perm_t = one_hot(place_of(row_ref[...], waves), 0, waves)
    field_ref[...] = synthesise(unpack(packed_ref[...]), table_ref, perm_t, rows, lon)


def partner_second_kernel(packed_ref, row_ref, table_ref, start_ref, reduced_ref, next_ref):
    waves = row_ref.shape[1]
    rows, lon = next_ref.shape
    perm_t = one_hot(place_of(row_ref[...], waves), 0, waves)
    field = synthesise(unpack(packed_ref[...]), table_ref, perm_t, rows, lon)
    next_ref[...] = start_ref[...] - first_step(reduced_ref[...]) * field


def finish_kernel(grp_ref, members_ref, sa_ref, sb_ref, start_ref, next_ref, reduced_ref, sums_ref, rhs_ref, image_ref, out_ref, control_ref):
    reduced, sums = reduced_ref[...], sums_ref[...]
    norm, field_norm = reduced[0:1, 0:1], reduced[0:1, 1:2]
    step = first_step(reduced)
    norm_next, cross, field_next, field_cross = (sums[0:1, i : i + 1] for i in range(4))
    ratio = norm_next / norm
    curve = norm_next + field_next + 2.0 * ratio * (cross + field_cross) + ratio * ratio * (norm + field_norm)
    step_next = norm_next / curve
    mean = (sa_ref[0] + sb_ref[0]) / MEM
    start = start_ref[0]
    increment = step * start + step_next * (next_ref[0] + ratio * start)
    offset = (mean + increment) - SPREAD_FACTOR * mean
    for k in range(members_ref.shape[0]):
        out_ref[k, 0] = (SPREAD_FACTOR * members_ref[k, 0].astype(F32) + offset).astype(BF)
    rhs = rhs_ref[...]
    residual = rhs - step * image_ref[...]
    control_ref[...] = step * rhs + step_next * (residual + ratio * rhs)


def shape(*dims):
    return jax.ShapeDtypeStruct(dims, F32)


def call(kernel, outs, name):
    return pl.pallas_call(kernel, out_shape=outs, compiler_params=PARAMS, name=name)


def butterfly(value, axis, count):
    step = 1
    while step < count:
        value = value + lax.ppermute(value, axis, [(i, i ^ step) for i in range(count)])
        step *= 2
    return value


def on_device(tables, lat_table, members, obs_value, obs_count, variance, wave_order):
    grp = lax.axis_index("grp")
    bands = lax.axis_size("tile")
    levels = lax.axis_size("lev")
    mem, _, rows, lon = members.shape
    waves = wave_order.shape[0]
    slots = waves // bands
    degrees = variance.shape[1]
    swap = [(0, 1), (1, 0)]
    own_waves = lax.dynamic_slice_in_dim(wave_order, lax.axis_index("tile") * slots, slots, 0)[:, None]
    own_variance = lax.dynamic_index_in_dim(variance, grp, 0, keepdims=True)
    order_col, order_row = wave_order[:, None], wave_order[None, :]
    grp_scalar = grp[None].astype(jnp.int32)

    def whole(array):
        return pl.BlockSpec(array.shape, lambda i, g: (0,) * array.ndim)

    def start_call(kernel, arrays, specs, outs, flip, name):
        member_spec = pl.BlockSpec((mem, 1, rows, lon), lambda i, g: (0, g[0] ^ flip, 0, 0))
        return pl.pallas_call(
            kernel,
            grid_spec=pltpu.PrefetchScalarGridSpec(
                num_scalar_prefetch=1,
                grid=(1,),
                in_specs=[member_spec] + specs,
                out_specs=[whole(o) for o in outs],
            ),
            out_shape=outs,
            compiler_params=PARAMS,
            name=name,
        )(grp_scalar, members, *arrays)

    chunk = shape(bands, slots, 128)
    packed = shape(waves * 3 // 4, 128)
    field = shape(rows, lon)
    vector = shape(2 * slots, degrees)
    with jax.named_scope("start"):
        sum_other, coeffs_other = start_call(
            other_kernel, (obs_count, order_col, tables), [whole(obs_count), whole(order_col), whole(tables)], [field, packed], 1, "other"
        )
        coeffs_in = lax.ppermute(coeffs_other, "grp", swap)
        obs_spec = pl.BlockSpec((1, rows, lon), lambda i, g: (g[0], 0, 0))
        sum_own, coeffs_own = start_call(
            own_kernel,
            (obs_value, obs_count, order_col, tables),
            [obs_spec, whole(obs_count), whole(order_col), whole(tables)],
            [field, shape(waves, 128)],
            0,
            "own",
        )
        sum_own_in = lax.ppermute(sum_other, "grp", swap)
        sum_other_in = lax.ppermute(sum_own, "grp", swap)
        coeffs = call(join_kernel, chunk, "join")(coeffs_own, coeffs_in)

    def exchange(chunks):
        return lax.all_to_all(chunks, "tile", 0, 0, tiled=True)

    with jax.named_scope("solve"):
        rhs, lat_values = call(latitude_first_kernel, [vector, chunk], "lat1")(exchange(coeffs), own_variance, own_waves, lat_table)
        field_own, packed_first, coeffs = call(grid_kernel, [field, packed, chunk], "grid")(
            exchange(lat_values), obs_count, order_row, order_col, tables
        )
        packed_first_in = lax.ppermute(packed_first, "grp", swap)
        arrived = exchange(coeffs)
        norm = arrived[0, 0:1, 49:50]
        curve = jnp.sum(arrived[:, 0, 48]).reshape(1, 1)
        reduced = butterfly(jnp.pad(jnp.concatenate([norm, curve], axis=1), ((0, 7), (0, 126))), "lev", levels)
        reduced = butterfly(reduced, "grp", 2)
        image, lat_values = call(latitude_second_kernel, [vector, chunk], "lat2")(arrived, own_variance, own_waves, rhs, lat_table)
        band = exchange(lat_values)
        packed_second_in = lax.ppermute(call(pack_kernel, packed, "pack")(band), "grp", swap)
        next_own, sums = call(last_kernel, [field, shape(8, 128)], "last")(
            band, obs_count, order_row, tables, field_own, rhs, image, reduced
        )
        sums = butterfly(sums, "tile", bands)
        sums = butterfly(sums, "lev", levels)
        sums = butterfly(sums, "grp", 2)
        field_other = call(partner_first_kernel, field, "partner1")(packed_first_in, order_row, tables)
        next_other = call(partner_second_kernel, field, "partner2")(packed_second_in, order_row, tables, field_other, reduced)

    with jax.named_scope("finish"):
        cut = 16

        def own_first(*dims):
            return pl.BlockSpec(dims, lambda h, r, g: (h ^ g[0], r, 0))

        def fixed(*dims):
            return pl.BlockSpec(dims, lambda h, r, g: (0,) * len(dims))

        member_spec = pl.BlockSpec((mem, 1, cut, lon), lambda h, r, g: (0, h, r, 0))
        piece = own_first(1, cut, lon)
        small = fixed(8, 128)
        vec = fixed(2 * slots, degrees)
        recentered, control = pl.pallas_call(
            finish_kernel,
            grid_spec=pltpu.PrefetchScalarGridSpec(
                num_scalar_prefetch=1,
                grid=(2, rows // cut),
                in_specs=[member_spec, piece, piece, piece, piece, small, small, vec, vec],
                out_specs=[member_spec, vec],
            ),
            out_shape=[jax.ShapeDtypeStruct(members.shape, BF), vector],
            compiler_params=PARAMS,
            name="finish",
        )(
            grp_scalar,
            members,
            jnp.stack([sum_own, sum_other]),
            jnp.stack([sum_own_in, sum_other_in]),
            jnp.stack([field_own, field_other]),
            jnp.stack([next_own, next_other]),
            reduced,
            sums,
            rhs,
            image,
        )
    return recentered, control.reshape(1, 1, 2, slots, degrees)


def solution(mesh):
    bands = mesh.shape["tile"]
    waves, degrees, rows, lon = 768, 768, 48, 3072
    tables = zonal_tables(waves, lon)
    lat_table = latitude_table(degrees, bands, rows)
    placed = (
        P("grp", "lev", "tile", None),
        P("lev", "tile", None),
        P("tile", None),
        P("lev", None),
        P(),
    )
    return jax.shard_map(
        lambda *args: on_device(jnp.asarray(tables), jnp.asarray(lat_table), *args),
        mesh=mesh,
        in_specs=placed,
        out_specs=(P("grp", "lev", "tile", None), P("lev", "grp", None, "tile", None)),
        check_vma=False,
    )
```

time: 703 us -> 259 us (0.37)
  blocking collectives: 274 us -> 13.8 us
  matrix products: 206 us -> 0 us
  Pallas kernels: 0 us -> 69.6 us
  starting transfers between devices: 7.17 us -> 59 us
  other arithmetic: 63.1 us -> 13.1 us
  local copies, waits for them, and re-layouts: 31.1 us -> 8.66 us
  between operations: 18.5 us -> 0.77 us
    psum x3 -> x0, blocking collectives: 222 us -> none  [the longest x2 148 us: squares(): return lax.psum(jnp.sum(vector * vector), ('grp', 'tile', 'lev'))]
    dot_general x10 -> x0, matrix products: 206 us -> none  [the longest x3 70.6 us: project(): values = jnp.einsum('csj,nj->csn', arrived, latitude, precision=HIGH)]
    ppermute x0 -> x16, waiting for transfers between devices: none -> 70.9 us  [the longest x11 58.7 us: butterfly(): lax.ppermute(value, axis, [(i, i ^ step) for i in range(count)])]
    pallas_call x0 -> x11, Pallas kernels: none -> 69.6 us  [the longest x2 14.2 us: start_call(): pl.pallas_call(kernel, grid_spec=pltpu.PrefetchScalarGridSpec(num_scalar_...]
    psum x1 -> x0, waiting for transfers between devices: 44.2 us -> none  [on_device(): paired_mean = lax.psum(member_sum, 'grp') / MEM]
    ppermute x0 -> x16, starting transfers between devices: none -> 43.7 us  [the longest x11 21.6 us: butterfly(): lax.ppermute(value, axis, [(i, i ^ step) for i in range(count)])]
    cos x1 -> x0, other arithmetic: 41.2 us -> none  [zonal_basis(): return jnp.stack([jnp.cos(angles), jnp.sin(angles)]) * factor]
    all_to_all x4 -> x1, blocking collectives: 52.3 us -> 13.8 us  [exchange(): return lax.all_to_all(chunks, 'tile', 0, 0, tiled=True)]
  transfers between devices with their start and end apart: 3 -> 19, of which waited for: 3 -> 11; matrix products, arithmetic and copies ran while one was open for 6% -> 4% of each run, Pallas kernels for 0% -> 12%
where the time goes in v1:
time: 259 us; the launch traced here: 254 us
  waiting for transfers between devices  88.7 us (34%)
  Pallas kernels  69.6 us (27%)
  starting transfers between devices  59 us (23%)
  blocking collectives  13.8 us (5%)
  other arithmetic  13.1 us (5%)
  local copies, waits for them, and re-layouts  8.66 us (3%)
    ppermute x11, waiting for transfers between devices, butterfly(): lax.ppermute(value, axis, [(i, i ^ step) for i in range(count)])  58.7 us
    ppermute x11, starting transfers between devices, butterfly(): lax.ppermute(value, axis, [(i, i ^ step) for i in range(count)])  21.6 us
    all_to_all x3, waiting for transfers between devices, exchange(): return lax.all_to_all(chunks, 'tile', 0, 0, tiled=True)  17.8 us
    all_to_all x3, starting transfers between devices, exchange(): return lax.all_to_all(chunks, 'tile', 0, 0, tiled=True)  15.3 us
    pallas_call x2, Pallas kernels, start_call(): pl.pallas_call(kernel, grid_spec=pltpu.PrefetchScalarGridSpec(num_scalar_...  14.2 us
    all_to_all x1, blocking collectives, exchange(): return lax.all_to_all(chunks, 'tile', 0, 0, tiled=True)  13.8 us
    pallas_call x1, Pallas kernels, on_device(): call(grid_kernel, [field, packed, chunk], 'grid')  8.39 us
    pallas_call x1, Pallas kernels, on_device(): call(latitude_second_kernel, [vector, chunk], 'lat2')  8.32 us
  transfers between devices with their start and end apart: 19, of which 11 were waited for; matrix products, arithmetic and copies ran while one was open for 4% of the time, Pallas kernels for 12%

profile of v1, /device:TPU:32, one launch (start us, length us, event | category | flops | bytes accessed | tf_op | source)
XLA Modules:
  0.0 253.7 jit_solution(6327770099956477828)
XLA Ops:
  2.3 7.1 %other.1 = (f32[48,3072]{1,0:T(8,128)}, f32[576,128]{1,0:T(8,128)}) custom-call(s32[1]{0:T(128)} %bitcast.grp_ref, bf16[8,2,48,3072]{3,2,1,0:T(8,128)(2,1)} %members_ref.5, s32[48,3072]{1,0:T(8,128)} %count_ref.7, s32[768,1]{1,0:T(8,128)} %broadcast_in_dim.16.order_ref, bf16[4,2,384,896]{3,2,1,0:T(8,128)(2,1)} %constant.30.clone.table_ref), custom_call_target="tpu_custom_call" | custom-call | tf_op jit(solution)/shard_map/start/other/pallas_call | solution.py:407
  9.3 6.3 %collective-permute-start.2 = (f32[576,128]{1,0:T(8,128)}, f32[576,128]{1,0:T(8,128)S(1)}, u32[]{:S(2)}, u32[]{:S(2)}) collective-permute-start(f32[576,128]{1,0:T(8,128)} %get-tuple-element.20), channel_id=1, source_target_pairs={{0,128},{128,0},{1,129},{129,1},{2,130},{130,2},{3,131},{131,3},{4... | collective-permute-start | bytes 884744 | tf_op jit(solution)/shard_map/start/ppermute | solution.py:428
  15.6 7.1 %own.1 = (f32[48,3072]{1,0:T(8,128)}, f32[768,128]{1,0:T(8,128)}) custom-call(s32[1]{0:T(128)} %bitcast.grp_ref, bf16[8,2,48,3072]{3,2,1,0:T(8,128)(2,1)} %members_ref.5, f32[2,48,3072]{2,1,0:T(8,128)} %obs_ref.1, s32[48,3072]{1,0:T(8,128)} %count_ref.7, s32[768,1]{1,0:T(8,128)} %broadcast_in_dim.16.order_ref, bf16[4,2,384,896]{3,2,1,0:T(8,128)(2,1)} %constant.30.clone.table_ref), custom_call_target="tpu_custom_call" | custom-call | tf_op jit(solution)/shard_map/start/own/pallas_call | solution.py:407
  22.8 6.5 %collective-permute-done.2.packed_ref = f32[576,128]{1,0:T(8,128)S(1)} collective-permute-done((f32[576,128]{1,0:T(8,128)}, f32[576,128]{1,0:T(8,128)S(1)}, u32[]{:S(2)}, u32[]{:S(2)}) %collective-permute-start.2) | collective-permute-done | bytes 294944 | tf_op jit(solution)/shard_map/start/ppermute | solution.py:428
  32.1 7.3 %all-to-all-start = ((f32[32,24,128]{2,1,0:T(8,128)}), f32[32,24,128]{2,1,0:T(8,128)S(1)}, u32[]{:S(2)}, u32[]{:S(2)}) async-start(f32[32,24,128]{2,1,0:T(8,128)} %join.1), calls=%async_computation | async-start | bytes 786432 | tf_op jit(solution)/shard_map/solve/all_to_all | solution.py:443
  40.8 8.6 %all-to-all-done.chunks_ref = f32[32,24,128]{2,1,0:T(8,128)S(1)} async-done(((f32[32,24,128]{2,1,0:T(8,128)}), f32[32,24,128]{2,1,0:T(8,128)S(1)}, u32[]{:S(2)}, u32[]{:S(2)}) %all-to-all-start) | async-done | bytes 393248 | tf_op jit(solution)/shard_map/solve/all_to_all | solution.py:443
  50.2 8.1 %lat1.1 = (f32[48,768]{1,0:T(8,128)}, f32[32,24,128]{2,1,0:T(8,128)}) custom-call(f32[32,24,128]{2,1,0:T(8,128)} %copy-done.4, f32[1,768]{1,0:T(1,128)} %constant_dynamic-slice_fusion.variance_ref, s32[24,1]{1,0:T(8,128)} %copy.13.waves_ref, bf16[2,768,2048]{2,1,0:T(8,128)(2,1)} %constant.31.clone.lat_ref), custom_call_target="tpu_custom_call" | custom-call | tf_op jit(solution)/shard_map/solve/lat1/pallas_call | solution.py:446
  58.3 4.1 %all-to-all-start.1 = ((f32[32,24,128]{2,1,0:T(8,128)}), f32[32,24,128]{2,1,0:T(8,128)S(1)}, u32[]{:S(2)}, u32[]{:S(2)}) async-start(f32[32,24,128]{2,1,0:T(8,128)} %get-tuple-element.21), calls=%async_computation.1 | async-start | bytes 786432 | tf_op jit(solution)/shard_map/solve/all_to_all | solution.py:443
  63.0 9.2 %all-to-all-done.1.band_ref = f32[32,24,128]{2,1,0:T(8,128)S(1)} async-done(((f32[32,24,128]{2,1,0:T(8,128)}), f32[32,24,128]{2,1,0:T(8,128)S(1)}, u32[]{:S(2)}, u32[]{:S(2)}) %all-to-all-start.1) | async-done | bytes 393248 | tf_op jit(solution)/shard_map/solve/all_to_all | solution.py:443
  72.9 8.4 %grid.1 = (f32[48,3072]{1,0:T(8,128)}, f32[576,128]{1,0:T(8,128)}, f32[32,24,128]{2,1,0:T(8,128)}) custom-call(f32[32,24,128]{2,1,0:T(8,128)} %copy-done.5, s32[48,3072]{1,0:T(8,128)} %count_ref.7, s32[1,768]{1,0:T(1,128)} %broadcast_in_dim.15.row_ref, s32[768,1]{1,0:T(8,128)} %broadcast_in_dim.16.order_ref, bf16[4,2,384,896]{3,2,1,0:T(8,128)(2,1)} %constant.30.clone.table_ref), custom_call_target="tpu_custom_call" | custom-call | tf_op jit(solution)/shard_map/solve/grid/pallas_call | solution.py:447
  81.3 13.8 %all_to_all.20.chunks_ref = f32[32,24,128]{2,1,0:T(8,128)S(1)} all-to-all(f32[32,24,128]{2,1,0:T(8,128)} %get-tuple-element.24), channel_id=1, replica_groups=mesh['grp'=2,'tile'=32,'lev'=4] {'tile'}, dimensions={0} | all-to-all | bytes 786432 | tf_op jit(solution)/shard_map/solve/all_to_all | solution.py:443
  97.9 8.3 %lat2.1 = (f32[48,768]{1,0:T(8,128)}, f32[32,24,128]{2,1,0:T(8,128)}) custom-call(f32[32,24,128]{2,1,0:T(8,128)} %copy-done.3, f32[1,768]{1,0:T(1,128)} %constant_dynamic-slice_fusion.variance_ref, s32[24,1]{1,0:T(8,128)} %copy.13.waves_ref, f32[48,768]{1,0:T(8,128)} %get-tuple-element.25.rhs_ref, bf16[2,768,2048]{2,1,0:T(8,128)(2,1)} %constant.31.clone.lat_ref), custom_call_target="tpu_custom_call" | custom-call | tf_op jit(solution)/shard_map/solve/lat2/pallas_call | solution.py:456
  106.2 3.9 %all-to-all-start.3 = ((f32[32,24,128]{2,1,0:T(8,128)}), f32[32,24,128]{2,1,0:T(8,128)S(1)}, u32[]{:S(2)}, u32[]{:S(2)}) async-start(f32[32,24,128]{2,1,0:T(8,128)} %get-tuple-element.26), calls=%async_computation.3 | async-start | bytes 786432 | tf_op jit(solution)/shard_map/solve/all_to_all | solution.py:443
  114.2 5.1 %collective-permute-start = (f32[48,3072]{1,0:T(8,128)S(1)}, f32[48,3072]{1,0:T(8,128)S(1)}, u32[]{:S(2)}, u32[]{:S(2)}) collective-permute-start(f32[48,3072]{1,0:T(8,128)S(1)} %copy-done.6), channel_id=1, source_target_pairs={{0,128},{128,0},{1,129},{129,1},{2,130},{130,2},{3,131},{131,3},{4... | collective-permute-start | bytes 1769480 | tf_op jit(solution)/shard_map/start/ppermute | solution.py:438
  121.4 5.4 %collective-permute-start.6 = (f32[8,128]{1,0:T(8,128)S(1)}, f32[8,128]{1,0:T(8,128)S(1)}, u32[]{:S(2)}, u32[]{:S(2)}) collective-permute-start(f32[8,128]{1,0:T(8,128)S(1)} %fusion.1), channel_id=1, source_target_pairs={{0,128},{128,0},{1,129},{129,1},{2,130},{130,2},{3,131},{131,3},{4... | collective-permute-start | bytes 12296 | tf_op jit(solution)/shard_map/solve/ppermute | solution.py:383
  126.8 44.7 %collective-permute-done.6 = f32[8,128]{1,0:T(8,128)S(1)} collective-permute-done((f32[8,128]{1,0:T(8,128)S(1)}, f32[8,128]{1,0:T(8,128)S(1)}, u32[]{:S(2)}, u32[]{:S(2)}) %collective-permute-start.6) | collective-permute-done | bytes 4128 | tf_op jit(solution)/shard_map/solve/ppermute | solution.py:383
  172.8 6.3 %last.1 = (f32[48,3072]{1,0:T(8,128)}, f32[8,128]{1,0:T(8,128)}) custom-call(f32[32,24,128]{2,1,0:T(8,128)} %copy-done.1, s32[48,3072]{1,0:T(8,128)} %count_ref.7, s32[1,768]{1,0:T(1,128)} %broadcast_in_dim.15.row_ref, bf16[4,2,384,896]{3,2,1,0:T(8,128)(2,1)} %constant.30.clone.table_ref, f32[48,3072]{1,0:T(8,128)} %get-tuple-element.22.field_ref, ...), custom_call_target="tpu_custom_call" | custom-call | tf_op jit(solution)/shard_map/solve/last/pallas_call | solution.py:459
  199.7 5.0 %collective-permute-start.3 = (f32[576,128]{1,0:T(8,128)S(1)}, f32[576,128]{1,0:T(8,128)S(1)}, u32[]{:S(2)}, u32[]{:S(2)}) collective-permute-start(f32[576,128]{1,0:T(8,128)S(1)} %copy-done.13), channel_id=1, source_target_pairs={{0,128},{128,0},{1,129},{129,1},{2,130},{130,2},{3,131},{131,3},{4... | collective-permute-start | bytes 884744 | tf_op jit(solution)/shard_map/solve/ppermute | solution.py:450
  208.5 5.8 %collective-permute-done.3.packed_ref = f32[576,128]{1,0:T(8,128)S(1)} collective-permute-done((f32[576,128]{1,0:T(8,128)S(1)}, f32[576,128]{1,0:T(8,128)S(1)}, u32[]{:S(2)}, u32[]{:S(2)}) %collective-permute-start.3) | collective-permute-done | bytes 294944 | tf_op jit(solution)/shard_map/solve/ppermute | solution.py:450
  215.0 5.8 %partner1.1.start_ref = f32[48,3072]{1,0:T(8,128)} custom-call(f32[576,128]{1,0:T(8,128)} %copy-done.9, s32[1,768]{1,0:T(1,128)} %broadcast_in_dim.15.row_ref, bf16[4,2,384,896]{3,2,1,0:T(8,128)(2,1)} %constant.30.clone.table_ref), custom_call_target="tpu_custom_call" | custom-call | tf_op jit(solution)/shard_map/solve/partner1/pallas_call | solution.py:465
  222.8 4.9 %collective-permute-start.7 = (f32[576,128]{1,0:T(8,128)}, f32[576,128]{1,0:T(8,128)S(1)}, u32[]{:S(2)}, u32[]{:S(2)}) collective-permute-start(f32[576,128]{1,0:T(8,128)} %pack.1), channel_id=1, source_target_pairs={{0,128},{128,0},{1,129},{129,1},{2,130},{130,2},{3,131},{131,3},{4... | collective-permute-start | bytes 884744 | tf_op jit(solution)/shard_map/solve/ppermute | solution.py:458
  231.0 4.9 %collective-permute-done.15 = f32[8,128]{1,0:T(8,128)S(1)} collective-permute-done((f32[8,128]{1,0:T(8,128)S(1)}, f32[8,128]{1,0:T(8,128)S(1)}, u32[]{:S(2)}, u32[]{:S(2)}) %collective-permute-start.15) | collective-permute-done | bytes 4128 | tf_op jit(solution)/shard_map/solve/ppermute | solution.py:383
  237.2 6.1 %partner2.1 = f32[48,3072]{1,0:T(8,128)} custom-call(f32[576,128]{1,0:T(8,128)} %copy-done.10, s32[1,768]{1,0:T(1,128)} %broadcast_in_dim.15.row_ref, bf16[4,2,384,896]{3,2,1,0:T(8,128)(2,1)} %constant.30.clone.table_ref, f32[48,3072]{1,0:T(8,128)} %partner1.1.start_ref, f32[8,128]{1,0:T(8,128)} %add.46.reduced_ref), custom_call_target="tpu_custom_call" | custom-call | tf_op jit(solution)/shard_map/solve/partner2/pallas_call | solution.py:466
  245.4 8.3 %finish.1 = (bf16[8,2,48,3072]{3,2,1,0:T(8,128)(2,1)}, f32[48,768]{1,0:T(8,128)}) custom-call(s32[1]{0:T(128)} %bitcast.grp_ref, bf16[8,2,48,3072]{3,2,1,0:T(8,128)(2,1)} %members_ref.5, f32[2,48,3072]{2,1,0:T(8,128)} %pad_maximum_fusion.sa_ref, f32[2,48,3072]{2,1,0:T(8,128)} %pad_maximum_fusion.1.sb_ref, f32[2,48,3072]{2,1,0:T(8,128)} %pad_maximum_fusion.2.start_ref, ...), custom_call_target="tpu_custom_call" | custom-call | tf_op jit(solution)/shard_map/finish/finish/pallas_call | solution.py:481
  (77 shorter events, 52.1 us)
Async XLA Ops:
  0.6 39.6 %copy-start = (f32[2,768]{1,0:T(2,128)S(1)}, f32[2,768]{1,0:T(2,128)}, u32[]{:S(2)}) copy-start(f32[2,768]{1,0:T(2,128)} %param.10) | copy-start | bytes 18436
  9.3 19.9 %collective-permute-start.2 = (f32[576,128]{1,0:T(8,128)}, f32[576,128]{1,0:T(8,128)S(1)}, u32[]{:S(2)}, u32[]{:S(2)}) collective-permute-start(f32[576,128]{1,0:T(8,128)} %get-tuple-element.20), channel_id=1, source_target_pairs={{0,128},{128,0},{1,129},{129,1},{2,130},{130,2},{3,131},{131,3},{4... | collective-permute-start | bytes 884744 | tf_op jit(solution)/shard_map/start/ppermute | solution.py:428
  22.8 16.7 %copy-start.12 = (s32[768]{0:T(1024)S(1)}, s32[768]{0:T(1024)}, u32[]{:S(2)}) copy-start(s32[768]{0:T(1024)} %param.11) | copy-start | bytes 9220
  32.1 17.3 %all-to-all-start = ((f32[32,24,128]{2,1,0:T(8,128)}), f32[32,24,128]{2,1,0:T(8,128)S(1)}, u32[]{:S(2)}, u32[]{:S(2)}) async-start(f32[32,24,128]{2,1,0:T(8,128)} %join.1), calls=%async_computation | async-start | bytes 786432 | tf_op jit(solution)/shard_map/solve/all_to_all | solution.py:443
  58.3 13.9 %all-to-all-start.1 = ((f32[32,24,128]{2,1,0:T(8,128)}), f32[32,24,128]{2,1,0:T(8,128)S(1)}, u32[]{:S(2)}, u32[]{:S(2)}) async-start(f32[32,24,128]{2,1,0:T(8,128)} %get-tuple-element.21), calls=%async_computation.1 | async-start | bytes 786432 | tf_op jit(solution)/shard_map/solve/all_to_all | solution.py:443
  97.8 12.3 %collective-permute-start.4 = (f32[8,128]{1,0:T(8,128)S(1)}, f32[8,128]{1,0:T(8,128)S(1)}, u32[]{:S(2)}, u32[]{:S(2)}) collective-permute-start(f32[8,128]{1,0:T(8,128)S(1)} %select_maximum_fusion), channel_id=1, source_target_pairs={{0,1},{1,0},{2,3},{3,2},{4,5},{5,4},{6,7},{7,6},{8,9},{9,8},{10,11... | collective-permute-start | bytes 12296 | tf_op jit(solution)/shard_map/solve/ppermute | solution.py:383
  97.9 16.4 %copy-start.6 = (f32[48,3072]{1,0:T(8,128)S(1)}, f32[48,3072]{1,0:T(8,128)}, u32[]{:S(2)}) copy-start(f32[48,3072]{1,0:T(8,128)} %get-tuple-element.18) | copy-start | bytes 1769476
  97.9 21.5 %copy-start.7 = (f32[48,3072]{1,0:T(8,128)S(1)}, f32[48,3072]{1,0:T(8,128)}, u32[]{:S(2)}) copy-start(f32[48,3072]{1,0:T(8,128)} %get-tuple-element.17) | copy-start | bytes 1769476
  106.2 65.9 %all-to-all-start.3 = ((f32[32,24,128]{2,1,0:T(8,128)}), f32[32,24,128]{2,1,0:T(8,128)S(1)}, u32[]{:S(2)}, u32[]{:S(2)}) async-start(f32[32,24,128]{2,1,0:T(8,128)} %get-tuple-element.26), calls=%async_computation.3 | async-start | bytes 786432 | tf_op jit(solution)/shard_map/solve/all_to_all | solution.py:443
  111.4 8.8 %collective-permute-start.5 = (f32[8,128]{1,0:T(8,128)S(1)}, f32[8,128]{1,0:T(8,128)S(1)}, u32[]{:S(2)}, u32[]{:S(2)}) collective-permute-start(f32[8,128]{1,0:T(8,128)S(1)} %fusion), channel_id=1, source_target_pairs={{0,2},{1,3},{2,0},{3,1},{4,6},{5,7},{6,4},{7,5},{8,10},{9,11},{10,... | collective-permute-start | bytes 12296 | tf_op jit(solution)/shard_map/solve/ppermute | solution.py:383
  114.2 93.2 %collective-permute-start = (f32[48,3072]{1,0:T(8,128)S(1)}, f32[48,3072]{1,0:T(8,128)S(1)}, u32[]{:S(2)}, u32[]{:S(2)}) collective-permute-start(f32[48,3072]{1,0:T(8,128)S(1)} %copy-done.6), channel_id=1, source_target_pairs={{0,128},{128,0},{1,129},{129,1},{2,130},{130,2},{3,131},{131,3},{4... | collective-permute-start | bytes 1769480 | tf_op jit(solution)/shard_map/start/ppermute | solution.py:438
  119.3 88.0 %collective-permute-start.1 = (f32[48,3072]{1,0:T(8,128)S(1)}, f32[48,3072]{1,0:T(8,128)S(1)}, u32[]{:S(2)}, u32[]{:S(2)}) collective-permute-start(f32[48,3072]{1,0:T(8,128)S(1)} %copy-done.7), channel_id=1, source_target_pairs={{0,128},{128,0},{1,129},{129,1},{2,130},{130,2},{3,131},{131,3},{4... | collective-permute-start | bytes 1769480 | tf_op jit(solution)/shard_map/start/ppermute | solution.py:439
  121.4 50.0 %collective-permute-start.6 = (f32[8,128]{1,0:T(8,128)S(1)}, f32[8,128]{1,0:T(8,128)S(1)}, u32[]{:S(2)}, u32[]{:S(2)}) collective-permute-start(f32[8,128]{1,0:T(8,128)S(1)} %fusion.1), channel_id=1, source_target_pairs={{0,128},{128,0},{1,129},{129,1},{2,130},{130,2},{3,131},{131,3},{4... | collective-permute-start | bytes 12296 | tf_op jit(solution)/shard_map/solve/ppermute | solution.py:383
  179.1 1.4 collective-permute-start.8
  181.1 3.6 %collective-permute-start.9 = (f32[8,128]{1,0:T(8,128)S(1)}, f32[8,128]{1,0:T(8,128)S(1)}, u32[]{:S(2)}, u32[]{:S(2)}) collective-permute-start(f32[8,128]{1,0:T(8,128)S(1)} %add.47), channel_id=1, source_target_pairs={{0,8},{4,12},{8,0},{12,4},{16,24},{20,28},{24,16},{28,20},{32,40},... | collective-permute-start | bytes 12296 | tf_op jit(solution)/shard_map/solve/ppermute | solution.py:383
  184.7 5.1 %collective-permute-start.10 = (f32[8,128]{1,0:T(8,128)S(1)}, f32[8,128]{1,0:T(8,128)S(1)}, u32[]{:S(2)}, u32[]{:S(2)}) collective-permute-start(f32[8,128]{1,0:T(8,128)S(1)} %add.48), channel_id=1, source_target_pairs={{0,16},{4,20},{8,24},{12,28},{16,0},{20,4},{24,8},{28,12},{32,48},... | collective-permute-start | bytes 12296 | tf_op jit(solution)/shard_map/solve/ppermute | solution.py:383
  189.8 3.6 %collective-permute-start.11 = (f32[8,128]{1,0:T(8,128)S(1)}, f32[8,128]{1,0:T(8,128)S(1)}, u32[]{:S(2)}, u32[]{:S(2)}) collective-permute-start(f32[8,128]{1,0:T(8,128)S(1)} %add.49), channel_id=1, source_target_pairs={{0,32},{4,36},{8,40},{12,44},{16,48},{20,52},{24,56},{28,60},{32,0... | collective-permute-start | bytes 12296 | tf_op jit(solution)/shard_map/solve/ppermute | solution.py:383
  193.5 5.1 %collective-permute-start.12 = (f32[8,128]{1,0:T(8,128)S(1)}, f32[8,128]{1,0:T(8,128)S(1)}, u32[]{:S(2)}, u32[]{:S(2)}) collective-permute-start(f32[8,128]{1,0:T(8,128)S(1)} %add.50), channel_id=1, source_target_pairs={{0,64},{4,68},{8,72},{12,76},{16,80},{20,84},{24,88},{28,92},{32,9... | collective-permute-start | bytes 12296 | tf_op jit(solution)/shard_map/solve/ppermute | solution.py:383
  198.6 6.2 %collective-permute-start.13 = (f32[8,128]{1,0:T(8,128)S(1)}, f32[8,128]{1,0:T(8,128)S(1)}, u32[]{:S(2)}, u32[]{:S(2)}) collective-permute-start(f32[8,128]{1,0:T(8,128)S(1)} %add.51), channel_id=1, source_target_pairs={{0,1},{1,0},{2,3},{3,2},{4,5},{5,4},{6,7},{7,6},{8,9},{9,8},{10,11... | collective-permute-start | bytes 12296 | tf_op jit(solution)/shard_map/solve/ppermute | solution.py:383
  199.7 14.5 %collective-permute-start.3 = (f32[576,128]{1,0:T(8,128)S(1)}, f32[576,128]{1,0:T(8,128)S(1)}, u32[]{:S(2)}, u32[]{:S(2)}) collective-permute-start(f32[576,128]{1,0:T(8,128)S(1)} %copy-done.13), channel_id=1, source_target_pairs={{0,128},{128,0},{1,129},{129,1},{2,130},{130,2},{3,131},{131,3},{4... | collective-permute-start | bytes 884744 | tf_op jit(solution)/shard_map/solve/ppermute | solution.py:450
  204.8 22.9 %collective-permute-start.14 = (f32[8,128]{1,0:T(8,128)S(1)}, f32[8,128]{1,0:T(8,128)S(1)}, u32[]{:S(2)}, u32[]{:S(2)}) collective-permute-start(f32[8,128]{1,0:T(8,128)S(1)} %add.52), channel_id=1, source_target_pairs={{0,2},{1,3},{2,0},{3,1},{4,6},{5,7},{6,4},{7,5},{8,10},{9,11},{10,... | collective-permute-start | bytes 12296 | tf_op jit(solution)/shard_map/solve/ppermute | solution.py:383
  208.5 20.2 %copy-start.2 = (f32[48,3072]{1,0:T(8,128)S(1)}, f32[48,3072]{1,0:T(8,128)}, u32[]{:S(2)}) copy-start(f32[48,3072]{1,0:T(8,128)} %get-tuple-element.22.field_ref) | copy-start | bytes 1769476
  222.8 13.6 %collective-permute-start.7 = (f32[576,128]{1,0:T(8,128)}, f32[576,128]{1,0:T(8,128)S(1)}, u32[]{:S(2)}, u32[]{:S(2)}) collective-permute-start(f32[576,128]{1,0:T(8,128)} %pack.1), channel_id=1, source_target_pairs={{0,128},{128,0},{1,129},{129,1},{2,130},{130,2},{3,131},{131,3},{4... | collective-permute-start | bytes 884744 | tf_op jit(solution)/shard_map/solve/ppermute | solution.py:458
  227.6 8.2 %collective-permute-start.15 = (f32[8,128]{1,0:T(8,128)S(1)}, f32[8,128]{1,0:T(8,128)S(1)}, u32[]{:S(2)}, u32[]{:S(2)}) collective-permute-start(f32[8,128]{1,0:T(8,128)S(1)} %add.53), channel_id=1, source_target_pairs={{0,128},{128,0},{1,129},{129,1},{2,130},{130,2},{3,131},{131,3},{4... | collective-permute-start | bytes 12296 | tf_op jit(solution)/shard_map/solve/ppermute | solution.py:383
  (9 other events, 15.1 us)

commit v2 on v1

v2 whole, which is shorter than its diff:
```python
import functools
import math
import numpy as np
import jax
import jax.numpy as jnp
import ml_dtypes
from jax import lax
from jax.experimental import pallas as pl
from jax.experimental.pallas import tpu as pltpu
from jax.sharding import PartitionSpec as P

BF = jnp.bfloat16
F32 = jnp.float32
MEM = 16
SPREAD_FACTOR = 1.2
LARGE_LIMIT = 52


def split_table(table):
    high = table.astype(ml_dtypes.bfloat16)
    low = (table - high.astype(np.float64)).astype(ml_dtypes.bfloat16)
    return np.stack([high, low])


def zonal_tables(waves, lon_count):
    quarter = lon_count // 4
    columns = quarter + 128
    place = np.arange(columns)
    parts = []
    for parity in (0, 1):
        m = np.arange(parity, waves, 2)
        turn = (m[:, None] * place[None, :]) % lon_count
        angle = turn * (2.0 * math.pi / lon_count)
        for wave in (np.cos(angle), np.sin(angle)):
            wave = wave * math.sqrt(2.0 / lon_count)
            wave[:, quarter + 1 :] = 0.0
            parts.append(split_table(wave))
    return np.stack(parts)


def latitude_table(degrees, bands, rows):
    lat_count = bands * rows
    n = np.arange(degrees)
    out = np.zeros((degrees, bands, 64))
    j = np.arange(lat_count)
    turn = (n[:, None] * (2 * j + 1)[None, :]) % (4 * lat_count)
    out[:, :, :rows] = (np.cos(turn * (math.pi / (2.0 * lat_count))) * math.sqrt(2.0 / lat_count)).reshape(degrees, bands, rows)
    return split_table(out.reshape(degrees, bands * 64))


class Loaded:
    def __init__(self, source, scratch, semaphores, indices, ahead=4):
        self.scratch = scratch
        self.copies = {
            index: pltpu.make_async_copy(source.at[index], scratch.at[index], semaphores.at[place])
            for place, index in enumerate(indices)
        }
        self.to_start = list(indices)
        self.to_wait = set(indices)
        for _ in range(ahead):
            self.start_next()

    def start_next(self):
        if self.to_start:
            self.copies[self.to_start.pop(0)].start()

    def __getitem__(self, index):
        if index in self.to_wait:
            while index in self.to_start:
                self.start_next()
            self.copies[index].wait()
            self.to_wait.remove(index)
            self.start_next()
        return self.scratch[index]


GROUPS = [(group, part) for group in range(4) for part in range(2)]


def halves(x):
    high = x.astype(BF)
    return high, (x - high.astype(F32)).astype(BF)


def lanes_like(x):
    return lax.broadcasted_iota(jnp.int32, x.shape, x.ndim - 1)


def flip_shift(x):
    lanes = lanes_like(x)
    return jnp.take_along_axis(x, (128 - lanes) % 128, axis=-1)


def block(x, q):
    return x[:, 128 * q : 128 * (q + 1)]


def mirrored(x, top, count, keep_first):
    out = []
    for q in range(count):
        body = flip_shift(block(x, top - 1 - q))
        first = lanes_like(body) == 0
        if q == 0 and not keep_first:
            out.append(jnp.where(first, 0.0, body))
        else:
            out.append(jnp.where(first, block(x, top - q), body))
    return jnp.concatenate(out, axis=1)


NT = (((1,), (1,)), ((), ()))
NN = (((1,), (0,)), ((), ()))
TN = (((0,), (0,)), ((), ()))


def dot(a, b, dims=NN):
    return lax.dot_general(a, b, dims, preferred_element_type=F32)


def fold(grid):
    q = grid.shape[1] // 4
    blocks = q // 128
    rows = grid.shape[0]
    zero = jnp.zeros((rows, 128), F32)
    a = grid[:, : q + 128]
    c = grid[:, 2 * q : 3 * q + 128]
    b = jnp.concatenate([mirrored(grid, 2 * blocks, blocks, False), zero], axis=1)
    d = jnp.concatenate([mirrored(grid, 4 * blocks, blocks, False), zero], axis=1)
    ac, bd, amc, bmd = a + c, b + d, a - c, b - d
    return ac + bd, ac - bd, amc - bmd, amc + bmd


def analyse(grid, table, perm):
    rows = grid.shape[0]
    pad = jnp.zeros((64 - rows, grid.shape[1] // 4 + 128), BF)
    parts = fold(grid)
    natural = []
    for parity in (0, 1):
        sums = []
        for c in (0, 1):
            high, low = halves(parts[2 * parity + c])
            both = jnp.concatenate([high, pad, low, pad], axis=0)
            if c == 1:
                both = jnp.concatenate([low, pad, high, pad], axis=0)
            acc = dot(table[2 * parity + c, 0], both, NT) + dot(table[2 * parity + c, 1], both, NT)
            sums.append(acc + pltpu.roll(acc, 64, 1))
        natural.append(jnp.where(lanes_like(sums[0]) < 64, sums[0], sums[1]))
    natural = jnp.concatenate(natural, axis=0)
    high, low = halves(natural)
    moved = dot(perm, jnp.concatenate([high, low], axis=1))
    return moved[:, :128] + moved[:, 128:]


def place_of(wave, waves):
    return wave // 2 + (wave % 2) * (waves // 2)


def to_natural(order_row):
    waves = order_row.shape[1]
    hit = lax.broadcasted_iota(jnp.int32, (waves, waves), 0) == place_of(order_row, waves)
    return hit.astype(F32).astype(BF)


def to_slots(order_row):
    waves = order_row.shape[1]
    place = jnp.broadcast_to(place_of(order_row, waves).astype(F32), (128, waves)).T
    lanes = lanes_like(place)
    hits = [(place == (lanes + first).astype(F32)).astype(F32).astype(BF) for first in range(0, waves, 128)]
    return jnp.concatenate(hits, axis=1)


def synthesise(band, table, perm_t, rows, lon):
    q = lon // 4
    blocks = q // 128
    waves = band.shape[0]
    high, low = halves(band)
    moved = dot(perm_t, jnp.concatenate([high, low], axis=1))
    natural = moved[:, :128] + moved[:, 128:]
    parts = []
    for parity in (0, 1):
        flipped = natural[parity * (waves // 2) : (parity + 1) * (waves // 2)].T
        high, low = halves(flipped)
        for c in (0, 1):
            lhs = jnp.concatenate([high[64 * c : 64 * c + 64], low[64 * c : 64 * c + 64]], axis=0)
            acc = dot(lhs, table[2 * parity + c, 0]) + dot(lhs, table[2 * parity + c, 1])
            parts.append(acc[:rows] + acc[64 : 64 + rows])
    ce, se, co, so = parts
    f1 = (ce + co + se + so)[:, :q]
    a = ce - co - se + so
    f3 = (ce - co + se - so)[:, :q]
    b = ce + co - se - so
    f2 = mirrored(a, blocks, blocks, True)
    f4 = mirrored(b, blocks, blocks, True)
    return jnp.concatenate([f1, f2, f3, f4], axis=1)


def turn(x, by):
    return pltpu.roll(x, by % 128, 1)


def pack(x):
    lanes = lanes_like(x)
    y = jnp.where(lanes < 48, x, turn(x, -16))
    k = x.shape[0] // 4
    a, b, c, d = (y[i * k : (i + 1) * k] for i in range(4))
    lanes = lanes[:k]
    return jnp.concatenate(
        [
            jnp.where(lanes < 96, a, turn(b, 96)),
            jnp.where(lanes < 64, turn(b, -32), turn(c, 64)),
            jnp.where(lanes < 32, turn(c, -64), turn(d, 32)),
        ],
        axis=0,
    )


def unpack(p):
    k = p.shape[0] // 3
    p0, p1, p2 = (p[i * k : (i + 1) * k] for i in range(3))
    lanes = lanes_like(p0)
    y = jnp.concatenate(
        [
            p0,
            jnp.where(lanes < 32, turn(p0, 32), turn(p1, 32)),
            jnp.where(lanes < 64, turn(p1, 64), turn(p2, 64)),
            turn(p2, -32),
        ],
        axis=0,
    )
    lanes = lanes_like(y)
    x = jnp.where(lanes < 48, y, turn(y, 16))
    return jnp.where((lanes < 48) | ((lanes >= 64) & (lanes < 112)), x, 0.0)


def total(x):
    return jnp.sum(jnp.sum(x, axis=0, keepdims=True), axis=1, keepdims=True)


def mark(x, values):
    rows = lax.broadcasted_iota(jnp.int32, x.shape, x.ndim - 2)
    lanes = lanes_like(x)
    for i, value in enumerate(values):
        value = value.reshape((1,) * x.ndim)
        x = jnp.where((rows == 0) & (lanes == 48 + i), value, x)
    return x


def spread(values, level):
    lanes = lax.broadcasted_iota(jnp.int32, (1, 128), 1)
    out = jnp.zeros((1, 128), F32)
    for i, value in enumerate(values):
        out = jnp.where(lanes == 8 * i + level, value, out)
    return out


def quantities(row, count):
    lanes = lanes_like(row)
    return [jnp.where(lanes < 8, turn(row, -8 * i), 0.0) for i in range(count)]


def level_sum(members_ref, level, held, semaphores):
    count = members_ref.shape[0]
    copies = [pltpu.make_async_copy(members_ref.at[k, level], held.at[k], semaphores.at[k]) for k in range(count)]
    for copy in copies:
        copy.start()

    def finish():
        acc = None
        for k in range(count):
            copies[k].wait()
            value = held[k].astype(F32)
            acc = value if acc is None else acc + value
        return acc

    return finish


PIECES = 3


def other_kernel(grp_ref, members_ref, count_ref, row_ref, table_ref, out_ref, sum_ref, held, held_table, sums_sem, table_sem):
    summed = level_sum(members_ref, 1 - grp_ref[0], held, sums_sem)
    table = Loaded(table_ref, held_table, table_sem, GROUPS)
    perm = to_slots(row_ref[...])
    acc = summed()
    sum_ref[...] = acc
    weights = count_ref[...].astype(F32) * 0.5
    out_ref[...] = pack(analyse(-weights * (acc / MEM), table, perm))


def own_kernel(grp_ref, members_ref, obs_ref, count_ref, row_ref, table_ref, out_ref, sum_ref, held, held_table, held_obs, sums_sem, table_sem, obs_sem):
    summed = level_sum(members_ref, grp_ref[0], held, sums_sem)
    obs = pltpu.make_async_copy(obs_ref.at[grp_ref[0]], held_obs, obs_sem)
    obs.start()
    table = Loaded(table_ref, held_table, table_sem, GROUPS)
    perm = to_slots(row_ref[...])
    acc = summed()
    sum_ref[...] = acc
    weights = count_ref[...].astype(F32) * 0.5
    obs.wait()
    out_ref[...] = analyse(weights * (held_obs[...] - acc / MEM), table, perm)


def join_kernel(own_ref, packed_ref, sum_own_ref, sum_other_ref, out_ref, sum_own_out, sum_other_out):
    out_ref[...] = (own_ref[...] + unpack(packed_ref[...])).reshape(out_ref.shape)


LAT_PIECES = 3


def load_latitude(lat_ref, held, semaphores):
    return Loaded(lat_ref, held, semaphores, [(piece, part) for piece in range(LAT_PIECES) for part in range(2)])


def latitude_analysis(chunks_ref, lat):
    bands, slots, _ = chunks_ref.shape
    cos, sin = [], []
    for p in range(bands // 2):
        x0, x1 = chunks_ref[2 * p], chunks_ref[2 * p + 1]
        lower = lanes_like(x0) < 64
        cos.append(jnp.where(lower, x0, turn(x1, 64)))
        sin.append(jnp.where(lower, turn(x0, 64), x1))
    x = jnp.concatenate([jnp.concatenate(cos, axis=1), jnp.concatenate(sin, axis=1)], axis=0)
    high, low = halves(x)
    lhs = jnp.concatenate([high, low], axis=0)
    pieces = []
    for piece in range(LAT_PIECES):
        acc = dot(lhs, lat[piece, 0], NT) + dot(lhs, lat[piece, 1], NT)
        pieces.append(acc[: 2 * slots] + acc[2 * slots :])
    return jnp.concatenate(pieces, axis=1)


def latitude_synthesis(vector, lat, out_ref, values):
    bands, slots, _ = out_ref.shape
    high, low = halves(vector)
    lhs = jnp.concatenate([high, low], axis=0)
    cut = vector.shape[1] // LAT_PIECES
    acc = 0.0
    for piece in range(LAT_PIECES):
        part = lhs[:, piece * cut : (piece + 1) * cut]
        acc = acc + dot(part, lat[piece, 0]) + dot(part, lat[piece, 1])
    y = acc[: 2 * slots] + acc[2 * slots :]
    for p in range(bands // 2):
        y0, y1 = block(y[:slots], p), block(y[slots:], p)
        lower = lanes_like(y0) < 64
        out_ref[2 * p] = mark(jnp.where(lower, y0, turn(y1, 64)), values)
        out_ref[2 * p + 1] = mark(jnp.where(lower, turn(y0, 64), y1), values)


def scale_of(variance, waves_col, degrees):
    slots = waves_col.shape[0]
    degree = lax.broadcasted_iota(jnp.int32, (slots, degrees), 1)
    scale = jnp.where(degree >= waves_col, jnp.sqrt(variance), 0.0)
    return jnp.concatenate([scale, scale], axis=0)


def latitude_first_kernel(chunks_ref, variance_ref, waves_ref, lat_ref, *refs):
    rhs_ref, out_ref, held, semaphores = refs[-4:]
    lat = load_latitude(lat_ref, held, semaphores)
    scale = scale_of(variance_ref[...], waves_ref[...], variance_ref.shape[1])
    rhs = latitude_analysis(chunks_ref, lat) * scale
    rhs_ref[...] = rhs
    latitude_synthesis(rhs * scale, lat, out_ref, [total(rhs * rhs)])


def latitude_second_kernel(chunks_ref, variance_ref, waves_ref, rhs_ref, lat_ref, *refs):
    image_ref, out_ref, quotient_ref, held, semaphores = refs[-5:]
    lat = load_latitude(lat_ref, held, semaphores)
    norm, field_norm = chunks_ref[0, 0:1, 49:50], marks(chunks_ref, 48)
    extra = jnp.where(norm > 0.0, field_norm / norm, 0.0)
    quotient_ref[...] = jnp.broadcast_to(1.0 + extra, (8, 128))
    scale = scale_of(variance_ref[...], waves_ref[...], variance_ref.shape[1])
    image = latitude_analysis(chunks_ref, lat) * scale - extra * rhs_ref[...]
    image_ref[...] = image
    latitude_synthesis(image * scale, lat, out_ref, [])


def marks(band_ref, lane):
    value = jnp.zeros((1, 1), F32)
    for t in range(band_ref.shape[0]):
        value = value + band_ref[t, 0:1, lane : lane + 1]
    return value


def grid_kernel(band_ref, count_ref, row_ref, table_ref, *refs):
    field_ref, out_ref, held, semaphores = refs[-4:]
    table = Loaded(table_ref, held, semaphores, GROUPS)
    bands, slots, _ = band_ref.shape
    rows, lon = count_ref.shape
    row = row_ref[...]
    field = synthesise(band_ref[...].reshape(bands * slots, 128), table, to_natural(row), rows, lon)
    field_ref[...] = field
    weighted = count_ref[...].astype(F32) * 0.5 * field
    out = analyse(weighted, table, to_slots(row)).reshape(bands, slots, 128)
    out_ref[...] = mark(out, [total(weighted * field), marks(band_ref, 48)])


def last_kernel(level_ref, band_ref, count_ref, row_ref, table_ref, field_ref, rhs_ref, image_ref, quotient_ref, *refs):
    next_ref, sums_ref, held, semaphores = refs[-4:]
    table = Loaded(table_ref, held, semaphores, GROUPS)
    bands, slots, _ = band_ref.shape
    rows, lon = count_ref.shape
    rhs, image, start = rhs_ref[...], image_ref[...], field_ref[...]
    weights = count_ref[...].astype(F32) * 0.5
    field = synthesise(band_ref[...].reshape(bands * slots, 128), table, to_natural(row_ref[...]), rows, lon)
    next_ref[...] = field
    weighted = weights * field
    row = spread(
        [
            total(rhs * rhs),
            total(weights * start * start),
            total(image * image),
            total(image * rhs),
            total(weighted * field),
            total(weighted * start),
            quotient_ref[0:1, 0:1] / bands,
        ],
        level_ref[0],
    )
    sums_ref[...] = jnp.broadcast_to(row[None], sums_ref.shape)


def combine_kernel(level_ref, sums_ref, sums_in_ref, rhs_ref, image_ref, first_ref, second_ref, control_ref, packed_ref, factors_ref):
    bands, slots, _ = first_ref.shape
    sums = sums_ref[...] + sums_in_ref[...]
    norm, field_norm, image_norm, cross, next_norm, field_cross, quotient = quantities(sums, 7)

    def over_levels(x):
        return jnp.sum(x, axis=1, keepdims=True)

    norm_all, field_all = over_levels(norm), over_levels(field_norm)
    step = norm_all / (norm_all + field_all)
    keep = 1.0 - step * quotient
    norm_next = over_levels(keep * keep * norm - 2.0 * step * keep * cross + step * step * image_norm)
    field_next = over_levels(keep * keep * field_norm - 2.0 * step * keep * field_cross + step * step * next_norm)
    mixed = over_levels(keep * (norm + field_norm) - step * (cross + field_cross))
    ratio = norm_next / norm_all
    curve = norm_next + field_next + 2.0 * ratio * mixed + ratio * ratio * (norm_all + field_all)
    step_next = norm_next / curve
    mine = lanes_like(keep) == level_ref[0]
    first = over_levels(jnp.where(mine, step + step_next * (keep + ratio), 0.0))
    second = -step_next * step
    control_ref[...] = first * rhs_ref[...] + second * image_ref[...]
    band = first * first_ref[...].reshape(bands * slots, 128) + second * second_ref[...].reshape(bands * slots, 128)
    packed_ref[...] = pack(band)
    lanes = lanes_like(sums)
    factors_ref[...] = jnp.where(lanes == 0, first, jnp.where(lanes == 1, second, 0.0))


class Recentering:
    def __init__(self, members_ref, level, sums, out_ref, scratch):
        self.near, self.near_sums, self.held, near_sem, sums_sem, self.out_sem = scratch
        self.out_ref, self.level = out_ref, level
        rows = members_ref.shape[2]
        self.cut = rows // PIECES
        self.loads = []
        for piece in range(PIECES):
            source = members_ref.at[:, level, pl.ds(piece * self.cut, self.cut)]
            self.loads.append(pltpu.make_async_copy(source, self.near.at[piece], near_sem.at[piece]))
        self.sum_loads = [
            pltpu.make_async_copy(source.at[index], self.near_sums.at[k], sums_sem.at[k]) for k, (source, index) in enumerate(sums)
        ]
        for copy in self.sum_loads + self.loads:
            copy.start()

    def run(self, increment):
        for copy in self.sum_loads:
            copy.wait()
        copies = []
        for piece in range(PIECES):
            here = slice(piece * self.cut, (piece + 1) * self.cut)
            mean = (self.near_sums[0, here] + self.near_sums[1, here]) / MEM
            offset = (mean + increment(here)) - SPREAD_FACTOR * mean
            self.loads[piece].wait()
            for k in range(self.near.shape[1]):
                self.held[piece, k] = (SPREAD_FACTOR * self.near[piece, k].astype(F32) + offset).astype(BF)
            target = self.out_ref.at[:, self.level, pl.ds(piece * self.cut, self.cut)]
            copies.append(pltpu.make_async_copy(self.held.at[piece], target, self.out_sem.at[piece]))
            copies[-1].start()
        for copy in copies:
            copy.wait()


def finish_own_kernel(grp_ref, members_ref, sums_own_ref, sums_other_ref, factors_ref, start_ref, next_ref, out_ref, *scratch):
    me = grp_ref[0]
    work = Recentering(members_ref, me, ((sums_own_ref, me), (sums_other_ref, 1 - me)), out_ref, scratch)
    first, second = factors_ref[0:1, 0:1], factors_ref[0:1, 1:2]
    work.run(lambda here: first * start_ref[here] + second * next_ref[here])


def finish_other_kernel(grp_ref, members_ref, sums_own_ref, sums_other_ref, packed_ref, row_ref, table_ref, half_ref, out_ref, *scratch):
    held_table, table_sem, scratch = scratch[0], scratch[1], scratch[2:]
    table = Loaded(table_ref, held_table, table_sem, GROUPS)
    me = grp_ref[0]
    work = Recentering(members_ref, 1 - me, ((sums_own_ref, 1 - me), (sums_other_ref, me)), out_ref, scratch)
    rows, lon = members_ref.shape[2:]
    field = synthesise(unpack(packed_ref[...]), table, to_natural(row_ref[...]), rows, lon)
    work.run(lambda here: field[here])


def shape(*dims):
    return jax.ShapeDtypeStruct(dims, F32)


def call(kernel, outs, name, hbm=(), hbm_outs=(), scalars=(), aliases=None, scratch=(), limit=LARGE_LIMIT):
    def run(*args):
        def space(i, far, scalars=()):
            return pltpu.SMEM if i in scalars else pltpu.HBM if i in far else pltpu.VMEM

        return pl.pallas_call(
            kernel,
            out_shape=outs,
            in_specs=[pl.BlockSpec(memory_space=space(i, hbm, scalars)) for i in range(len(args))],
            out_specs=[pl.BlockSpec(memory_space=space(o, hbm_outs)) for o in range(len(outs))],
            input_output_aliases=aliases or {},
            scratch_shapes=scratch,
            compiler_params=pltpu.CompilerParams(vmem_limit_bytes=limit * 2**20),
            cost_estimate=pl.CostEstimate(flops=1, bytes_accessed=1, transcendentals=0),
            name=name,
        )(*args)

    return run


def butterfly(value, axis, count):
    step = 1
    while step < count:
        value = value + lax.ppermute(value, axis, [(i, i ^ step) for i in range(count)])
        step *= 2
    return value


def on_device(tables, lat_table, members, obs_value, obs_count, variance, wave_order):
    grp = lax.axis_index("grp")
    bands = lax.axis_size("tile")
    levels = lax.axis_size("lev")
    mem, _, rows, lon = members.shape
    waves = wave_order.shape[0]
    slots = waves // bands
    degrees = variance.shape[1]
    swap = [(0, 1), (1, 0)]
    own_waves = lax.dynamic_slice_in_dim(wave_order, lax.axis_index("tile") * slots, slots, 0)[:, None]
    own_variance = lax.dynamic_index_in_dim(variance, grp, 0, keepdims=True)
    row = wave_order[None, :]
    grp_scalar = grp[None].astype(jnp.int32)

    chunk = shape(bands, slots, 128)
    packed = shape(waves * 3 // 4, 128)
    field = shape(rows, lon)
    vector = shape(2 * slots, degrees)
    small = shape(8, 128)
    dma = pltpu.SemaphoreType.DMA
    zonal = [pltpu.VMEM(tables.shape, BF), dma((len(GROUPS),))]
    latitude = [pltpu.VMEM(lat_table.shape, BF), dma((2 * LAT_PIECES,))]
    level = pltpu.VMEM((mem, rows, lon), BF)
    cut = rows // PIECES
    level_scalar = (2 * lax.axis_index("lev") + grp)[None].astype(jnp.int32)

    def trade(array):
        return lax.ppermute(array, "grp", swap)

    with jax.named_scope("start"):
        coeffs_other, sum_other = call(
            other_kernel, [packed, field], "other", (1, 4), scalars=(0,), scratch=[level, zonal[0], dma((mem,)), zonal[1]]
        )(grp_scalar, members, obs_count, row, tables)
        coeffs_in = trade(coeffs_other)
        coeffs_own, sum_own = call(
            own_kernel,
            [shape(waves, 128), field],
            "own",
            (1, 2, 5),
            scalars=(0,),
            scratch=[level, zonal[0], pltpu.VMEM((rows, lon), F32), dma((mem,)), zonal[1], dma],
        )(grp_scalar, members, obs_value, obs_count, row, tables)
        coeffs, sum_own, sum_other = call(join_kernel, [chunk, field, field], "join", (2, 3), (1, 2), aliases={2: 1, 3: 2})(
            coeffs_own, coeffs_in, sum_own, sum_other
        )
        sums_own = lax.all_gather(sum_own, "grp")
        sums_other = lax.all_gather(sum_other, "grp")

    def exchange(chunks):
        return lax.all_to_all(chunks, "tile", 0, 0, tiled=True)

    with jax.named_scope("solve"):
        rhs, lat_values = call(latitude_first_kernel, [vector, chunk], "lat1", (3,), scratch=latitude)(
            exchange(coeffs), own_variance, own_waves, lat_table
        )
        band_first = exchange(lat_values)
        field_own, coeffs = call(grid_kernel, [field, chunk], "grid", (3,), scratch=zonal)(
            band_first, obs_count, row, tables
        )
        image, lat_values, quotient = call(latitude_second_kernel, [vector, chunk, small], "lat2", (4,), scratch=latitude)(
            exchange(coeffs), own_variance, own_waves, rhs, lat_table
        )
        band_second = exchange(lat_values)
        sum_row = jax.ShapeDtypeStruct((bands, 1, 128), F32)
        next_own, sums = call(last_kernel, [field, sum_row], "last", (4,), scalars=(0,), scratch=zonal)(
            level_scalar, band_second, obs_count, row, tables, field_own, rhs, image, quotient
        )
        sums = jnp.sum(exchange(sums), axis=0)
        sums = sums + sum(lax.ppermute(sums, "lev", [(i, (i + k) % levels) for i in range(levels)]) for k in range(1, levels))

    with jax.named_scope("finish"):
        control, control_band, factors = call(combine_kernel, [vector, packed, shape(1, 128)], "combine", scalars=(0,), limit=16)(
            level_scalar, sums, trade(sums), rhs, image, band_first, band_second
        )
        control_band = trade(control_band)
        near = pltpu.VMEM((PIECES, mem, cut, lon), BF)
        scratch = [near, pltpu.VMEM((2, rows, lon), F32), near, dma((PIECES,)), dma((2,)), dma((PIECES,))]
        whole_out = jax.ShapeDtypeStruct(members.shape, BF)
        (half,) = call(finish_own_kernel, [whole_out], "finish_own", (1, 2, 3), (0,), scalars=(0,), scratch=scratch, limit=56)(
            grp_scalar, members, sums_own, sums_other, factors, field_own, next_own
        )
        (recentered,) = call(
            finish_other_kernel, [whole_out], "finish_other", (1, 2, 3, 6, 7), (0,), scalars=(0,), aliases={7: 0}, scratch=zonal + scratch, limit=56
        )(grp_scalar, members, sums_own, sums_other, control_band, row, tables, half)
    return recentered, control.reshape(1, 1, 2, slots, degrees)


def solution(mesh):
    bands = mesh.shape["tile"]
    waves, degrees, rows, lon = 768, 768, 48, 3072
    tables = zonal_tables(waves, lon)
    lat_table = latitude_table(degrees, bands, rows)
    lat_table = lat_table.reshape(2, LAT_PIECES, degrees // LAT_PIECES, -1).swapaxes(0, 1)
    placed = (
        P("grp", "lev", "tile", None),
        P("lev", "tile", None),
        P("tile", None),
        P("lev", None),
        P(),
    )
    return jax.shard_map(
        lambda *args: on_device(jnp.asarray(tables), jnp.asarray(lat_table), *args),
        mesh=mesh,
        in_specs=placed,
        out_specs=(P("grp", "lev", "tile", None), P("lev", "grp", None, "tile", None)),
        check_vma=False,
    )
```

time: 259 us -> 184 us (0.71)
  waiting for transfers between devices: 88.7 us -> 48.8 us
  starting transfers between devices: 59 us -> 34.7 us
  Pallas kernels: 69.6 us -> 52.4 us
  between operations: 0.77 us -> 14.2 us
  other arithmetic: 13.1 us -> 0.06 us
  blocking collectives: 13.8 us -> 24.8 us
    ppermute x16 -> x6, waiting for transfers between devices: 70.9 us -> 19.9 us  [the longest x3 16.3 us: trade(): return lax.ppermute(array, 'grp', swap)]
    ppermute x16 -> x6, starting transfers between devices: 43.7 us -> 19.3 us  [the longest x3 16.1 us: trade(): return lax.ppermute(array, 'grp', swap)]
    pallas_call x11 -> x10, Pallas kernels: 69.6 us -> 52.4 us  [run(): pl.pallas_call(kernel, out_shape=outs, in_specs=[pl.BlockSpec(memory_spac...]
    all_to_all x1 -> x2, blocking collectives: 13.8 us -> 24.8 us  [exchange(): return lax.all_to_all(chunks, 'tile', 0, 0, tiled=True)]
    all_to_all x3, waiting for transfers between devices: 17.8 us -> 28.2 us  [exchange(): return lax.all_to_all(chunks, 'tile', 0, 0, tiled=True)]
    another operation x4 -> x0, other arithmetic: 6.69 us -> none  [the longest x1 2.24 us: on_device(): jnp.stack([field_own, field_other])]
    add x11 -> x1, other arithmetic: 4.43 us -> 0.01 us  [on_device(): sums + sum((lax.ppermute(sums, 'lev', [(i, (i + k) % levels) for i in ran...]
  transfers between devices with their start and end apart: 19 -> 11, of which waited for: 11 -> 9; matrix products, arithmetic and copies ran while one was open for 4% -> 1% of each run, Pallas kernels for 12% -> 21%
where the time goes in v2:
time: 184 us; the launch traced here: 181 us
  Pallas kernels  52.4 us (28%)
  waiting for transfers between devices  48.8 us (27%)
  starting transfers between devices  34.7 us (19%)
  blocking collectives  24.8 us (13%)
  between operations  14.2 us (8%)
  local copies, waits for them, and re-layouts  6.3 us (3%)
    pallas_call x10, Pallas kernels, run(): pl.pallas_call(kernel, out_shape=outs, in_specs=[pl.BlockSpec(memory_spac...  52.4 us
    all_to_all x3, waiting for transfers between devices, exchange(): return lax.all_to_all(chunks, 'tile', 0, 0, tiled=True)  28.2 us
    all_to_all x2, blocking collectives, exchange(): return lax.all_to_all(chunks, 'tile', 0, 0, tiled=True)  24.8 us
    ppermute x3, waiting for transfers between devices, trade(): return lax.ppermute(array, 'grp', swap)  16.3 us
    ppermute x3, starting transfers between devices, trade(): return lax.ppermute(array, 'grp', swap)  16.1 us
    all_to_all x3, starting transfers between devices, exchange(): return lax.all_to_all(chunks, 'tile', 0, 0, tiled=True)  15.3 us
    unnamed x18, local copies, waits for them, and re-layouts  4.75 us
  transfers between devices with their start and end apart: 11, of which 9 were waited for; matrix products, arithmetic and copies ran while one was open for 1% of the time, Pallas kernels for 21%

profile of v2, /device:TPU:32, one launch (start us, length us, event | category | flops | bytes accessed | tf_op | source)
XLA Modules:
  0.0 181.3 jit_solution(15367745530024568278)
XLA Ops:
  9.0 5.9 %other.1 = (f32[576,128]{1,0:T(8,128)S(1)}, f32[48,3072]{1,0:T(8,128)S(1)}) custom-call(s32[1]{0:T(128)} %bitcast.grp_ref, bf16[8,2,48,3072]{3,2,1,0:T(8,128)(2,1)} %members_ref.7, s32[48,3072]{1,0:T(8,128)S(1)} %copy-done.1, s32[1,768]{1,0:T(1,128)S(1)} %broadcast_in_dim.13.row_ref, bf16[4,2,384,896]{3,2,1,0:T(8,128)(2,1)} %constant.33.clone.table_ref), custom_call_target="tpu_custom_call" | custom-call | flops 1 | bytes 1 | tf_op jit(solution)/shard_map/start/other/pallas_call | solution.py:509
  15.7 6.3 %collective-permute-start = (f32[576,128]{1,0:T(8,128)S(1)}, f32[576,128]{1,0:T(8,128)S(1)}, u32[]{:S(2)}, u32[]{:S(2)}) collective-permute-start(f32[576,128]{1,0:T(8,128)S(1)} %get-tuple-element.22), channel_id=1, source_target_pairs={{0,128},{128,0},{1,129},{129,1},{2,130},{130,2},{3,131},{131,3},{4... | collective-permute-start | bytes 884744 | tf_op jit(solution)/shard_map/start/ppermute | solution.py:559
  22.0 6.0 %own.1 = (f32[768,128]{1,0:T(8,128)S(1)}, f32[48,3072]{1,0:T(8,128)}) custom-call(s32[1]{0:T(128)} %bitcast.grp_ref, bf16[8,2,48,3072]{3,2,1,0:T(8,128)(2,1)} %members_ref.7, f32[2,48,3072]{2,1,0:T(8,128)} %obs_ref.1, s32[48,3072]{1,0:T(8,128)S(1)} %copy-done.1, s32[1,768]{1,0:T(1,128)S(1)} %broadcast_in_dim.13.row_ref, ...), custom_call_target="tpu_custom_call" | custom-call | flops 1 | bytes 1 | tf_op jit(solution)/shard_map/start/own/pallas_call | solution.py:509
  28.0 7.4 %collective-permute-done.packed_ref = f32[576,128]{1,0:T(8,128)S(1)} collective-permute-done((f32[576,128]{1,0:T(8,128)S(1)}, f32[576,128]{1,0:T(8,128)S(1)}, u32[]{:S(2)}, u32[]{:S(2)}) %collective-permute-start) | collective-permute-done | bytes 294944 | tf_op jit(solution)/shard_map/start/ppermute | solution.py:559
  36.5 7.5 %all-to-all-start = ((f32[32,24,128]{2,1,0:T(8,128)}), f32[32,24,128]{2,1,0:T(8,128)S(1)}, u32[]{:S(2)}, u32[]{:S(2)}) async-start(f32[32,24,128]{2,1,0:T(8,128)} %get-tuple-element.27), calls=%async_computation | async-start | bytes 786432 | tf_op jit(solution)/shard_map/solve/all_to_all | solution.py:581
  44.8 9.1 %all-to-all-done.chunks_ref = f32[32,24,128]{2,1,0:T(8,128)S(1)} async-done(((f32[32,24,128]{2,1,0:T(8,128)}), f32[32,24,128]{2,1,0:T(8,128)S(1)}, u32[]{:S(2)}, u32[]{:S(2)}) %all-to-all-start) | async-done | bytes 393248 | tf_op jit(solution)/shard_map/solve/all_to_all | solution.py:581
  53.9 6.2 %lat1.1 = (f32[48,768]{1,0:T(8,128)S(1)}, f32[32,24,128]{2,1,0:T(8,128)S(1)}) custom-call(f32[32,24,128]{2,1,0:T(8,128)S(1)} %all-to-all-done.chunks_ref, f32[1,768]{1,0:T(1,128)S(1)} %constant_dynamic-slice_fusion.variance_ref, s32[24,1]{1,0:T(8,128)S(1)} %copy.12.waves_ref, bf16[3,2,256,2048]{3,2,1,0:T(8,128)(2,1)} %constant.34.clone.lat_ref), custom_call_target="tpu_custom_call" | custom-call | flops 1 | bytes 1 | tf_op jit(solution)/shard_map/solve/lat1/pallas_call | solution.py:509
  60.1 13.8 %all_to_all.25.band_ref.first_ref = f32[32,24,128]{2,1,0:T(8,128)S(1)} all-to-all(f32[32,24,128]{2,1,0:T(8,128)S(1)} %get-tuple-element.28), channel_id=1, replica_groups=mesh['grp'=2,'tile'=32,'lev'=4] {'tile'}, dimensions={0} | all-to-all | bytes 786432 | tf_op jit(solution)/shard_map/solve/all_to_all | solution.py:581
  73.9 7.1 %grid.1 = (f32[48,3072]{1,0:T(8,128)S(1)}, f32[32,24,128]{2,1,0:T(8,128)}) custom-call(f32[32,24,128]{2,1,0:T(8,128)S(1)} %all_to_all.25.band_ref.first_ref, s32[48,3072]{1,0:T(8,128)S(1)} %copy-done.2, s32[1,768]{1,0:T(1,128)S(1)} %broadcast_in_dim.13.row_ref, bf16[4,2,384,896]{3,2,1,0:T(8,128)(2,1)} %constant.33.clone.table_ref), custom_call_target="tpu_custom_call" | custom-call | flops 1 | bytes 1 | tf_op jit(solution)/shard_map/solve/grid/pallas_call | solution.py:509
  81.8 3.9 %all-to-all-start.2 = ((f32[32,24,128]{2,1,0:T(8,128)}), f32[32,24,128]{2,1,0:T(8,128)S(1)}, u32[]{:S(2)}, u32[]{:S(2)}) async-start(f32[32,24,128]{2,1,0:T(8,128)} %get-tuple-element.29), calls=%async_computation.2 | async-start | bytes 786432 | tf_op jit(solution)/shard_map/solve/all_to_all | solution.py:581
  86.5 9.2 %all-to-all-done.2.chunks_ref = f32[32,24,128]{2,1,0:T(8,128)S(1)} async-done(((f32[32,24,128]{2,1,0:T(8,128)}), f32[32,24,128]{2,1,0:T(8,128)S(1)}, u32[]{:S(2)}, u32[]{:S(2)}) %all-to-all-start.2) | async-done | bytes 393248 | tf_op jit(solution)/shard_map/solve/all_to_all | solution.py:581
  95.7 7.1 %lat2.1 = (f32[48,768]{1,0:T(8,128)S(1)}, f32[32,24,128]{2,1,0:T(8,128)}, f32[8,128]{1,0:T(8,128)S(1)}) custom-call(f32[32,24,128]{2,1,0:T(8,128)S(1)} %all-to-all-done.2.chunks_ref, f32[1,768]{1,0:T(1,128)S(1)} %constant_dynamic-slice_fusion.variance_ref, s32[24,1]{1,0:T(8,128)S(1)} %copy.12.waves_ref, f32[48,768]{1,0:T(8,128)S(1)} %get-tuple-element.30.rhs_ref, ...), custom_call_target="tpu_custom_call" | custom-call | flops 1 | bytes 1 | tf_op jit(solution)/shard_map/solve/lat2/pallas_call | solution.py:509
  102.7 3.9 %all-to-all-start.3 = ((f32[32,24,128]{2,1,0:T(8,128)}), f32[32,24,128]{2,1,0:T(8,128)S(1)}, u32[]{:S(2)}, u32[]{:S(2)}) async-start(f32[32,24,128]{2,1,0:T(8,128)} %get-tuple-element.31), calls=%async_computation.3 | async-start | bytes 786432 | tf_op jit(solution)/shard_map/solve/all_to_all | solution.py:581
  106.7 9.9 %all-to-all-done.3.band_ref.second_ref = f32[32,24,128]{2,1,0:T(8,128)S(1)} async-done(((f32[32,24,128]{2,1,0:T(8,128)}), f32[32,24,128]{2,1,0:T(8,128)S(1)}, u32[]{:S(2)}, u32[]{:S(2)}) %all-to-all-start.3) | async-done | bytes 393248 | tf_op jit(solution)/shard_map/solve/all_to_all | solution.py:581
  116.6 5.8 %last.1 = (f32[48,3072]{1,0:T(8,128)S(1)}, f32[32,1,128]{2,1,0:T(1,128)S(1)}) custom-call(s32[1]{0:T(128)} %bitcast.3.level_ref, f32[32,24,128]{2,1,0:T(8,128)S(1)} %all-to-all-done.3.band_ref.second_ref, s32[48,3072]{1,0:T(8,128)S(1)} %copy-done.2, s32[1,768]{1,0:T(1,128)S(1)} %broadcast_in_dim.13.row_ref, ...), custom_call_target="tpu_custom_call" | custom-call | flops 1 | bytes 1 | tf_op jit(solution)/shard_map/solve/last/pallas_call | solution.py:509
  123.3 11.0 %all_to_all.26 = f32[32,1,128]{2,1,0:T(1,128)S(1)} all-to-all(f32[32,1,128]{2,1,0:T(1,128)S(1)} %get-tuple-element.35), channel_id=1, replica_groups=mesh['grp'=2,'tile'=32,'lev'=4] {'tile'}, dimensions={0} | all-to-all | bytes 32768 | tf_op jit(solution)/shard_map/solve/all_to_all | solution.py:581
  134.7 2.9 %collective-permute-start.2 = (f32[1,128]{1,0:T(1,128)S(1)}, f32[1,128]{1,0:T(1,128)S(1)}, u32[]{:S(2)}, u32[]{:S(2)}) collective-permute-start(f32[1,128]{1,0:T(1,128)S(1)} %bitcast.14), channel_id=1, source_target_pairs={{0,2},{1,3},{2,0},{3,1},{4,6},{5,7},{6,4},{7,5},{8,10},{9,11},{10,... | collective-permute-start | bytes 1544 | tf_op jit(solution)/shard_map/solve/ppermute | solution.py:600
  139.2 1.9 %collective-permute-done.1 = f32[1,128]{1,0:T(1,128)S(1)} collective-permute-done((f32[1,128]{1,0:T(1,128)S(1)}, f32[1,128]{1,0:T(1,128)S(1)}, u32[]{:S(2)}, u32[]{:S(2)}) %collective-permute-start.1) | collective-permute-done | bytes 544 | tf_op jit(solution)/shard_map/solve/ppermute | solution.py:600
  141.1 4.9 %collective-permute-start.4 = (f32[1,128]{1,0:T(1,128)S(1)}, f32[1,128]{1,0:T(1,128)S(1)}, u32[]{:S(2)}, u32[]{:S(2)}) collective-permute-start(f32[1,128]{1,0:T(1,128)S(1)} %add_add_fusion.sums_ref), channel_id=1, source_target_pairs={{0,128},{128,0},{1,129},{129,1},{2,130},{130,2},{3,131},{131,3},{4... | collective-permute-start | bytes 1544 | tf_op jit(solution)/shard_map/finish/ppermute | solution.py:559
  146.0 2.5 %collective-permute-done.4.sums_in_ref = f32[1,128]{1,0:T(1,128)S(1)} collective-permute-done((f32[1,128]{1,0:T(1,128)S(1)}, f32[1,128]{1,0:T(1,128)S(1)}, u32[]{:S(2)}, u32[]{:S(2)}) %collective-permute-start.4) | collective-permute-done | bytes 544 | tf_op jit(solution)/shard_map/finish/ppermute | solution.py:559
  150.2 4.9 %collective-permute-start.5 = (f32[576,128]{1,0:T(8,128)S(1)}, f32[576,128]{1,0:T(8,128)S(1)}, u32[]{:S(2)}, u32[]{:S(2)}) collective-permute-start(f32[576,128]{1,0:T(8,128)S(1)} %get-tuple-element.36), channel_id=1, source_target_pairs={{0,128},{128,0},{1,129},{129,1},{2,130},{130,2},{3,131},{131,3},{4... | collective-permute-start | bytes 884744 | tf_op jit(solution)/shard_map/finish/ppermute | solution.py:559
  155.2 4.8 %finish_own.1.half_ref = bf16[8,2,48,3072]{3,2,1,0:T(8,128)(2,1)} custom-call(s32[1]{0:T(128)} %bitcast.grp_ref, bf16[8,2,48,3072]{3,2,1,0:T(8,128)(2,1)} %members_ref.7, f32[2,48,3072]{2,1,0:T(8,128)} %bitcast.9, f32[2,48,3072]{2,1,0:T(8,128)} %bitcast.11, f32[1,128]{1,0:T(1,128)} %copy-done.7, f32[48,3072]{1,0:T(8,128)} %copy-done.3, f32[48,3072]{1,0:T(8,128)} %copy-done.5), custom_call_target="tpu_custom_call" | custom-call | flops 1 | bytes 1 | tf_op jit(solution)/shard_map/finish/finish_own/pallas_call | solution.py:509
  160.0 6.4 %collective-permute-done.5.packed_ref = f32[576,128]{1,0:T(8,128)S(1)} collective-permute-done((f32[576,128]{1,0:T(8,128)S(1)}, f32[576,128]{1,0:T(8,128)S(1)}, u32[]{:S(2)}, u32[]{:S(2)}) %collective-permute-start.5) | collective-permute-done | bytes 294944 | tf_op jit(solution)/shard_map/finish/ppermute | solution.py:559
  167.1 7.3 %finish_other.1 = bf16[8,2,48,3072]{3,2,1,0:T(8,128)(2,1)} custom-call(s32[1]{0:T(128)} %bitcast.grp_ref, bf16[8,2,48,3072]{3,2,1,0:T(8,128)(2,1)} %members_ref.7, f32[2,48,3072]{2,1,0:T(8,128)} %bitcast.10, f32[2,48,3072]{2,1,0:T(8,128)} %bitcast.12, f32[576,128]{1,0:T(8,128)} %copy-done.8, s32[1,768]{1,0:T(1,128)} %copy-done.6, ...), custom_call_target="tpu_custom_call", output_to_operand_aliasing={{}: (7, {})} | custom-call | flops 1 | bytes 1 | tf_op jit(solution)/shard_map/finish/finish_other/pallas_call | solution.py:509
  (36 shorter events, 11.3 us)
Async XLA Ops:
  7.2 37.7 %copy-start = (f32[2,768]{1,0:T(2,128)S(1)}, f32[2,768]{1,0:T(2,128)}, u32[]{:S(2)}) copy-start(f32[2,768]{1,0:T(2,128)} %param.10) | copy-start | bytes 18436
  7.2 148.0 %all-gather.5.cloned.1.call-start = ((), (), s32[]{:S(2)}) async-start(), calls=%async_computation.5 | async-start | bytes 1769472 | tf_op jit(solution)/shard_map/start/all_gather | solution.py:577
  7.9 108.7 %copy-start.6 = (s32[1,768]{1,0:T(1,128)}, s32[1,768]{1,0:T(1,128)S(1)}, u32[]{:S(2)}) copy-start(s32[1,768]{1,0:T(1,128)S(1)} %broadcast_in_dim.13.row_ref) | copy-start | bytes 9220
  7.9 1.1 copy-start.1
  14.9 0.8 copy-start.4
  15.7 19.7 %collective-permute-start = (f32[576,128]{1,0:T(8,128)S(1)}, f32[576,128]{1,0:T(8,128)S(1)}, u32[]{:S(2)}, u32[]{:S(2)}) collective-permute-start(f32[576,128]{1,0:T(8,128)S(1)} %get-tuple-element.22), channel_id=1, source_target_pairs={{0,128},{128,0},{1,129},{129,1},{2,130},{130,2},{3,131},{131,3},{4... | collective-permute-start | bytes 884744 | tf_op jit(solution)/shard_map/start/ppermute | solution.py:559
  36.5 37.5 %copy-start.2 = (s32[48,3072]{1,0:T(8,128)S(1)}, s32[48,3072]{1,0:T(8,128)}, u32[]{:S(2)}) copy-start(s32[48,3072]{1,0:T(8,128)} %count_ref.7) | copy-start | bytes 1769476
  36.5 17.4 %all-to-all-start = ((f32[32,24,128]{2,1,0:T(8,128)}), f32[32,24,128]{2,1,0:T(8,128)S(1)}, u32[]{:S(2)}, u32[]{:S(2)}) async-start(f32[32,24,128]{2,1,0:T(8,128)} %get-tuple-element.27), calls=%async_computation | async-start | bytes 786432 | tf_op jit(solution)/shard_map/solve/all_to_all | solution.py:581
  81.0 0.8 copy-start.3
  81.8 13.9 %all-to-all-start.2 = ((f32[32,24,128]{2,1,0:T(8,128)}), f32[32,24,128]{2,1,0:T(8,128)S(1)}, u32[]{:S(2)}, u32[]{:S(2)}) async-start(f32[32,24,128]{2,1,0:T(8,128)} %get-tuple-element.29), calls=%async_computation.2 | async-start | bytes 786432 | tf_op jit(solution)/shard_map/solve/all_to_all | solution.py:581
  85.7 69.4 %all-gather.7.cloned.1.call-start = ((), (), s32[]{:S(2)}) async-start(), calls=%async_computation.6 | async-start | bytes 1769472 | tf_op jit(solution)/shard_map/start/all_gather | solution.py:578
  102.7 13.9 %all-to-all-start.3 = ((f32[32,24,128]{2,1,0:T(8,128)}), f32[32,24,128]{2,1,0:T(8,128)S(1)}, u32[]{:S(2)}, u32[]{:S(2)}) async-start(f32[32,24,128]{2,1,0:T(8,128)} %get-tuple-element.31), calls=%async_computation.3 | async-start | bytes 786432 | tf_op jit(solution)/shard_map/solve/all_to_all | solution.py:581
  122.4 0.8 copy-start.5
  134.4 3.8 %collective-permute-start.3 = (f32[1,128]{1,0:T(1,128)S(1)}, f32[1,128]{1,0:T(1,128)S(1)}, u32[]{:S(2)}, u32[]{:S(2)}) collective-permute-start(f32[1,128]{1,0:T(1,128)S(1)} %bitcast.13), channel_id=1, source_target_pairs={{0,3},{1,0},{2,1},{3,2},{4,7},{5,4},{6,5},{7,6},{8,11},{9,8},{10,9... | collective-permute-start | bytes 1544 | tf_op jit(solution)/shard_map/solve/ppermute | solution.py:600
  134.7 4.5 %collective-permute-start.2 = (f32[1,128]{1,0:T(1,128)S(1)}, f32[1,128]{1,0:T(1,128)S(1)}, u32[]{:S(2)}, u32[]{:S(2)}) collective-permute-start(f32[1,128]{1,0:T(1,128)S(1)} %bitcast.14), channel_id=1, source_target_pairs={{0,2},{1,3},{2,0},{3,1},{4,6},{5,7},{6,4},{7,5},{8,10},{9,11},{10,... | collective-permute-start | bytes 1544 | tf_op jit(solution)/shard_map/solve/ppermute | solution.py:600
  137.5 3.5 %collective-permute-start.1 = (f32[1,128]{1,0:T(1,128)S(1)}, f32[1,128]{1,0:T(1,128)S(1)}, u32[]{:S(2)}, u32[]{:S(2)}) collective-permute-start(f32[1,128]{1,0:T(1,128)S(1)} %bitcast.15), channel_id=1, source_target_pairs={{0,1},{1,2},{2,3},{3,0},{4,5},{5,6},{6,7},{7,4},{8,9},{9,10},{10,1... | collective-permute-start | bytes 1544 | tf_op jit(solution)/shard_map/solve/ppermute | solution.py:600
  141.1 7.4 %collective-permute-start.4 = (f32[1,128]{1,0:T(1,128)S(1)}, f32[1,128]{1,0:T(1,128)S(1)}, u32[]{:S(2)}, u32[]{:S(2)}) collective-permute-start(f32[1,128]{1,0:T(1,128)S(1)} %add_add_fusion.sums_ref), channel_id=1, source_target_pairs={{0,128},{128,0},{1,129},{129,1},{2,130},{130,2},{3,131},{131,3},{4... | collective-permute-start | bytes 1544 | tf_op jit(solution)/shard_map/finish/ppermute | solution.py:559
  149.7 0.5 copy-start.7
  150.2 16.2 %collective-permute-start.5 = (f32[576,128]{1,0:T(8,128)S(1)}, f32[576,128]{1,0:T(8,128)S(1)}, u32[]{:S(2)}, u32[]{:S(2)}) collective-permute-start(f32[576,128]{1,0:T(8,128)S(1)} %get-tuple-element.36), channel_id=1, source_target_pairs={{0,128},{128,0},{1,129},{129,1},{2,130},{130,2},{3,131},{131,3},{4... | collective-permute-start | bytes 884744 | tf_op jit(solution)/shard_map/finish/ppermute | solution.py:559
  166.4 0.7 copy-start.8
Sparse Core Ops, SparseCore 0:
  36.6 45.3 all-gather.4
  88.4 45.2 all-gather.6

commit v3 on v2

--- a/solution.py
+++ b/solution.py
@@ -12,6 +12,7 @@
 BF = jnp.bfloat16
 F32 = jnp.float32
 MEM = 16
+ROWS = 48
 SPREAD_FACTOR = 1.2
 LARGE_LIMIT = 52
 
@@ -40,12 +41,12 @@
 
 def latitude_table(degrees, bands, rows):
     lat_count = bands * rows
-    n = np.arange(degrees)
-    out = np.zeros((degrees, bands, 64))
-    j = np.arange(lat_count)
-    turn = (n[:, None] * (2 * j + 1)[None, :]) % (4 * lat_count)
-    out[:, :, :rows] = (np.cos(turn * (math.pi / (2.0 * lat_count))) * math.sqrt(2.0 / lat_count)).reshape(degrees, bands, rows)
-    return split_table(out.reshape(degrees, bands * 64))
+    turn_index = (np.arange(degrees)[:, None] * (2 * np.arange(lat_count // 2) + 1)[None, :]) % (4 * lat_count)
+    values = np.cos(turn_index * (math.pi / (2.0 * lat_count))) * math.sqrt(2.0 / lat_count)
+    out = np.zeros((degrees, bands // 2, 64))
+    out[:, :, :rows] = values.reshape(degrees, bands // 2, rows)
+    out = out.reshape(degrees, -1)
+    return np.stack([split_table(out[0::2]), split_table(out[1::2])])
 
 
 class Loaded:
@@ -277,12 +278,21 @@
 PIECES = 3
 
 
+HALVES = 1
+
+
+def store_halves(value, refs):
+    cut = refs[0].shape[0]
+    for k, ref in enumerate(refs):
+        ref[...] = value[k * cut : (k + 1) * cut]
+
+
 def other_kernel(grp_ref, members_ref, count_ref, row_ref, table_ref, out_ref, sum_ref, held, held_table, sums_sem, table_sem):
     summed = level_sum(members_ref, 1 - grp_ref[0], held, sums_sem)
     table = Loaded(table_ref, held_table, table_sem, GROUPS)
     perm = to_slots(row_ref[...])
     acc = summed()
-    sum_ref[...] = acc
+    store_halves(acc, (sum_ref,))
     weights = count_ref[...].astype(F32) * 0.5
     out_ref[...] = pack(analyse(-weights * (acc / MEM), table, perm))
 
@@ -294,84 +304,97 @@
     table = Loaded(table_ref, held_table, table_sem, GROUPS)
     perm = to_slots(row_ref[...])
     acc = summed()
-    sum_ref[...] = acc
+    store_halves(acc, (sum_ref,))
     weights = count_ref[...].astype(F32) * 0.5
     obs.wait()
     out_ref[...] = analyse(weights * (held_obs[...] - acc / MEM), table, perm)
 
 
-def join_kernel(own_ref, packed_ref, sum_own_ref, sum_other_ref, out_ref, sum_own_out, sum_other_out):
+def join_kernel(own_ref, packed_ref, out_ref):
     out_ref[...] = (own_ref[...] + unpack(packed_ref[...])).reshape(out_ref.shape)
 
 
-LAT_PIECES = 3
-
-
-def load_latitude(lat_ref, held, semaphores):
-    return Loaded(lat_ref, held, semaphores, [(piece, part) for piece in range(LAT_PIECES) for part in range(2)])
-
-
-def latitude_analysis(chunks_ref, lat):
-    bands, slots, _ = chunks_ref.shape
-    cos, sin = [], []
-    for p in range(bands // 2):
-        x0, x1 = chunks_ref[2 * p], chunks_ref[2 * p + 1]
-        lower = lanes_like(x0) < 64
-        cos.append(jnp.where(lower, x0, turn(x1, 64)))
-        sin.append(jnp.where(lower, turn(x0, 64), x1))
-    x = jnp.concatenate([jnp.concatenate(cos, axis=1), jnp.concatenate(sin, axis=1)], axis=0)
-    high, low = halves(x)
-    lhs = jnp.concatenate([high, low], axis=0)
-    pieces = []
-    for piece in range(LAT_PIECES):
-        acc = dot(lhs, lat[piece, 0], NT) + dot(lhs, lat[piece, 1], NT)
-        pieces.append(acc[: 2 * slots] + acc[2 * slots :])
-    return jnp.concatenate(pieces, axis=1)
-
-
-def latitude_synthesis(vector, lat, out_ref, values):
-    bands, slots, _ = out_ref.shape
-    high, low = halves(vector)
-    lhs = jnp.concatenate([high, low], axis=0)
-    cut = vector.shape[1] // LAT_PIECES
-    acc = 0.0
-    for piece in range(LAT_PIECES):
-        part = lhs[:, piece * cut : (piece + 1) * cut]
-        acc = acc + dot(part, lat[piece, 0]) + dot(part, lat[piece, 1])
-    y = acc[: 2 * slots] + acc[2 * slots :]
-    for p in range(bands // 2):
+LAT_GROUPS = [(parity, part) for parity in range(2) for part in range(2)]
+
+
+def southern(x, rows):
+    lanes = lanes_like(x)
+    index = jnp.where(lanes < rows, rows - 1 - lanes, jnp.where((lanes >= 64) & (lanes < 64 + rows), 127 + rows - lanes, lanes))
+    return jnp.take_along_axis(x, index, axis=-1)
+
+
+def side_by_side(chunks):
+    lower = lanes_like(chunks[0]) < 64
+    pairs = [(chunks[k], chunks[k + 1]) for k in range(0, len(chunks), 2)]
+    cos = [jnp.where(lower, x0, turn(x1, 64)) for x0, x1 in pairs]
+    sin = [jnp.where(lower, turn(x0, 64), x1) for x0, x1 in pairs]
+    return jnp.concatenate([jnp.concatenate(cos, axis=1), jnp.concatenate(sin, axis=1)], axis=0)
+
+
+def apart(y):
+    slots = y.shape[0] // 2
+    out = []
+    for p in range(y.shape[1] // 128):
         y0, y1 = block(y[:slots], p), block(y[slots:], p)
         lower = lanes_like(y0) < 64
-        out_ref[2 * p] = mark(jnp.where(lower, y0, turn(y1, 64)), values)
-        out_ref[2 * p + 1] = mark(jnp.where(lower, turn(y0, 64), y1), values)
+        out += [jnp.where(lower, y0, turn(y1, 64)), jnp.where(lower, turn(y0, 64), y1)]
+    return out
+
+
+def latitude_analysis(chunks_ref, lat, rows):
+    bands, slots, _ = chunks_ref.shape
+    north = [chunks_ref[t] for t in range(bands // 2)]
+    south = [southern(chunks_ref[bands - 1 - t], rows) for t in range(bands // 2)]
+    out = []
+    for parity in range(2):
+        x = side_by_side([a + b if parity == 0 else a - b for a, b in zip(north, south)])
+        lhs = jnp.concatenate(halves(x), axis=0)
+        acc = dot(lhs, lat[parity, 0], NT) + dot(lhs, lat[parity, 1], NT)
+        out.append(acc[: 2 * slots] + acc[2 * slots :])
+    return jnp.concatenate(out, axis=1)
+
+
+def latitude_synthesis(vector, lat, out_ref, values, rows):
+    bands, slots, _ = out_ref.shape
+    half = vector.shape[1] // 2
+    y = []
+    for parity in range(2):
+        lhs = jnp.concatenate(halves(vector[:, parity * half : (parity + 1) * half]), axis=0)
+        acc = dot(lhs, lat[parity, 0]) + dot(lhs, lat[parity, 1])
+        y.append(acc[: 2 * slots] + acc[2 * slots :])
+    for t, chunk in enumerate(apart(y[0] + y[1])):
+        out_ref[t] = mark(chunk, values)
+    for t, chunk in enumerate(apart(y[0] - y[1])):
+        out_ref[bands - 1 - t] = mark(southern(chunk, rows), values)
 
 
 def scale_of(variance, waves_col, degrees):
     slots = waves_col.shape[0]
-    degree = lax.broadcasted_iota(jnp.int32, (slots, degrees), 1)
+    lane = lax.broadcasted_iota(jnp.int32, (slots, degrees), 1)
+    degree = 2 * (lane % (degrees // 2)) + lane // (degrees // 2)
     scale = jnp.where(degree >= waves_col, jnp.sqrt(variance), 0.0)
     return jnp.concatenate([scale, scale], axis=0)
 
 
 def latitude_first_kernel(chunks_ref, variance_ref, waves_ref, lat_ref, *refs):
     rhs_ref, out_ref, held, semaphores = refs[-4:]
-    lat = load_latitude(lat_ref, held, semaphores)
+    lat = Loaded(lat_ref, held, semaphores, LAT_GROUPS)
     scale = scale_of(variance_ref[...], waves_ref[...], variance_ref.shape[1])
-    rhs = latitude_analysis(chunks_ref, lat) * scale
+    rhs = latitude_analysis(chunks_ref, lat, ROWS) * scale
     rhs_ref[...] = rhs
-    latitude_synthesis(rhs * scale, lat, out_ref, [total(rhs * rhs)])
+    latitude_synthesis(rhs * scale, lat, out_ref, [total(rhs * rhs)], ROWS)
 
 
 def latitude_second_kernel(chunks_ref, variance_ref, waves_ref, rhs_ref, lat_ref, *refs):
     image_ref, out_ref, quotient_ref, held, semaphores = refs[-5:]
-    lat = load_latitude(lat_ref, held, semaphores)
+    lat = Loaded(lat_ref, held, semaphores, LAT_GROUPS)
     norm, field_norm = chunks_ref[0, 0:1, 49:50], marks(chunks_ref, 48)
     extra = jnp.where(norm > 0.0, field_norm / norm, 0.0)
     quotient_ref[...] = jnp.broadcast_to(1.0 + extra, (8, 128))
     scale = scale_of(variance_ref[...], waves_ref[...], variance_ref.shape[1])
-    image = latitude_analysis(chunks_ref, lat) * scale - extra * rhs_ref[...]
+    image = latitude_analysis(chunks_ref, lat, ROWS) * scale - extra * rhs_ref[...]
     image_ref[...] = image
-    latitude_synthesis(image * scale, lat, out_ref, [])
+    latitude_synthesis(image * scale, lat, out_ref, [], ROWS)
 
 
 def marks(band_ref, lane):
@@ -456,9 +479,11 @@
         for piece in range(PIECES):
             source = members_ref.at[:, level, pl.ds(piece * self.cut, self.cut)]
             self.loads.append(pltpu.make_async_copy(source, self.near.at[piece], near_sem.at[piece]))
-        self.sum_loads = [
-            pltpu.make_async_copy(source.at[index], self.near_sums.at[k], sums_sem.at[k]) for k, (source, index) in enumerate(sums)
-        ]
+        self.sum_loads = []
+        for k, source in enumerate(sums):
+            half = source.shape[0]
+            target = self.near_sums.at[k // HALVES, pl.ds(k % HALVES * half, half)]
+            self.sum_loads.append(pltpu.make_async_copy(source, target, sums_sem.at[k]))
         for copy in self.sum_loads + self.loads:
             copy.start()
 
@@ -480,18 +505,18 @@
             copy.wait()
 
 
-def finish_own_kernel(grp_ref, members_ref, sums_own_ref, sums_other_ref, factors_ref, start_ref, next_ref, out_ref, *scratch):
-    me = grp_ref[0]
-    work = Recentering(members_ref, me, ((sums_own_ref, me), (sums_other_ref, 1 - me)), out_ref, scratch)
+def finish_own_kernel(grp_ref, members_ref, *refs):
+    sums, (factors_ref, start_ref, next_ref, out_ref), scratch = refs[: 2 * HALVES], refs[2 * HALVES : 2 * HALVES + 4], refs[2 * HALVES + 4 :]
+    work = Recentering(members_ref, grp_ref[0], sums, out_ref, scratch)
     first, second = factors_ref[0:1, 0:1], factors_ref[0:1, 1:2]
     work.run(lambda here: first * start_ref[here] + second * next_ref[here])
 
 
-def finish_other_kernel(grp_ref, members_ref, sums_own_ref, sums_other_ref, packed_ref, row_ref, table_ref, half_ref, out_ref, *scratch):
-    held_table, table_sem, scratch = scratch[0], scratch[1], scratch[2:]
+def finish_other_kernel(grp_ref, members_ref, *refs):
+    sums, (packed_ref, row_ref, table_ref, half_ref, out_ref) = refs[: 2 * HALVES], refs[2 * HALVES : 2 * HALVES + 5]
+    held_table, table_sem, *scratch = refs[2 * HALVES + 5 :]
     table = Loaded(table_ref, held_table, table_sem, GROUPS)
-    me = grp_ref[0]
-    work = Recentering(members_ref, 1 - me, ((sums_own_ref, 1 - me), (sums_other_ref, me)), out_ref, scratch)
+    work = Recentering(members_ref, 1 - grp_ref[0], sums, out_ref, scratch)
     rows, lon = members_ref.shape[2:]
     field = synthesise(unpack(packed_ref[...]), table, to_natural(row_ref[...]), rows, lon)
     work.run(lambda here: field[here])
@@ -521,14 +546,6 @@
     return run
 
 
-def butterfly(value, axis, count):
-    step = 1
-    while step < count:
-        value = value + lax.ppermute(value, axis, [(i, i ^ step) for i in range(count)])
-        step *= 2
-    return value
-
-
 def on_device(tables, lat_table, members, obs_value, obs_count, variance, wave_order):
     grp = lax.axis_index("grp")
     bands = lax.axis_size("tile")
@@ -539,7 +556,8 @@
     degrees = variance.shape[1]
     swap = [(0, 1), (1, 0)]
     own_waves = lax.dynamic_slice_in_dim(wave_order, lax.axis_index("tile") * slots, slots, 0)[:, None]
-    own_variance = lax.dynamic_index_in_dim(variance, grp, 0, keepdims=True)
+    own_variance = lax.dynamic_index_in_dim(variance, grp, 0, keepdims=False)
+    own_variance = own_variance.reshape(degrees // 2, 2).T.reshape(1, degrees)
     row = wave_order[None, :]
     grp_scalar = grp[None].astype(jnp.int32)
 
@@ -550,32 +568,31 @@
     small = shape(8, 128)
     dma = pltpu.SemaphoreType.DMA
     zonal = [pltpu.VMEM(tables.shape, BF), dma((len(GROUPS),))]
-    latitude = [pltpu.VMEM(lat_table.shape, BF), dma((2 * LAT_PIECES,))]
+    latitude = [pltpu.VMEM(lat_table.shape, BF), dma((len(LAT_GROUPS),))]
     level = pltpu.VMEM((mem, rows, lon), BF)
     cut = rows // PIECES
+    halves_out = [shape(rows // HALVES, lon)] * HALVES
     level_scalar = (2 * lax.axis_index("lev") + grp)[None].astype(jnp.int32)
 
     def trade(array):
         return lax.ppermute(array, "grp", swap)
 
     with jax.named_scope("start"):
-        coeffs_other, sum_other = call(
-            other_kernel, [packed, field], "other", (1, 4), scalars=(0,), scratch=[level, zonal[0], dma((mem,)), zonal[1]]
+        coeffs_other, *sum_other = call(
+            other_kernel, [packed] + halves_out, "other", (1, 4), scalars=(0,), scratch=[level, zonal[0], dma((mem,)), zonal[1]]
         )(grp_scalar, members, obs_count, row, tables)
         coeffs_in = trade(coeffs_other)
-        coeffs_own, sum_own = call(
+        coeffs_own, *sum_own = call(
             own_kernel,
-            [shape(waves, 128), field],
+            [shape(waves, 128)] + halves_out,
             "own",
             (1, 2, 5),
             scalars=(0,),
             scratch=[level, zonal[0], pltpu.VMEM((rows, lon), F32), dma((mem,)), zonal[1], dma],
         )(grp_scalar, members, obs_value, obs_count, row, tables)
-        coeffs, sum_own, sum_other = call(join_kernel, [chunk, field, field], "join", (2, 3), (1, 2), aliases={2: 1, 3: 2})(
-            coeffs_own, coeffs_in, sum_own, sum_other
-        )
-        sums_own = lax.all_gather(sum_own, "grp")
-        sums_other = lax.all_gather(sum_other, "grp")
+        (coeffs,) = call(join_kernel, [chunk], "join")(coeffs_own, coeffs_in)
+        sum_own_in = [trade(piece) for piece in sum_other]
+        sum_other_in = [trade(piece) for piece in sum_own]
 
     def exchange(chunks):
         return lax.all_to_all(chunks, "tile", 0, 0, tiled=True)
@@ -585,8 +602,8 @@
             exchange(coeffs), own_variance, own_waves, lat_table
         )
         band_first = exchange(lat_values)
-        field_own, coeffs = call(grid_kernel, [field, chunk], "grid", (3,), scratch=zonal)(
-            band_first, obs_count, row, tables
+        field_own, coeffs = call(grid_kernel, [field, chunk], "grid", (3, 4), scratch=zonal)(
+            band_first, obs_count, row, tables, sum_own_in[0]
         )
         image, lat_values, quotient = call(latitude_second_kernel, [vector, chunk, small], "lat2", (4,), scratch=latitude)(
             exchange(coeffs), own_variance, own_waves, rhs, lat_table
@@ -597,7 +614,8 @@
             level_scalar, band_second, obs_count, row, tables, field_own, rhs, image, quotient
         )
         sums = jnp.sum(exchange(sums), axis=0)
-        sums = sums + sum(lax.ppermute(sums, "lev", [(i, (i + k) % levels) for i in range(levels)]) for k in range(1, levels))
+        for step in (1, 2):
+            sums = sums + lax.ppermute(sums, "lev", [(i, i ^ step) for i in range(levels)])
 
     with jax.named_scope("finish"):
         control, control_band, factors = call(combine_kernel, [vector, packed, shape(1, 128)], "combine", scalars=(0,), limit=16)(
@@ -605,14 +623,25 @@
         )
         control_band = trade(control_band)
         near = pltpu.VMEM((PIECES, mem, cut, lon), BF)
-        scratch = [near, pltpu.VMEM((2, rows, lon), F32), near, dma((PIECES,)), dma((2,)), dma((PIECES,))]
+        scratch = [near, pltpu.VMEM((2, rows, lon), F32), near, dma((PIECES,)), dma((2 * HALVES,)), dma((PIECES,))]
         whole_out = jax.ShapeDtypeStruct(members.shape, BF)
-        (half,) = call(finish_own_kernel, [whole_out], "finish_own", (1, 2, 3), (0,), scalars=(0,), scratch=scratch, limit=56)(
-            grp_scalar, members, sums_own, sums_other, factors, field_own, next_own
+        far = tuple(range(1, 2 + 2 * HALVES))
+        (half,) = call(finish_own_kernel, [whole_out], "finish_own", far, (0,), scalars=(0,), scratch=scratch, limit=56)(
+            grp_scalar, members, *sum_own, *sum_own_in, factors, field_own, next_own
         )
+        last_arg = 5 + 2 * HALVES
         (recentered,) = call(
-            finish_other_kernel, [whole_out], "finish_other", (1, 2, 3, 6, 7), (0,), scalars=(0,), aliases={7: 0}, scratch=zonal + scratch, limit=56
-        )(grp_scalar, members, sums_own, sums_other, control_band, row, tables, half)
+            finish_other_kernel,
+            [whole_out],
+            "finish_other",
+            far + (last_arg - 1, last_arg),
+            (0,),
+            scalars=(0,),
+            aliases={last_arg: 0},
+            scratch=zonal + scratch,
+            limit=56,
+        )(grp_scalar, members, *sum_other, *sum_other_in, control_band, row, tables, half)
+    control = control.reshape(2 * slots, 2, degrees // 2).swapaxes(1, 2)
     return recentered, control.reshape(1, 1, 2, slots, degrees)
 
 
@@ -621,7 +650,6 @@
     waves, degrees, rows, lon = 768, 768, 48, 3072
     tables = zonal_tables(waves, lon)
     lat_table = latitude_table(degrees, bands, rows)
-    lat_table = lat_table.reshape(2, LAT_PIECES, degrees // LAT_PIECES, -1).swapaxes(0, 1)
     placed = (
         P("grp", "lev", "tile", None),
         P("lev", "tile", None),

time: 184 us -> 173 us (0.940); the launches traced: 181 us -> 172 us
  between operations: 14.2 us -> 1.03 us
  starting transfers between devices: 34.7 us -> 43.5 us
  Pallas kernels: 52.4 us -> 46.8 us
  waiting for transfers between devices: 48.8 us -> 44.4 us
  blocking collectives: 24.8 us -> 28 us
  local copies, waits for them, and re-layouts: 6.3 us -> 8.57 us
    all_to_all x3, waiting for transfers between devices: 28.2 us -> 7.58 us  [exchange(): return lax.all_to_all(chunks, 'tile', 0, 0, tiled=True)]
    ppermute x3 -> x5, waiting for transfers between devices: 16.3 us -> 29.4 us  [trade(): return lax.ppermute(array, 'grp', swap)]
    ppermute x3 -> x5, starting transfers between devices: 16.1 us -> 26.2 us  [trade(): return lax.ppermute(array, 'grp', swap)]
    pallas_call x10, Pallas kernels: 52.4 us -> 46.8 us  [run(): pl.pallas_call(kernel, out_shape=outs, in_specs=[pl.BlockSpec(memory_spac...]
    ppermute x3 -> x2, waiting for transfers between devices: 3.54 us -> 7.43 us  [on_device(): lax.ppermute(sums, 'lev', [(i, i ^ step) for i in range(levels)])]
    all_to_all x2, blocking collectives: 24.8 us -> 28 us  [exchange(): return lax.all_to_all(chunks, 'tile', 0, 0, tiled=True)]
    unnamed x18 -> x26, local copies, waits for them, and re-layouts: 4.75 us -> 5.78 us
  transfers between devices with their start and end apart: 11 -> 10, of which waited for: 9 -> 8; matrix products, arithmetic and copies ran while one was open for 1% -> 2% of each run, Pallas kernels for 21% -> 13%
where the time goes in v3:
time: 173 us; the launch traced here: 172 us
  Pallas kernels  46.8 us (27%)
  waiting for transfers between devices  44.4 us (26%)
  starting transfers between devices  43.5 us (25%)
  blocking collectives  28 us (16%)
  local copies, waits for them, and re-layouts  8.57 us (5%)
    pallas_call x10, Pallas kernels, run(): pl.pallas_call(kernel, out_shape=outs, in_specs=[pl.BlockSpec(memory_spac...  46.8 us
    ppermute x5, waiting for transfers between devices, trade(): return lax.ppermute(array, 'grp', swap)  29.4 us
    all_to_all x2, blocking collectives, exchange(): return lax.all_to_all(chunks, 'tile', 0, 0, tiled=True)  28 us
    ppermute x5, starting transfers between devices, trade(): return lax.ppermute(array, 'grp', swap)  26.2 us
    all_to_all x3, starting transfers between devices, exchange(): return lax.all_to_all(chunks, 'tile', 0, 0, tiled=True)  15.7 us
    all_to_all x3, waiting for transfers between devices, exchange(): return lax.all_to_all(chunks, 'tile', 0, 0, tiled=True)  7.58 us
    ppermute x2, waiting for transfers between devices, on_device(): lax.ppermute(sums, 'lev', [(i, i ^ step) for i in range(levels)])  7.43 us
    unnamed x26, local copies, waits for them, and re-layouts  5.78 us
  transfers between devices with their start and end apart: 10, of which 8 were waited for; matrix products, arithmetic and copies ran while one was open for 2% of the time, Pallas kernels for 13%

profile of v3, /device:TPU:32, one launch (start us, length us, event | category | flops | bytes accessed | tf_op | source)
XLA Modules:
  0.0 172.4 jit_solution(773668001765495860)
XLA Ops:
  2.4 5.9 %other.1 = (f32[576,128]{1,0:T(8,128)S(1)}, f32[48,3072]{1,0:T(8,128)S(1)}) custom-call(s32[1]{0:T(128)} %bitcast.grp_ref, bf16[8,2,48,3072]{3,2,1,0:T(8,128)(2,1)} %members_ref.7, s32[48,3072]{1,0:T(8,128)S(1)} %copy-done.1, s32[1,768]{1,0:T(1,128)S(1)} %broadcast_in_dim.13.row_ref.refs_3_, bf16[4,2,384,896]{3,2,1,0:T(8,128)(2,1)} %constant.33.clone.table_ref.refs_4_), custom_call_target="tpu_custom_call" | custom-call | flops 1 | bytes 1 | tf_op jit(solution)/shard_map/start/other/pallas_call | solution.py:534
  8.4 6.4 %collective-permute-start.1 = (f32[576,128]{1,0:T(8,128)S(1)}, f32[576,128]{1,0:T(8,128)S(1)}, u32[]{:S(2)}, u32[]{:S(2)}) collective-permute-start(f32[576,128]{1,0:T(8,128)S(1)} %get-tuple-element.21), channel_id=1, source_target_pairs={{0,128},{128,0},{1,129},{129,1},{2,130},{130,2},{3,131},{131,3},{4... | collective-permute-start | bytes 884744 | tf_op jit(solution)/shard_map/start/ppermute | solution.py:578
  14.7 6.0 %own.1 = (f32[768,128]{1,0:T(8,128)S(1)}, f32[48,3072]{1,0:T(8,128)S(1)}) custom-call(s32[1]{0:T(128)} %bitcast.grp_ref, bf16[8,2,48,3072]{3,2,1,0:T(8,128)(2,1)} %members_ref.7, f32[2,48,3072]{2,1,0:T(8,128)} %obs_ref.1, s32[48,3072]{1,0:T(8,128)S(1)} %copy-done.1, s32[1,768]{1,0:T(1,128)S(1)} %broadcast_in_dim.13.row_ref.refs_3_, ...), custom_call_target="tpu_custom_call" | custom-call | flops 1 | bytes 1 | tf_op jit(solution)/shard_map/start/own/pallas_call | solution.py:534
  20.7 7.4 %collective-permute-done.1.packed_ref = f32[576,128]{1,0:T(8,128)S(1)} collective-permute-done((f32[576,128]{1,0:T(8,128)S(1)}, f32[576,128]{1,0:T(8,128)S(1)}, u32[]{:S(2)}, u32[]{:S(2)}) %collective-permute-start.1) | collective-permute-done | bytes 294944 | tf_op jit(solution)/shard_map/start/ppermute | solution.py:578
  29.2 7.3 %all-to-all-start = ((f32[32,24,128]{2,1,0:T(8,128)}), f32[32,24,128]{2,1,0:T(8,128)S(1)}, u32[]{:S(2)}, u32[]{:S(2)}) async-start(f32[32,24,128]{2,1,0:T(8,128)} %join.1), calls=%async_computation | async-start | bytes 786432 | tf_op jit(solution)/shard_map/solve/all_to_all | solution.py:598
  36.5 5.7 %collective-permute-start.2 = (f32[48,3072]{1,0:T(8,128)S(1)}, f32[48,3072]{1,0:T(8,128)S(1)}, u32[]{:S(2)}, u32[]{:S(2)}) collective-permute-start(f32[48,3072]{1,0:T(8,128)S(1)} %get-tuple-element.18.refs_0_), channel_id=1, source_target_pairs={{0,128},{128,0},{1,129},{129,1},{2,130},{130,2},{3,131},{131,3},{4... | collective-permute-start | bytes 1769480 | tf_op jit(solution)/shard_map/start/ppermute | solution.py:578
  46.4 4.4 %lat1.1 = (f32[48,768]{1,0:T(8,128)S(1)}, f32[32,24,128]{2,1,0:T(8,128)}) custom-call(f32[32,24,128]{2,1,0:T(8,128)S(1)} %all-to-all-done.chunks_ref, f32[1,768]{1,0:T(1,128)S(1)} %bitcast.13, s32[24,1]{1,0:T(8,128)S(1)} %copy.14.waves_ref, bf16[2,2,384,1024]{3,2,1,0:T(8,128)(2,1)} %constant.34.clone.lat_ref), custom_call_target="tpu_custom_call" | custom-call | flops 1 | bytes 1 | tf_op jit(solution)/shard_map/solve/lat1/pallas_call | solution.py:534
  50.9 4.5 %all-to-all-start.1 = ((f32[32,24,128]{2,1,0:T(8,128)}), f32[32,24,128]{2,1,0:T(8,128)S(1)}, u32[]{:S(2)}, u32[]{:S(2)}) async-start(f32[32,24,128]{2,1,0:T(8,128)} %get-tuple-element.22), calls=%async_computation.1 | async-start | bytes 786432 | tf_op jit(solution)/shard_map/solve/all_to_all | solution.py:598
  55.4 13.2 %collective-permute-done.2.refs_0_.refs_1_ = f32[48,3072]{1,0:T(8,128)S(1)} collective-permute-done((f32[48,3072]{1,0:T(8,128)S(1)}, f32[48,3072]{1,0:T(8,128)S(1)}, u32[]{:S(2)}, u32[]{:S(2)}) %collective-permute-start.2) | collective-permute-done | bytes 589856 | tf_op jit(solution)/shard_map/start/ppermute | solution.py:578
  69.4 6.3 %grid.1 = (f32[48,3072]{1,0:T(8,128)S(1)}, f32[32,24,128]{2,1,0:T(8,128)S(1)}) custom-call(f32[32,24,128]{2,1,0:T(8,128)S(1)} %all-to-all-done.1.band_ref.first_ref, s32[48,3072]{1,0:T(8,128)S(1)} %copy-done.2, s32[1,768]{1,0:T(1,128)S(1)} %broadcast_in_dim.13.row_ref.refs_3_, bf16[4,2,384,896]{3,2,1,0:T(8,128)(2,1)} %constant.33.clone.table_ref.refs_4_, ...), custom_call_target="tpu_custom_call" | custom-call | flops 1 | bytes 1 | tf_op jit(solution)/shard_map/solve/grid/pallas_call | solution.py:534
  76.6 17.0 %all_to_all.25.chunks_ref = f32[32,24,128]{2,1,0:T(8,128)S(1)} all-to-all(f32[32,24,128]{2,1,0:T(8,128)S(1)} %get-tuple-element.23), channel_id=1, replica_groups=mesh['grp'=2,'tile'=32,'lev'=4] {'tile'}, dimensions={0} | all-to-all | bytes 786432 | tf_op jit(solution)/shard_map/solve/all_to_all | solution.py:598
  93.6 4.5 %lat2.1 = (f32[48,768]{1,0:T(8,128)S(1)}, f32[32,24,128]{2,1,0:T(8,128)}, f32[8,128]{1,0:T(8,128)S(1)}) custom-call(f32[32,24,128]{2,1,0:T(8,128)S(1)} %all_to_all.25.chunks_ref, f32[1,768]{1,0:T(1,128)S(1)} %bitcast.14, s32[24,1]{1,0:T(8,128)S(1)} %copy.14.waves_ref, f32[48,768]{1,0:T(8,128)S(1)} %get-tuple-element.24.rhs_ref, ...), custom_call_target="tpu_custom_call" | custom-call | flops 1 | bytes 1 | tf_op jit(solution)/shard_map/solve/lat2/pallas_call | solution.py:534
  98.1 3.9 %all-to-all-start.3 = ((f32[32,24,128]{2,1,0:T(8,128)}), f32[32,24,128]{2,1,0:T(8,128)S(1)}, u32[]{:S(2)}, u32[]{:S(2)}) async-start(f32[32,24,128]{2,1,0:T(8,128)} %get-tuple-element.25), calls=%async_computation.3 | async-start | bytes 786432 | tf_op jit(solution)/shard_map/solve/all_to_all | solution.py:598
  102.0 5.5 %collective-permute-start = (f32[48,3072]{1,0:T(8,128)S(1)}, f32[48,3072]{1,0:T(8,128)S(1)}, u32[]{:S(2)}, u32[]{:S(2)}) collective-permute-start(f32[48,3072]{1,0:T(8,128)S(1)} %get-tuple-element.19.refs_0_), channel_id=1, source_target_pairs={{0,128},{128,0},{1,129},{129,1},{2,130},{130,2},{3,131},{131,3},{4... | collective-permute-start | bytes 1769480 | tf_op jit(solution)/shard_map/start/ppermute | solution.py:578
  107.5 4.5 %all-to-all-done.3.band_ref.second_ref = f32[32,24,128]{2,1,0:T(8,128)S(1)} async-done(((f32[32,24,128]{2,1,0:T(8,128)}), f32[32,24,128]{2,1,0:T(8,128)S(1)}, u32[]{:S(2)}, u32[]{:S(2)}) %all-to-all-start.3) | async-done | bytes 393248 | tf_op jit(solution)/shard_map/solve/all_to_all | solution.py:598
  111.9 5.8 %last.1 = (f32[48,3072]{1,0:T(8,128)S(1)}, f32[32,1,128]{2,1,0:T(1,128)S(1)}) custom-call(s32[1]{0:T(128)} %bitcast.1.level_ref, f32[32,24,128]{2,1,0:T(8,128)S(1)} %all-to-all-done.3.band_ref.second_ref, s32[48,3072]{1,0:T(8,128)S(1)} %copy-done.2, s32[1,768]{1,0:T(1,128)S(1)} %broadcast_in_dim.13.row_ref.refs_3_, ...), custom_call_target="tpu_custom_call" | custom-call | flops 1 | bytes 1 | tf_op jit(solution)/shard_map/solve/last/pallas_call | solution.py:534
  118.6 11.0 %all_to_all.26 = f32[32,1,128]{2,1,0:T(1,128)S(1)} all-to-all(f32[32,1,128]{2,1,0:T(1,128)S(1)} %get-tuple-element.29), channel_id=1, replica_groups=mesh['grp'=2,'tile'=32,'lev'=4] {'tile'}, dimensions={0} | all-to-all | bytes 32768 | tf_op jit(solution)/shard_map/solve/all_to_all | solution.py:598
  129.8 4.6 %collective-permute-done.3 = f32[1,128]{1,0:T(1,128)S(1)} collective-permute-done((f32[1,128]{1,0:T(1,128)S(1)}, f32[1,128]{1,0:T(1,128)S(1)}, u32[]{:S(2)}, u32[]{:S(2)}) %collective-permute-start.3) | collective-permute-done | bytes 544 | tf_op jit(solution)/shard_map/solve/ppermute | solution.py:618
  138.8 4.3 %collective-permute-start.5 = (f32[1,128]{1,0:T(1,128)S(1)}, f32[1,128]{1,0:T(1,128)S(1)}, u32[]{:S(2)}, u32[]{:S(2)}) collective-permute-start(f32[1,128]{1,0:T(1,128)S(1)} %add.20.sums_ref), channel_id=1, source_target_pairs={{0,128},{128,0},{1,129},{129,1},{2,130},{130,2},{3,131},{131,3},{4... | collective-permute-start | bytes 1544 | tf_op jit(solution)/shard_map/finish/ppermute | solution.py:578
  143.1 3.1 %collective-permute-done.5.sums_in_ref = f32[1,128]{1,0:T(1,128)S(1)} collective-permute-done((f32[1,128]{1,0:T(1,128)S(1)}, f32[1,128]{1,0:T(1,128)S(1)}, u32[]{:S(2)}, u32[]{:S(2)}) %collective-permute-start.5) | collective-permute-done | bytes 544 | tf_op jit(solution)/shard_map/finish/ppermute | solution.py:578
  147.4 4.3 %collective-permute-start.6 = (f32[576,128]{1,0:T(8,128)S(1)}, f32[576,128]{1,0:T(8,128)S(1)}, u32[]{:S(2)}, u32[]{:S(2)}) collective-permute-start(f32[576,128]{1,0:T(8,128)S(1)} %get-tuple-element.30), channel_id=1, source_target_pairs={{0,128},{128,0},{1,129},{129,1},{2,130},{130,2},{3,131},{131,3},{4... | collective-permute-start | bytes 884744 | tf_op jit(solution)/shard_map/finish/ppermute | solution.py:578
  151.7 4.8 %finish_own.1.refs_5_ = bf16[8,2,48,3072]{3,2,1,0:T(8,128)(2,1)} custom-call(s32[1]{0:T(128)} %bitcast.grp_ref, bf16[8,2,48,3072]{3,2,1,0:T(8,128)(2,1)} %members_ref.7, f32[48,3072]{1,0:T(8,128)} %copy-done.5, f32[48,3072]{1,0:T(8,128)} %copy-done.9, f32[1,128]{1,0:T(1,128)} %copy-done.8, f32[48,3072]{1,0:T(8,128)} %copy-done.3, f32[48,3072]{1,0:T(8,128)} %copy-done.6), custom_call_target="tpu_custom_call" | custom-call | flops 1 | bytes 1 | tf_op jit(solution)/shard_map/finish/finish_own/pallas_call | solution.py:534
  158.6 5.6 %collective-permute-done.6.refs_2_ = f32[576,128]{1,0:T(8,128)S(1)} collective-permute-done((f32[576,128]{1,0:T(8,128)S(1)}, f32[576,128]{1,0:T(8,128)S(1)}, u32[]{:S(2)}, u32[]{:S(2)}) %collective-permute-start.6) | collective-permute-done | bytes 294944 | tf_op jit(solution)/shard_map/finish/ppermute | solution.py:578
  164.8 7.4 %finish_other.1 = bf16[8,2,48,3072]{3,2,1,0:T(8,128)(2,1)} custom-call(s32[1]{0:T(128)} %bitcast.grp_ref, bf16[8,2,48,3072]{3,2,1,0:T(8,128)(2,1)} %members_ref.7, f32[48,3072]{1,0:T(8,128)} %copy-done.4, f32[48,3072]{1,0:T(8,128)} %copy-done.10, f32[576,128]{1,0:T(8,128)} %copy-done.11, s32[1,768]{1,0:T(1,128)} %copy-done.7, ...), custom_call_target="tpu_custom_call", output_to_operand_aliasing={{}: (7, {})} | custom-call | flops 1 | bytes 1 | tf_op jit(solution)/shard_map/finish/finish_other/pallas_call | solution.py:534
  (46 shorter events, 17.9 us)
Async XLA Ops:
  0.6 42.4 %copy-start = (f32[2,768]{1,0:T(2,128)S(1)}, f32[2,768]{1,0:T(2,128)}, u32[]{:S(2)}) copy-start(f32[2,768]{1,0:T(2,128)} %param.10) | copy-start | bytes 18436
  1.3 110.6 %copy-start.7 = (s32[1,768]{1,0:T(1,128)}, s32[1,768]{1,0:T(1,128)S(1)}, u32[]{:S(2)}) copy-start(s32[1,768]{1,0:T(1,128)S(1)} %broadcast_in_dim.13.row_ref.refs_3_) | copy-start | bytes 9220
  1.3 1.1 copy-start.1
  8.4 28.1 %copy-start.4 = (f32[48,3072]{1,0:T(8,128)}, f32[48,3072]{1,0:T(8,128)S(1)}, u32[]{:S(2)}) copy-start(f32[48,3072]{1,0:T(8,128)S(1)} %get-tuple-element.18.refs_0_) | copy-start | bytes 1769476
  8.4 19.8 %collective-permute-start.1 = (f32[576,128]{1,0:T(8,128)S(1)}, f32[576,128]{1,0:T(8,128)S(1)}, u32[]{:S(2)}, u32[]{:S(2)}) collective-permute-start(f32[576,128]{1,0:T(8,128)S(1)} %get-tuple-element.21), channel_id=1, source_target_pairs={{0,128},{128,0},{1,129},{129,1},{2,130},{130,2},{3,131},{131,3},{4... | collective-permute-start | bytes 884744 | tf_op jit(solution)/shard_map/start/ppermute | solution.py:578
  20.7 81.3 %copy-start.5 = (f32[48,3072]{1,0:T(8,128)}, f32[48,3072]{1,0:T(8,128)S(1)}, u32[]{:S(2)}) copy-start(f32[48,3072]{1,0:T(8,128)S(1)} %get-tuple-element.19.refs_0_) | copy-start | bytes 1769476
  20.7 48.7 %copy-start.2 = (s32[48,3072]{1,0:T(8,128)S(1)}, s32[48,3072]{1,0:T(8,128)}, u32[]{:S(2)}) copy-start(s32[48,3072]{1,0:T(8,128)} %count_ref.7) | copy-start | bytes 1769476
  29.2 17.2 %all-to-all-start = ((f32[32,24,128]{2,1,0:T(8,128)}), f32[32,24,128]{2,1,0:T(8,128)S(1)}, u32[]{:S(2)}, u32[]{:S(2)}) async-start(f32[32,24,128]{2,1,0:T(8,128)} %join.1), calls=%async_computation | async-start | bytes 786432 | tf_op jit(solution)/shard_map/solve/all_to_all | solution.py:598
  36.5 32.1 %collective-permute-start.2 = (f32[48,3072]{1,0:T(8,128)S(1)}, f32[48,3072]{1,0:T(8,128)S(1)}, u32[]{:S(2)}, u32[]{:S(2)}) collective-permute-start(f32[48,3072]{1,0:T(8,128)S(1)} %get-tuple-element.18.refs_0_), channel_id=1, source_target_pairs={{0,128},{128,0},{1,129},{129,1},{2,130},{130,2},{3,131},{131,3},{4... | collective-permute-start | bytes 1769480 | tf_op jit(solution)/shard_map/start/ppermute | solution.py:578
  50.9 17.7 %all-to-all-start.1 = ((f32[32,24,128]{2,1,0:T(8,128)}), f32[32,24,128]{2,1,0:T(8,128)S(1)}, u32[]{:S(2)}, u32[]{:S(2)}) async-start(f32[32,24,128]{2,1,0:T(8,128)} %get-tuple-element.22), calls=%async_computation.1 | async-start | bytes 786432 | tf_op jit(solution)/shard_map/solve/all_to_all | solution.py:598
  68.6 0.8 copy-start.9
  75.7 0.8 copy-start.3
  98.1 13.9 %all-to-all-start.3 = ((f32[32,24,128]{2,1,0:T(8,128)}), f32[32,24,128]{2,1,0:T(8,128)S(1)}, u32[]{:S(2)}, u32[]{:S(2)}) async-start(f32[32,24,128]{2,1,0:T(8,128)} %get-tuple-element.25), calls=%async_computation.3 | async-start | bytes 786432 | tf_op jit(solution)/shard_map/solve/all_to_all | solution.py:598
  102.0 56.6 %collective-permute-start = (f32[48,3072]{1,0:T(8,128)S(1)}, f32[48,3072]{1,0:T(8,128)S(1)}, u32[]{:S(2)}, u32[]{:S(2)}) collective-permute-start(f32[48,3072]{1,0:T(8,128)S(1)} %get-tuple-element.19.refs_0_), channel_id=1, source_target_pairs={{0,128},{128,0},{1,129},{129,1},{2,130},{130,2},{3,131},{131,3},{4... | collective-permute-start | bytes 1769480 | tf_op jit(solution)/shard_map/start/ppermute | solution.py:578
  117.8 0.8 copy-start.6
  129.7 4.7 %collective-permute-start.3 = (f32[1,128]{1,0:T(1,128)S(1)}, f32[1,128]{1,0:T(1,128)S(1)}, u32[]{:S(2)}, u32[]{:S(2)}) collective-permute-start(f32[1,128]{1,0:T(1,128)S(1)} %bitcast.18), channel_id=1, source_target_pairs={{0,1},{1,0},{2,3},{3,2},{4,5},{5,4},{6,7},{7,6},{8,9},{9,8},{10,11... | collective-permute-start | bytes 1544 | tf_op jit(solution)/shard_map/solve/ppermute | solution.py:618
  134.4 4.4 %collective-permute-start.4 = (f32[1,128]{1,0:T(1,128)S(1)}, f32[1,128]{1,0:T(1,128)S(1)}, u32[]{:S(2)}, u32[]{:S(2)}) collective-permute-start(f32[1,128]{1,0:T(1,128)S(1)} %bitcast_add_fusion), channel_id=1, source_target_pairs={{0,2},{1,3},{2,0},{3,1},{4,6},{5,7},{6,4},{7,5},{8,10},{9,11},{10,... | collective-permute-start | bytes 1544 | tf_op jit(solution)/shard_map/solve/ppermute | solution.py:618
  138.8 7.4 %collective-permute-start.5 = (f32[1,128]{1,0:T(1,128)S(1)}, f32[1,128]{1,0:T(1,128)S(1)}, u32[]{:S(2)}, u32[]{:S(2)}) collective-permute-start(f32[1,128]{1,0:T(1,128)S(1)} %add.20.sums_ref), channel_id=1, source_target_pairs={{0,128},{128,0},{1,129},{129,1},{2,130},{130,2},{3,131},{131,3},{4... | collective-permute-start | bytes 1544 | tf_op jit(solution)/shard_map/finish/ppermute | solution.py:578
  146.9 0.5 copy-start.8
  147.4 16.7 %collective-permute-start.6 = (f32[576,128]{1,0:T(8,128)S(1)}, f32[576,128]{1,0:T(8,128)S(1)}, u32[]{:S(2)}, u32[]{:S(2)}) collective-permute-start(f32[576,128]{1,0:T(8,128)S(1)} %get-tuple-element.30), channel_id=1, source_target_pairs={{0,128},{128,0},{1,129},{129,1},{2,130},{130,2},{3,131},{131,3},{4... | collective-permute-start | bytes 884744 | tf_op jit(solution)/shard_map/finish/ppermute | solution.py:578
  158.5 5.6 %copy-start.10 = (f32[48,3072]{1,0:T(8,128)}, f32[48,3072]{1,0:T(8,128)S(1)}, u32[]{:S(2)}) copy-start(f32[48,3072]{1,0:T(8,128)S(1)} %collective-permute-done.refs_1_) | copy-start | bytes 1769476
  164.1 0.7 copy-start.11

commit v4 on v3

--- a/solution.py
+++ b/solution.py
@@ -278,33 +278,25 @@
 PIECES = 3
 
 
-HALVES = 1
-
-
-def store_halves(value, refs):
-    cut = refs[0].shape[0]
-    for k, ref in enumerate(refs):
-        ref[...] = value[k * cut : (k + 1) * cut]
-
-
 def other_kernel(grp_ref, members_ref, count_ref, row_ref, table_ref, out_ref, sum_ref, held, held_table, sums_sem, table_sem):
     summed = level_sum(members_ref, 1 - grp_ref[0], held, sums_sem)
     table = Loaded(table_ref, held_table, table_sem, GROUPS)
     perm = to_slots(row_ref[...])
     acc = summed()
-    store_halves(acc, (sum_ref,))
+    sum_ref[...] = acc
     weights = count_ref[...].astype(F32) * 0.5
     out_ref[...] = pack(analyse(-weights * (acc / MEM), table, perm))
 
 
-def own_kernel(grp_ref, members_ref, obs_ref, count_ref, row_ref, table_ref, out_ref, sum_ref, held, held_table, held_obs, sums_sem, table_sem, obs_sem):
+def own_kernel(grp_ref, members_ref, obs_ref, count_ref, row_ref, table_ref, sum_other_ref, out_ref, sums_ref, held, held_table, held_obs, sums_sem, table_sem, obs_sem):
     summed = level_sum(members_ref, grp_ref[0], held, sums_sem)
     obs = pltpu.make_async_copy(obs_ref.at[grp_ref[0]], held_obs, obs_sem)
     obs.start()
     table = Loaded(table_ref, held_table, table_sem, GROUPS)
     perm = to_slots(row_ref[...])
     acc = summed()
-    store_halves(acc, (sum_ref,))
+    sums_ref[0] = sum_other_ref[...]
+    sums_ref[1] = acc
     weights = count_ref[...].astype(F32) * 0.5
     obs.wait()
     out_ref[...] = analyse(weights * (held_obs[...] - acc / MEM), table, perm)
@@ -479,11 +471,9 @@
         for piece in range(PIECES):
             source = members_ref.at[:, level, pl.ds(piece * self.cut, self.cut)]
             self.loads.append(pltpu.make_async_copy(source, self.near.at[piece], near_sem.at[piece]))
-        self.sum_loads = []
-        for k, source in enumerate(sums):
-            half = source.shape[0]
-            target = self.near_sums.at[k // HALVES, pl.ds(k % HALVES * half, half)]
-            self.sum_loads.append(pltpu.make_async_copy(source, target, sums_sem.at[k]))
+        self.sum_loads = [
+            pltpu.make_async_copy(source.at[index], self.near_sums.at[k], sums_sem.at[k]) for k, (source, index) in enumerate(sums)
+        ]
         for copy in self.sum_loads + self.loads:
             copy.start()
 
@@ -505,18 +495,15 @@
             copy.wait()
 
 
-def finish_own_kernel(grp_ref, members_ref, *refs):
-    sums, (factors_ref, start_ref, next_ref, out_ref), scratch = refs[: 2 * HALVES], refs[2 * HALVES : 2 * HALVES + 4], refs[2 * HALVES + 4 :]
-    work = Recentering(members_ref, grp_ref[0], sums, out_ref, scratch)
+def finish_own_kernel(grp_ref, members_ref, sums_ref, sums_in_ref, factors_ref, start_ref, next_ref, out_ref, *scratch):
+    work = Recentering(members_ref, grp_ref[0], ((sums_ref, 1), (sums_in_ref, 0)), out_ref, scratch)
     first, second = factors_ref[0:1, 0:1], factors_ref[0:1, 1:2]
     work.run(lambda here: first * start_ref[here] + second * next_ref[here])
 
 
-def finish_other_kernel(grp_ref, members_ref, *refs):
-    sums, (packed_ref, row_ref, table_ref, half_ref, out_ref) = refs[: 2 * HALVES], refs[2 * HALVES : 2 * HALVES + 5]
-    held_table, table_sem, *scratch = refs[2 * HALVES + 5 :]
+def finish_other_kernel(grp_ref, members_ref, sums_ref, sums_in_ref, packed_ref, row_ref, table_ref, half_ref, out_ref, held_table, table_sem, *scratch):
     table = Loaded(table_ref, held_table, table_sem, GROUPS)
-    work = Recentering(members_ref, 1 - grp_ref[0], sums, out_ref, scratch)
+    work = Recentering(members_ref, 1 - grp_ref[0], ((sums_ref, 0), (sums_in_ref, 1)), out_ref, scratch)
     rows, lon = members_ref.shape[2:]
     field = synthesise(unpack(packed_ref[...]), table, to_natural(row_ref[...]), rows, lon)
     work.run(lambda here: field[here])
@@ -571,28 +558,26 @@
     latitude = [pltpu.VMEM(lat_table.shape, BF), dma((len(LAT_GROUPS),))]
     level = pltpu.VMEM((mem, rows, lon), BF)
     cut = rows // PIECES
-    halves_out = [shape(rows // HALVES, lon)] * HALVES
     level_scalar = (2 * lax.axis_index("lev") + grp)[None].astype(jnp.int32)
 
     def trade(array):
         return lax.ppermute(array, "grp", swap)
 
     with jax.named_scope("start"):
-        coeffs_other, *sum_other = call(
-            other_kernel, [packed] + halves_out, "other", (1, 4), scalars=(0,), scratch=[level, zonal[0], dma((mem,)), zonal[1]]
+        coeffs_other, sum_other = call(
+            other_kernel, [packed, field], "other", (1, 4), scalars=(0,), scratch=[level, zonal[0], dma((mem,)), zonal[1]]
         )(grp_scalar, members, obs_count, row, tables)
         coeffs_in = trade(coeffs_other)
-        coeffs_own, *sum_own = call(
+        coeffs_own, sums = call(
             own_kernel,
-            [shape(waves, 128)] + halves_out,
+            [shape(waves, 128), shape(2, rows, lon)],
             "own",
             (1, 2, 5),
             scalars=(0,),
             scratch=[level, zonal[0], pltpu.VMEM((rows, lon), F32), dma((mem,)), zonal[1], dma],
-        )(grp_scalar, members, obs_value, obs_count, row, tables)
+        )(grp_scalar, members, obs_value, obs_count, row, tables, sum_other)
         (coeffs,) = call(join_kernel, [chunk], "join")(coeffs_own, coeffs_in)
-        sum_own_in = [trade(piece) for piece in sum_other]
-        sum_other_in = [trade(piece) for piece in sum_own]
+        sums_in = trade(sums)
 
     def exchange(chunks):
         return lax.all_to_all(chunks, "tile", 0, 0, tiled=True)
@@ -602,45 +587,35 @@
             exchange(coeffs), own_variance, own_waves, lat_table
         )
         band_first = exchange(lat_values)
-        field_own, coeffs = call(grid_kernel, [field, chunk], "grid", (3, 4), scratch=zonal)(
-            band_first, obs_count, row, tables, sum_own_in[0]
+        field_own, coeffs = call(grid_kernel, [field, chunk], "grid", (3,), scratch=zonal)(
+            band_first, obs_count, row, tables
         )
-        image, lat_values, quotient = call(latitude_second_kernel, [vector, chunk, small], "lat2", (4,), scratch=latitude)(
-            exchange(coeffs), own_variance, own_waves, rhs, lat_table
+        image, lat_values, quotient = call(latitude_second_kernel, [vector, chunk, small], "lat2", (4, 5), scratch=latitude)(
+            exchange(coeffs), own_variance, own_waves, rhs, lat_table, sums_in
         )
         band_second = exchange(lat_values)
         sum_row = jax.ShapeDtypeStruct((bands, 1, 128), F32)
-        next_own, sums = call(last_kernel, [field, sum_row], "last", (4,), scalars=(0,), scratch=zonal)(
+        next_own, scalars = call(last_kernel, [field, sum_row], "last", (4,), scalars=(0,), scratch=zonal)(
             level_scalar, band_second, obs_count, row, tables, field_own, rhs, image, quotient
         )
-        sums = jnp.sum(exchange(sums), axis=0)
+        scalars = jnp.sum(exchange(scalars), axis=0)
         for step in (1, 2):
-            sums = sums + lax.ppermute(sums, "lev", [(i, i ^ step) for i in range(levels)])
+            scalars = scalars + lax.ppermute(scalars, "lev", [(i, i ^ step) for i in range(levels)])
 
     with jax.named_scope("finish"):
         control, control_band, factors = call(combine_kernel, [vector, packed, shape(1, 128)], "combine", scalars=(0,), limit=16)(
-            level_scalar, sums, trade(sums), rhs, image, band_first, band_second
+            level_scalar, scalars, trade(scalars), rhs, image, band_first, band_second
         )
         control_band = trade(control_band)
         near = pltpu.VMEM((PIECES, mem, cut, lon), BF)
-        scratch = [near, pltpu.VMEM((2, rows, lon), F32), near, dma((PIECES,)), dma((2 * HALVES,)), dma((PIECES,))]
+        scratch = [near, pltpu.VMEM((2, rows, lon), F32), near, dma((PIECES,)), dma((2,)), dma((PIECES,))]
         whole_out = jax.ShapeDtypeStruct(members.shape, BF)
-        far = tuple(range(1, 2 + 2 * HALVES))
-        (half,) = call(finish_own_kernel, [whole_out], "finish_own", far, (0,), scalars=(0,), scratch=scratch, limit=56)(
-            grp_scalar, members, *sum_own, *sum_own_in, factors, field_own, next_own
+        (half,) = call(finish_own_kernel, [whole_out], "finish_own", (1, 2, 3), (0,), scalars=(0,), scratch=scratch)(
+            grp_scalar, members, sums, sums_in, factors, field_own, next_own
         )
-        last_arg = 5 + 2 * HALVES
         (recentered,) = call(
-            finish_other_kernel,
-            [whole_out],
-            "finish_other",
-            far + (last_arg - 1, last_arg),
-            (0,),
-            scalars=(0,),
-            aliases={last_arg: 0},
-            scratch=zonal + scratch,
-            limit=56,
-        )(grp_scalar, members, *sum_other, *sum_other_in, control_band, row, tables, half)
+            finish_other_kernel, [whole_out], "finish_other", (1, 2, 3, 6, 7), (0,), scalars=(0,), aliases={7: 0}, scratch=zonal + scratch
+        )(grp_scalar, members, sums, sums_in, control_band, row, tables, half)
     control = control.reshape(2 * slots, 2, degrees // 2).swapaxes(1, 2)
     return recentered, control.reshape(1, 1, 2, slots, degrees)
 

time: 173 us -> 164 us (0.948)
  starting transfers between devices: 43.5 us -> 33.9 us
  waiting for transfers between devices: 44.4 us -> 53.3 us
  blocking collectives: 28 us -> 24.7 us
  local copies, waits for them, and re-layouts: 8.57 us -> 5.7 us
  Pallas kernels: 46.8 us -> 44.4 us
    all_to_all x3, waiting for transfers between devices: 7.58 us -> 28.7 us  [exchange(): return lax.all_to_all(chunks, 'tile', 0, 0, tiled=True)]
    ppermute x5 -> x4, waiting for transfers between devices: 29.4 us -> 16.7 us  [trade(): return lax.ppermute(array, 'grp', swap)]
    ppermute x5 -> x4, starting transfers between devices: 26.2 us -> 18.5 us  [trade(): return lax.ppermute(array, 'grp', swap)]
    all_to_all x2, blocking collectives: 28 us -> 24.7 us  [exchange(): return lax.all_to_all(chunks, 'tile', 0, 0, tiled=True)]
    unnamed x26 -> x14, local copies, waits for them, and re-layouts: 5.78 us -> 2.9 us
    pallas_call x10, Pallas kernels: 46.8 us -> 44.4 us  [run(): pl.pallas_call(kernel, out_shape=outs, in_specs=[pl.BlockSpec(memory_spac...]
  transfers between devices with their start and end apart: 10 -> 9, of which waited for: 8 -> 8; matrix products, arithmetic and copies ran while one was open for 2% -> 2% of each run, Pallas kernels for 13% -> 13%
where the time goes in v4:
time: 164 us; the launch traced here: 163 us
  waiting for transfers between devices  53.3 us (32%)
  Pallas kernels  44.4 us (27%)
  starting transfers between devices  33.9 us (21%)
  blocking collectives  24.7 us (15%)
  local copies, waits for them, and re-layouts  5.7 us (3%)
    pallas_call x10, Pallas kernels, run(): pl.pallas_call(kernel, out_shape=outs, in_specs=[pl.BlockSpec(memory_spac...  44.4 us
    all_to_all x3, waiting for transfers between devices, exchange(): return lax.all_to_all(chunks, 'tile', 0, 0, tiled=True)  28.7 us
    all_to_all x2, blocking collectives, exchange(): return lax.all_to_all(chunks, 'tile', 0, 0, tiled=True)  24.7 us
    ppermute x4, starting transfers between devices, trade(): return lax.ppermute(array, 'grp', swap)  18.5 us
    ppermute x4, waiting for transfers between devices, trade(): return lax.ppermute(array, 'grp', swap)  16.7 us
    all_to_all x3, starting transfers between devices, exchange(): return lax.all_to_all(chunks, 'tile', 0, 0, tiled=True)  15.2 us
    ppermute x2, waiting for transfers between devices, on_device(): lax.ppermute(scalars, 'lev', [(i, i ^ step) for i in range(levels)])  7.96 us
  transfers between devices with their start and end apart: 9, of which 8 were waited for; matrix products, arithmetic and copies ran while one was open for 2% of the time, Pallas kernels for 13%

profile of v4, /device:TPU:32, one launch (start us, length us, event | category | flops | bytes accessed | tf_op | source)
XLA Modules:
  0.0 163.1 jit_solution(8096327294475701801)
XLA Ops:
  2.4 5.9 %other.1 = (f32[576,128]{1,0:T(8,128)S(1)}, f32[48,3072]{1,0:T(8,128)S(1)}) custom-call(s32[1]{0:T(128)} %bitcast.grp_ref, bf16[8,2,48,3072]{3,2,1,0:T(8,128)(2,1)} %members_ref.7, s32[48,3072]{1,0:T(8,128)S(1)} %copy-done.1, s32[1,768]{1,0:T(1,128)S(1)} %broadcast_in_dim.13.row_ref, bf16[4,2,384,896]{3,2,1,0:T(8,128)(2,1)} %constant.33.clone.table_ref), custom_call_target="tpu_custom_call" | custom-call | flops 1 | bytes 1 | tf_op jit(solution)/shard_map/start/other/pallas_call | solution.py:521
  8.4 6.4 %collective-permute-start.1 = (f32[576,128]{1,0:T(8,128)S(1)}, f32[576,128]{1,0:T(8,128)S(1)}, u32[]{:S(2)}, u32[]{:S(2)}) collective-permute-start(f32[576,128]{1,0:T(8,128)S(1)} %get-tuple-element.21), channel_id=1, source_target_pairs={{0,128},{128,0},{1,129},{129,1},{2,130},{130,2},{3,131},{131,3},{4... | collective-permute-start | bytes 884744 | tf_op jit(solution)/shard_map/start/ppermute | solution.py:564
  14.7 6.0 %own.1 = (f32[768,128]{1,0:T(8,128)S(1)}, f32[2,48,3072]{2,1,0:T(8,128)}) custom-call(s32[1]{0:T(128)} %bitcast.grp_ref, bf16[8,2,48,3072]{3,2,1,0:T(8,128)(2,1)} %members_ref.7, f32[2,48,3072]{2,1,0:T(8,128)} %obs_ref.1, s32[48,3072]{1,0:T(8,128)S(1)} %copy-done.1, s32[1,768]{1,0:T(1,128)S(1)} %broadcast_in_dim.13.row_ref, ...), custom_call_target="tpu_custom_call" | custom-call | flops 1 | bytes 1 | tf_op jit(solution)/shard_map/start/own/pallas_call | solution.py:521
  20.8 11.1 %collective-permute-done.1.packed_ref = f32[576,128]{1,0:T(8,128)S(1)} collective-permute-done((f32[576,128]{1,0:T(8,128)S(1)}, f32[576,128]{1,0:T(8,128)S(1)}, u32[]{:S(2)}, u32[]{:S(2)}) %collective-permute-start.1) | collective-permute-done | bytes 294944 | tf_op jit(solution)/shard_map/start/ppermute | solution.py:564
  33.0 7.3 %all-to-all-start = ((f32[32,24,128]{2,1,0:T(8,128)}), f32[32,24,128]{2,1,0:T(8,128)S(1)}, u32[]{:S(2)}, u32[]{:S(2)}) async-start(f32[32,24,128]{2,1,0:T(8,128)} %join.1), calls=%async_computation | async-start | bytes 786432 | tf_op jit(solution)/shard_map/solve/all_to_all | solution.py:583
  41.5 8.8 %all-to-all-done.chunks_ref = f32[32,24,128]{2,1,0:T(8,128)S(1)} async-done(((f32[32,24,128]{2,1,0:T(8,128)}), f32[32,24,128]{2,1,0:T(8,128)S(1)}, u32[]{:S(2)}, u32[]{:S(2)}) %all-to-all-start) | async-done | bytes 393248 | tf_op jit(solution)/shard_map/solve/all_to_all | solution.py:583
  50.3 3.7 %lat1.1 = (f32[48,768]{1,0:T(8,128)S(1)}, f32[32,24,128]{2,1,0:T(8,128)S(1)}) custom-call(f32[32,24,128]{2,1,0:T(8,128)S(1)} %all-to-all-done.chunks_ref, f32[1,768]{1,0:T(1,128)S(1)} %bitcast.13, s32[24,1]{1,0:T(8,128)S(1)} %copy.14.waves_ref, bf16[2,2,384,1024]{3,2,1,0:T(8,128)(2,1)} %constant.34.clone.lat_ref), custom_call_target="tpu_custom_call" | custom-call | flops 1 | bytes 1 | tf_op jit(solution)/shard_map/solve/lat1/pallas_call | solution.py:521
  54.0 13.6 %all_to_all.25.band_ref.first_ref = f32[32,24,128]{2,1,0:T(8,128)S(1)} all-to-all(f32[32,24,128]{2,1,0:T(8,128)S(1)} %get-tuple-element.22), channel_id=1, replica_groups=mesh['grp'=2,'tile'=32,'lev'=4] {'tile'}, dimensions={0} | all-to-all | bytes 786432 | tf_op jit(solution)/shard_map/solve/all_to_all | solution.py:583
  67.6 7.1 %grid.1 = (f32[48,3072]{1,0:T(8,128)S(1)}, f32[32,24,128]{2,1,0:T(8,128)}) custom-call(f32[32,24,128]{2,1,0:T(8,128)S(1)} %all_to_all.25.band_ref.first_ref, s32[48,3072]{1,0:T(8,128)S(1)} %copy-done.2, s32[1,768]{1,0:T(1,128)S(1)} %broadcast_in_dim.13.row_ref, bf16[4,2,384,896]{3,2,1,0:T(8,128)(2,1)} %constant.33.clone.table_ref), custom_call_target="tpu_custom_call" | custom-call | flops 1 | bytes 1 | tf_op jit(solution)/shard_map/solve/grid/pallas_call | solution.py:521
  75.5 3.9 %all-to-all-start.2 = ((f32[32,24,128]{2,1,0:T(8,128)}), f32[32,24,128]{2,1,0:T(8,128)S(1)}, u32[]{:S(2)}, u32[]{:S(2)}) async-start(f32[32,24,128]{2,1,0:T(8,128)} %get-tuple-element.23), calls=%async_computation.2 | async-start | bytes 786432 | tf_op jit(solution)/shard_map/solve/all_to_all | solution.py:583
  79.4 9.9 %all-to-all-done.2.chunks_ref = f32[32,24,128]{2,1,0:T(8,128)S(1)} async-done(((f32[32,24,128]{2,1,0:T(8,128)}), f32[32,24,128]{2,1,0:T(8,128)S(1)}, u32[]{:S(2)}, u32[]{:S(2)}) %all-to-all-start.2) | async-done | bytes 393248 | tf_op jit(solution)/shard_map/solve/all_to_all | solution.py:583
  89.4 4.5 %lat2.1 = (f32[48,768]{1,0:T(8,128)S(1)}, f32[32,24,128]{2,1,0:T(8,128)}, f32[8,128]{1,0:T(8,128)S(1)}) custom-call(f32[32,24,128]{2,1,0:T(8,128)S(1)} %all-to-all-done.2.chunks_ref, f32[1,768]{1,0:T(1,128)S(1)} %bitcast.14, s32[24,1]{1,0:T(8,128)S(1)} %copy.14.waves_ref, f32[48,768]{1,0:T(8,128)S(1)} %get-tuple-element.24.rhs_ref, ...), custom_call_target="tpu_custom_call" | custom-call | flops 1 | bytes 1 | tf_op jit(solution)/shard_map/solve/lat2/pallas_call | solution.py:521
  93.9 4.0 %all-to-all-start.3 = ((f32[32,24,128]{2,1,0:T(8,128)}), f32[32,24,128]{2,1,0:T(8,128)S(1)}, u32[]{:S(2)}, u32[]{:S(2)}) async-start(f32[32,24,128]{2,1,0:T(8,128)} %get-tuple-element.25), calls=%async_computation.3 | async-start | bytes 786432 | tf_op jit(solution)/shard_map/solve/all_to_all | solution.py:583
  97.9 9.9 %all-to-all-done.3.band_ref.second_ref = f32[32,24,128]{2,1,0:T(8,128)S(1)} async-done(((f32[32,24,128]{2,1,0:T(8,128)}), f32[32,24,128]{2,1,0:T(8,128)S(1)}, u32[]{:S(2)}, u32[]{:S(2)}) %all-to-all-start.3) | async-done | bytes 393248 | tf_op jit(solution)/shard_map/solve/all_to_all | solution.py:583
  107.9 5.8 %last.1 = (f32[48,3072]{1,0:T(8,128)S(1)}, f32[32,1,128]{2,1,0:T(1,128)S(1)}) custom-call(s32[1]{0:T(128)} %bitcast.1.level_ref, f32[32,24,128]{2,1,0:T(8,128)S(1)} %all-to-all-done.3.band_ref.second_ref, s32[48,3072]{1,0:T(8,128)S(1)} %copy-done.2, s32[1,768]{1,0:T(1,128)S(1)} %broadcast_in_dim.13.row_ref, ...), custom_call_target="tpu_custom_call" | custom-call | flops 1 | bytes 1 | tf_op jit(solution)/shard_map/solve/last/pallas_call | solution.py:521
  113.7 11.1 %all_to_all.26 = f32[32,1,128]{2,1,0:T(1,128)S(1)} all-to-all(f32[32,1,128]{2,1,0:T(1,128)S(1)} %get-tuple-element.29), channel_id=1, replica_groups=mesh['grp'=2,'tile'=32,'lev'=4] {'tile'}, dimensions={0} | all-to-all | bytes 32768 | tf_op jit(solution)/shard_map/solve/all_to_all | solution.py:583
  124.9 3.5 %collective-permute-done.2 = f32[1,128]{1,0:T(1,128)S(1)} collective-permute-done((f32[1,128]{1,0:T(1,128)S(1)}, f32[1,128]{1,0:T(1,128)S(1)}, u32[]{:S(2)}, u32[]{:S(2)}) %collective-permute-start.2) | collective-permute-done | bytes 544 | tf_op jit(solution)/shard_map/solve/ppermute | solution.py:603
  128.4 4.4 %collective-permute-done.3 = f32[1,128]{1,0:T(1,128)S(1)} collective-permute-done((f32[1,128]{1,0:T(1,128)S(1)}, f32[1,128]{1,0:T(1,128)S(1)}, u32[]{:S(2)}, u32[]{:S(2)}) %collective-permute-start.3) | collective-permute-done | bytes 544 | tf_op jit(solution)/shard_map/solve/ppermute | solution.py:603
  132.9 6.0 %collective-permute-start.4 = (f32[1,128]{1,0:T(1,128)S(1)}, f32[1,128]{1,0:T(1,128)S(1)}, u32[]{:S(2)}, u32[]{:S(2)}) collective-permute-start(f32[1,128]{1,0:T(1,128)S(1)} %add.20.sums_ref), channel_id=1, source_target_pairs={{0,128},{128,0},{1,129},{129,1},{2,130},{130,2},{3,131},{131,3},{4... | collective-permute-start | bytes 1544 | tf_op jit(solution)/shard_map/finish/ppermute | solution.py:564
  138.9 1.5 collective-permute-done.4.sums_in_ref
  141.0 6.0 %collective-permute-start.5 = (f32[576,128]{1,0:T(8,128)S(1)}, f32[576,128]{1,0:T(8,128)S(1)}, u32[]{:S(2)}, u32[]{:S(2)}) collective-permute-start(f32[576,128]{1,0:T(8,128)S(1)} %get-tuple-element.30), channel_id=1, source_target_pairs={{0,128},{128,0},{1,129},{129,1},{2,130},{130,2},{3,131},{131,3},{4... | collective-permute-start | bytes 884744 | tf_op jit(solution)/shard_map/finish/ppermute | solution.py:564
  147.0 3.7 %finish_own.1.half_ref = bf16[8,2,48,3072]{3,2,1,0:T(8,128)(2,1)} custom-call(s32[1]{0:T(128)} %bitcast.grp_ref, bf16[8,2,48,3072]{3,2,1,0:T(8,128)(2,1)} %members_ref.7, f32[2,48,3072]{2,1,0:T(8,128)} %get-tuple-element.19.sums_ref, f32[2,48,3072]{2,1,0:T(8,128)} %collective-permute-done.refs_0_.sums_in_ref, f32[1,128]{1,0:T(1,128)S(1)} %get-tuple-element.31.factors_ref, ...), custom_call_target="tpu_custom_call" | custom-call | flops 1 | bytes 1 | tf_op jit(solution)/shard_map/finish/finish_own/pallas_call | solution.py:521
  152.7 4.0 %collective-permute-done.5.packed_ref = f32[576,128]{1,0:T(8,128)S(1)} collective-permute-done((f32[576,128]{1,0:T(8,128)S(1)}, f32[576,128]{1,0:T(8,128)S(1)}, u32[]{:S(2)}, u32[]{:S(2)}) %collective-permute-start.5) | collective-permute-done | bytes 294944 | tf_op jit(solution)/shard_map/finish/ppermute | solution.py:564
  156.8 6.1 %finish_other.1 = bf16[8,2,48,3072]{3,2,1,0:T(8,128)(2,1)} custom-call(s32[1]{0:T(128)} %bitcast.grp_ref, bf16[8,2,48,3072]{3,2,1,0:T(8,128)(2,1)} %members_ref.7, f32[2,48,3072]{2,1,0:T(8,128)S(1)} %copy-done.3, f32[2,48,3072]{2,1,0:T(8,128)} %collective-permute-done.refs_0_.sums_in_ref, ...), custom_call_target="tpu_custom_call", output_to_operand_aliasing={{}: (7, {})} | custom-call | flops 1 | bytes 1 | tf_op jit(solution)/shard_map/finish/finish_other/pallas_call | solution.py:521
  (32 shorter events, 7.6 us)
Async XLA Ops:
  0.6 40.6 %copy-start = (f32[2,768]{1,0:T(2,128)S(1)}, f32[2,768]{1,0:T(2,128)}, u32[]{:S(2)}) copy-start(f32[2,768]{1,0:T(2,128)} %param.10) | copy-start | bytes 18436
  1.3 1.1 copy-start.1
  8.4 23.6 %collective-permute-start.1 = (f32[576,128]{1,0:T(8,128)S(1)}, f32[576,128]{1,0:T(8,128)S(1)}, u32[]{:S(2)}, u32[]{:S(2)}) collective-permute-start(f32[576,128]{1,0:T(8,128)S(1)} %get-tuple-element.21), channel_id=1, source_target_pairs={{0,128},{128,0},{1,129},{129,1},{2,130},{130,2},{3,131},{131,3},{4... | collective-permute-start | bytes 884744 | tf_op jit(solution)/shard_map/start/ppermute | solution.py:564
  20.7 46.9 %copy-start.2 = (s32[48,3072]{1,0:T(8,128)S(1)}, s32[48,3072]{1,0:T(8,128)}, u32[]{:S(2)}) copy-start(s32[48,3072]{1,0:T(8,128)} %count_ref.7) | copy-start | bytes 1769476
  20.7 58.7 %collective-permute-start = (f32[2,48,3072]{2,1,0:T(8,128)}, f32[2,48,3072]{2,1,0:T(8,128)}, u32[]{:S(2)}, u32[]{:S(2)}) collective-permute-start(f32[2,48,3072]{2,1,0:T(8,128)} %get-tuple-element.19.sums_ref), channel_id=1, source_target_pairs={{0,128},{128,0},{1,129},{129,1},{2,130},{130,2},{3,131},{131,3},{4... | collective-permute-start | bytes 3538952 | tf_op jit(solution)/shard_map/start/ppermute | solution.py:564
  33.0 17.3 %all-to-all-start = ((f32[32,24,128]{2,1,0:T(8,128)}), f32[32,24,128]{2,1,0:T(8,128)S(1)}, u32[]{:S(2)}, u32[]{:S(2)}) async-start(f32[32,24,128]{2,1,0:T(8,128)} %join.1), calls=%async_computation | async-start | bytes 786432 | tf_op jit(solution)/shard_map/solve/all_to_all | solution.py:583
  74.7 0.8 copy-start.4
  75.5 13.8 %all-to-all-start.2 = ((f32[32,24,128]{2,1,0:T(8,128)}), f32[32,24,128]{2,1,0:T(8,128)S(1)}, u32[]{:S(2)}, u32[]{:S(2)}) async-start(f32[32,24,128]{2,1,0:T(8,128)} %get-tuple-element.23), calls=%async_computation.2 | async-start | bytes 786432 | tf_op jit(solution)/shard_map/solve/all_to_all | solution.py:583
  93.9 53.2 %copy-start.5 = (f32[48,3072]{1,0:T(8,128)S(1)}, f32[48,3072]{1,0:T(8,128)}, u32[]{:S(2)}) copy-start(f32[48,3072]{1,0:T(8,128)} %copy-done.4) | copy-start | bytes 1769476
  93.9 14.0 %all-to-all-start.3 = ((f32[32,24,128]{2,1,0:T(8,128)}), f32[32,24,128]{2,1,0:T(8,128)S(1)}, u32[]{:S(2)}, u32[]{:S(2)}) async-start(f32[32,24,128]{2,1,0:T(8,128)} %get-tuple-element.25), calls=%async_computation.3 | async-start | bytes 786432 | tf_op jit(solution)/shard_map/solve/all_to_all | solution.py:583
  124.8 3.6 %collective-permute-start.2 = (f32[1,128]{1,0:T(1,128)S(1)}, f32[1,128]{1,0:T(1,128)S(1)}, u32[]{:S(2)}, u32[]{:S(2)}) collective-permute-start(f32[1,128]{1,0:T(1,128)S(1)} %bitcast.18), channel_id=1, source_target_pairs={{0,1},{1,0},{2,3},{3,2},{4,5},{5,4},{6,7},{7,6},{8,9},{9,8},{10,11... | collective-permute-start | bytes 1544 | tf_op jit(solution)/shard_map/solve/ppermute | solution.py:603
  128.4 4.4 %collective-permute-start.3 = (f32[1,128]{1,0:T(1,128)S(1)}, f32[1,128]{1,0:T(1,128)S(1)}, u32[]{:S(2)}, u32[]{:S(2)}) collective-permute-start(f32[1,128]{1,0:T(1,128)S(1)} %bitcast_add_fusion), channel_id=1, source_target_pairs={{0,2},{1,3},{2,0},{3,1},{4,6},{5,7},{6,4},{7,5},{8,10},{9,11},{10,... | collective-permute-start | bytes 1544 | tf_op jit(solution)/shard_map/solve/ppermute | solution.py:603
  132.9 7.5 %collective-permute-start.4 = (f32[1,128]{1,0:T(1,128)S(1)}, f32[1,128]{1,0:T(1,128)S(1)}, u32[]{:S(2)}, u32[]{:S(2)}) collective-permute-start(f32[1,128]{1,0:T(1,128)S(1)} %add.20.sums_ref), channel_id=1, source_target_pairs={{0,128},{128,0},{1,129},{129,1},{2,130},{130,2},{3,131},{131,3},{4... | collective-permute-start | bytes 1544 | tf_op jit(solution)/shard_map/finish/ppermute | solution.py:564
  141.0 15.7 %collective-permute-start.5 = (f32[576,128]{1,0:T(8,128)S(1)}, f32[576,128]{1,0:T(8,128)S(1)}, u32[]{:S(2)}, u32[]{:S(2)}) collective-permute-start(f32[576,128]{1,0:T(8,128)S(1)} %get-tuple-element.30), channel_id=1, source_target_pairs={{0,128},{128,0},{1,129},{129,1},{2,130},{130,2},{3,131},{131,3},{4... | collective-permute-start | bytes 884744 | tf_op jit(solution)/shard_map/finish/ppermute | solution.py:564
  147.0 9.7 %copy-start.3 = (f32[2,48,3072]{2,1,0:T(8,128)S(1)}, f32[2,48,3072]{2,1,0:T(8,128)}, u32[]{:S(2)}) copy-start(f32[2,48,3072]{2,1,0:T(8,128)} %get-tuple-element.19.sums_ref) | copy-start | bytes 3538948

commit v5 on v4

--- a/solution.py
+++ b/solution.py
@@ -278,13 +278,16 @@
 PIECES = 3
 
 
-def other_kernel(grp_ref, members_ref, count_ref, row_ref, table_ref, out_ref, sum_ref, held, held_table, sums_sem, table_sem):
+def other_kernel(grp_ref, members_ref, count_ref, order_ref, table_ref, out_ref, sum_ref, held, held_table, held_count, sums_sem, table_sem, count_sem):
     summed = level_sum(members_ref, 1 - grp_ref[0], held, sums_sem)
+    count = pltpu.make_async_copy(count_ref, held_count, count_sem)
+    count.start()
     table = Loaded(table_ref, held_table, table_sem, GROUPS)
-    perm = to_slots(row_ref[...])
+    perm = to_slots(order_ref[...].reshape(1, order_ref.shape[0]))
     acc = summed()
     sum_ref[...] = acc
-    weights = count_ref[...].astype(F32) * 0.5
+    count.wait()
+    weights = held_count[...].astype(F32) * 0.5
     out_ref[...] = pack(analyse(-weights * (acc / MEM), table, perm))
 
 
@@ -502,7 +505,7 @@
 
 
 def finish_other_kernel(grp_ref, members_ref, sums_ref, sums_in_ref, packed_ref, row_ref, table_ref, half_ref, out_ref, held_table, table_sem, *scratch):
-    table = Loaded(table_ref, held_table, table_sem, GROUPS)
+    table = Loaded(table_ref, held_table, table_sem, GROUPS, ahead=len(GROUPS))
     work = Recentering(members_ref, 1 - grp_ref[0], ((sums_ref, 0), (sums_in_ref, 1)), out_ref, scratch)
     rows, lon = members_ref.shape[2:]
     field = synthesise(unpack(packed_ref[...]), table, to_natural(row_ref[...]), rows, lon)
@@ -565,8 +568,8 @@
 
     with jax.named_scope("start"):
         coeffs_other, sum_other = call(
-            other_kernel, [packed, field], "other", (1, 4), scalars=(0,), scratch=[level, zonal[0], dma((mem,)), zonal[1]]
-        )(grp_scalar, members, obs_count, row, tables)
+            other_kernel, [packed, field], "other", (1, 2, 4), scalars=(0,), scratch=[level, zonal[0], pltpu.VMEM((rows, lon), jnp.int32), dma((mem,)), zonal[1], dma]
+        )(grp_scalar, members, obs_count, wave_order, tables)
         coeffs_in = trade(coeffs_other)
         coeffs_own, sums = call(
             own_kernel,

time: 164 us -> 163 us (level)
    unnamed x14 -> x16, local copies, waits for them, and re-layouts: 2.9 us -> 3.58 us
where the time goes in v5:
time: 163 us; the launch traced here: 162 us
  waiting for transfers between devices  53.3 us (33%)
  Pallas kernels  43.4 us (27%)
  starting transfers between devices  33.8 us (21%)
  blocking collectives  24.7 us (15%)
  local copies, waits for them, and re-layouts  5.69 us (3%)
    pallas_call x10, Pallas kernels, run(): pl.pallas_call(kernel, out_shape=outs, in_specs=[pl.BlockSpec(memory_spac...  43.4 us
    all_to_all x3, waiting for transfers between devices, exchange(): return lax.all_to_all(chunks, 'tile', 0, 0, tiled=True)  28.7 us
    all_to_all x2, blocking collectives, exchange(): return lax.all_to_all(chunks, 'tile', 0, 0, tiled=True)  24.7 us
    ppermute x4, starting transfers between devices, trade(): return lax.ppermute(array, 'grp', swap)  18.5 us
    ppermute x4, waiting for transfers between devices, trade(): return lax.ppermute(array, 'grp', swap)  16.7 us
    all_to_all x3, starting transfers between devices, exchange(): return lax.all_to_all(chunks, 'tile', 0, 0, tiled=True)  15.2 us
    ppermute x2, waiting for transfers between devices, on_device(): lax.ppermute(scalars, 'lev', [(i, i ^ step) for i in range(levels)])  7.96 us
    unnamed x16, local copies, waits for them, and re-layouts  3.58 us
  transfers between devices with their start and end apart: 9, of which 8 were waited for; matrix products, arithmetic and copies ran while one was open for 2% of the time, Pallas kernels for 13%

profile of v5, /device:TPU:32, one launch (start us, length us, event | category | flops | bytes accessed | tf_op | source)
XLA Modules:
  0.0 162.1 jit_solution(13720269756227628459)
XLA Ops:
  2.4 5.5 %other.1 = (f32[576,128]{1,0:T(8,128)S(1)}, f32[48,3072]{1,0:T(8,128)S(1)}) custom-call(s32[1]{0:T(128)} %bitcast.grp_ref, bf16[8,2,48,3072]{3,2,1,0:T(8,128)(2,1)} %members_ref.7, s32[48,3072]{1,0:T(8,128)S(1)} %copy-done.1, s32[768]{0:T(1024)S(1)} %copy-done.6, bf16[4,2,384,896]{3,2,1,0:T(8,128)(2,1)} %constant.33.clone.table_ref), custom_call_target="tpu_custom_call" | custom-call | flops 1 | bytes 1 | tf_op jit(solution)/shard_map/start/other/pallas_call | solution.py:524
  7.9 6.4 %collective-permute-start.1 = (f32[576,128]{1,0:T(8,128)S(1)}, f32[576,128]{1,0:T(8,128)S(1)}, u32[]{:S(2)}, u32[]{:S(2)}) collective-permute-start(f32[576,128]{1,0:T(8,128)S(1)} %get-tuple-element.21), channel_id=1, source_target_pairs={{0,128},{128,0},{1,129},{129,1},{2,130},{130,2},{3,131},{131,3},{4... | collective-permute-start | bytes 884744 | tf_op jit(solution)/shard_map/start/ppermute | solution.py:567
  14.3 6.0 %own.1 = (f32[768,128]{1,0:T(8,128)S(1)}, f32[2,48,3072]{2,1,0:T(8,128)}) custom-call(s32[1]{0:T(128)} %bitcast.grp_ref, bf16[8,2,48,3072]{3,2,1,0:T(8,128)(2,1)} %members_ref.7, f32[2,48,3072]{2,1,0:T(8,128)} %obs_ref.1, s32[48,3072]{1,0:T(8,128)S(1)} %copy-done.1, s32[1,768]{1,0:T(1,128)S(1)} %broadcast_in_dim.13.row_ref, ...), custom_call_target="tpu_custom_call" | custom-call | flops 1 | bytes 1 | tf_op jit(solution)/shard_map/start/own/pallas_call | solution.py:524
  20.4 11.1 %collective-permute-done.1.packed_ref = f32[576,128]{1,0:T(8,128)S(1)} collective-permute-done((f32[576,128]{1,0:T(8,128)S(1)}, f32[576,128]{1,0:T(8,128)S(1)}, u32[]{:S(2)}, u32[]{:S(2)}) %collective-permute-start.1) | collective-permute-done | bytes 294944 | tf_op jit(solution)/shard_map/start/ppermute | solution.py:567
  32.6 7.3 %all-to-all-start = ((f32[32,24,128]{2,1,0:T(8,128)}), f32[32,24,128]{2,1,0:T(8,128)S(1)}, u32[]{:S(2)}, u32[]{:S(2)}) async-start(f32[32,24,128]{2,1,0:T(8,128)} %join.1), calls=%async_computation | async-start | bytes 786432 | tf_op jit(solution)/shard_map/solve/all_to_all | solution.py:586
  41.1 8.8 %all-to-all-done.chunks_ref = f32[32,24,128]{2,1,0:T(8,128)S(1)} async-done(((f32[32,24,128]{2,1,0:T(8,128)}), f32[32,24,128]{2,1,0:T(8,128)S(1)}, u32[]{:S(2)}, u32[]{:S(2)}) %all-to-all-start) | async-done | bytes 393248 | tf_op jit(solution)/shard_map/solve/all_to_all | solution.py:586
  49.9 3.7 %lat1.1 = (f32[48,768]{1,0:T(8,128)S(1)}, f32[32,24,128]{2,1,0:T(8,128)S(1)}) custom-call(f32[32,24,128]{2,1,0:T(8,128)S(1)} %all-to-all-done.chunks_ref, f32[1,768]{1,0:T(1,128)S(1)} %bitcast.13, s32[24,1]{1,0:T(8,128)S(1)} %copy.14.waves_ref, bf16[2,2,384,1024]{3,2,1,0:T(8,128)(2,1)} %constant.34.clone.lat_ref), custom_call_target="tpu_custom_call" | custom-call | flops 1 | bytes 1 | tf_op jit(solution)/shard_map/solve/lat1/pallas_call | solution.py:524
  53.5 13.6 %all_to_all.25.band_ref.first_ref = f32[32,24,128]{2,1,0:T(8,128)S(1)} all-to-all(f32[32,24,128]{2,1,0:T(8,128)S(1)} %get-tuple-element.22), channel_id=1, replica_groups=mesh['grp'=2,'tile'=32,'lev'=4] {'tile'}, dimensions={0} | all-to-all | bytes 786432 | tf_op jit(solution)/shard_map/solve/all_to_all | solution.py:586
  67.2 7.1 %grid.1 = (f32[48,3072]{1,0:T(8,128)S(1)}, f32[32,24,128]{2,1,0:T(8,128)}) custom-call(f32[32,24,128]{2,1,0:T(8,128)S(1)} %all_to_all.25.band_ref.first_ref, s32[48,3072]{1,0:T(8,128)S(1)} %copy-done.2, s32[1,768]{1,0:T(1,128)S(1)} %broadcast_in_dim.13.row_ref, bf16[4,2,384,896]{3,2,1,0:T(8,128)(2,1)} %constant.33.clone.table_ref), custom_call_target="tpu_custom_call" | custom-call | flops 1 | bytes 1 | tf_op jit(solution)/shard_map/solve/grid/pallas_call | solution.py:524
  75.1 3.9 %all-to-all-start.2 = ((f32[32,24,128]{2,1,0:T(8,128)}), f32[32,24,128]{2,1,0:T(8,128)S(1)}, u32[]{:S(2)}, u32[]{:S(2)}) async-start(f32[32,24,128]{2,1,0:T(8,128)} %get-tuple-element.23), calls=%async_computation.2 | async-start | bytes 786432 | tf_op jit(solution)/shard_map/solve/all_to_all | solution.py:586
  79.0 9.9 %all-to-all-done.2.chunks_ref = f32[32,24,128]{2,1,0:T(8,128)S(1)} async-done(((f32[32,24,128]{2,1,0:T(8,128)}), f32[32,24,128]{2,1,0:T(8,128)S(1)}, u32[]{:S(2)}, u32[]{:S(2)}) %all-to-all-start.2) | async-done | bytes 393248 | tf_op jit(solution)/shard_map/solve/all_to_all | solution.py:586
  89.0 4.5 %lat2.1 = (f32[48,768]{1,0:T(8,128)S(1)}, f32[32,24,128]{2,1,0:T(8,128)}, f32[8,128]{1,0:T(8,128)S(1)}) custom-call(f32[32,24,128]{2,1,0:T(8,128)S(1)} %all-to-all-done.2.chunks_ref, f32[1,768]{1,0:T(1,128)S(1)} %bitcast.14, s32[24,1]{1,0:T(8,128)S(1)} %copy.14.waves_ref, f32[48,768]{1,0:T(8,128)S(1)} %get-tuple-element.24.rhs_ref, ...), custom_call_target="tpu_custom_call" | custom-call | flops 1 | bytes 1 | tf_op jit(solution)/shard_map/solve/lat2/pallas_call | solution.py:524
  93.5 4.0 %all-to-all-start.3 = ((f32[32,24,128]{2,1,0:T(8,128)}), f32[32,24,128]{2,1,0:T(8,128)S(1)}, u32[]{:S(2)}, u32[]{:S(2)}) async-start(f32[32,24,128]{2,1,0:T(8,128)} %get-tuple-element.25), calls=%async_computation.3 | async-start | bytes 786432 | tf_op jit(solution)/shard_map/solve/all_to_all | solution.py:586
  97.5 9.9 %all-to-all-done.3.band_ref.second_ref = f32[32,24,128]{2,1,0:T(8,128)S(1)} async-done(((f32[32,24,128]{2,1,0:T(8,128)}), f32[32,24,128]{2,1,0:T(8,128)S(1)}, u32[]{:S(2)}, u32[]{:S(2)}) %all-to-all-start.3) | async-done | bytes 393248 | tf_op jit(solution)/shard_map/solve/all_to_all | solution.py:586
  107.5 5.8 %last.1 = (f32[48,3072]{1,0:T(8,128)S(1)}, f32[32,1,128]{2,1,0:T(1,128)S(1)}) custom-call(s32[1]{0:T(128)} %bitcast.1.level_ref, f32[32,24,128]{2,1,0:T(8,128)S(1)} %all-to-all-done.3.band_ref.second_ref, s32[48,3072]{1,0:T(8,128)S(1)} %copy-done.2, s32[1,768]{1,0:T(1,128)S(1)} %broadcast_in_dim.13.row_ref, ...), custom_call_target="tpu_custom_call" | custom-call | flops 1 | bytes 1 | tf_op jit(solution)/shard_map/solve/last/pallas_call | solution.py:524
  113.3 11.1 %all_to_all.26 = f32[32,1,128]{2,1,0:T(1,128)S(1)} all-to-all(f32[32,1,128]{2,1,0:T(1,128)S(1)} %get-tuple-element.29), channel_id=1, replica_groups=mesh['grp'=2,'tile'=32,'lev'=4] {'tile'}, dimensions={0} | all-to-all | bytes 32768 | tf_op jit(solution)/shard_map/solve/all_to_all | solution.py:586
  124.5 3.5 %collective-permute-done.2 = f32[1,128]{1,0:T(1,128)S(1)} collective-permute-done((f32[1,128]{1,0:T(1,128)S(1)}, f32[1,128]{1,0:T(1,128)S(1)}, u32[]{:S(2)}, u32[]{:S(2)}) %collective-permute-start.2) | collective-permute-done | bytes 544 | tf_op jit(solution)/shard_map/solve/ppermute | solution.py:606
  128.0 4.4 %collective-permute-done.3 = f32[1,128]{1,0:T(1,128)S(1)} collective-permute-done((f32[1,128]{1,0:T(1,128)S(1)}, f32[1,128]{1,0:T(1,128)S(1)}, u32[]{:S(2)}, u32[]{:S(2)}) %collective-permute-start.3) | collective-permute-done | bytes 544 | tf_op jit(solution)/shard_map/solve/ppermute | solution.py:606
  132.5 6.0 %collective-permute-start.4 = (f32[1,128]{1,0:T(1,128)S(1)}, f32[1,128]{1,0:T(1,128)S(1)}, u32[]{:S(2)}, u32[]{:S(2)}) collective-permute-start(f32[1,128]{1,0:T(1,128)S(1)} %add.20.sums_ref), channel_id=1, source_target_pairs={{0,128},{128,0},{1,129},{129,1},{2,130},{130,2},{3,131},{131,3},{4... | collective-permute-start | bytes 1544 | tf_op jit(solution)/shard_map/finish/ppermute | solution.py:567
  138.5 1.5 collective-permute-done.4.sums_in_ref
  140.6 6.0 %collective-permute-start.5 = (f32[576,128]{1,0:T(8,128)S(1)}, f32[576,128]{1,0:T(8,128)S(1)}, u32[]{:S(2)}, u32[]{:S(2)}) collective-permute-start(f32[576,128]{1,0:T(8,128)S(1)} %get-tuple-element.30), channel_id=1, source_target_pairs={{0,128},{128,0},{1,129},{129,1},{2,130},{130,2},{3,131},{131,3},{4... | collective-permute-start | bytes 884744 | tf_op jit(solution)/shard_map/finish/ppermute | solution.py:567
  146.6 3.7 %finish_own.1.half_ref = bf16[8,2,48,3072]{3,2,1,0:T(8,128)(2,1)} custom-call(s32[1]{0:T(128)} %bitcast.grp_ref, bf16[8,2,48,3072]{3,2,1,0:T(8,128)(2,1)} %members_ref.7, f32[2,48,3072]{2,1,0:T(8,128)} %get-tuple-element.19.sums_ref, f32[2,48,3072]{2,1,0:T(8,128)} %collective-permute-done.refs_0_.sums_in_ref, f32[1,128]{1,0:T(1,128)S(1)} %get-tuple-element.31.factors_ref, ...), custom_call_target="tpu_custom_call" | custom-call | flops 1 | bytes 1 | tf_op jit(solution)/shard_map/finish/finish_own/pallas_call | solution.py:524
  152.3 4.0 %collective-permute-done.5.packed_ref = f32[576,128]{1,0:T(8,128)S(1)} collective-permute-done((f32[576,128]{1,0:T(8,128)S(1)}, f32[576,128]{1,0:T(8,128)S(1)}, u32[]{:S(2)}, u32[]{:S(2)}) %collective-permute-start.5) | collective-permute-done | bytes 294944 | tf_op jit(solution)/shard_map/finish/ppermute | solution.py:567
  156.3 5.5 %finish_other.1 = bf16[8,2,48,3072]{3,2,1,0:T(8,128)(2,1)} custom-call(s32[1]{0:T(128)} %bitcast.grp_ref, bf16[8,2,48,3072]{3,2,1,0:T(8,128)(2,1)} %members_ref.7, f32[2,48,3072]{2,1,0:T(8,128)S(1)} %copy-done.3, f32[2,48,3072]{2,1,0:T(8,128)} %collective-permute-done.refs_0_.sums_in_ref, ...), custom_call_target="tpu_custom_call", output_to_operand_aliasing={{}: (7, {})} | custom-call | flops 1 | bytes 1 | tf_op jit(solution)/shard_map/finish/finish_other/pallas_call | solution.py:524
  (34 shorter events, 7.6 us)
Async XLA Ops:
  0.6 40.1 %copy-start = (f32[2,768]{1,0:T(2,128)S(1)}, f32[2,768]{1,0:T(2,128)}, u32[]{:S(2)}) copy-start(f32[2,768]{1,0:T(2,128)} %param.10) | copy-start | bytes 18436
  0.7 1.1 copy-start.1
  1.7 0.7 copy-start.6
  7.9 23.6 %collective-permute-start.1 = (f32[576,128]{1,0:T(8,128)S(1)}, f32[576,128]{1,0:T(8,128)S(1)}, u32[]{:S(2)}, u32[]{:S(2)}) collective-permute-start(f32[576,128]{1,0:T(8,128)S(1)} %get-tuple-element.21), channel_id=1, source_target_pairs={{0,128},{128,0},{1,129},{129,1},{2,130},{130,2},{3,131},{131,3},{4... | collective-permute-start | bytes 884744 | tf_op jit(solution)/shard_map/start/ppermute | solution.py:567
  20.3 46.9 %copy-start.2 = (s32[48,3072]{1,0:T(8,128)S(1)}, s32[48,3072]{1,0:T(8,128)}, u32[]{:S(2)}) copy-start(s32[48,3072]{1,0:T(8,128)} %count_ref.7) | copy-start | bytes 1769476
  20.3 58.7 %collective-permute-start = (f32[2,48,3072]{2,1,0:T(8,128)}, f32[2,48,3072]{2,1,0:T(8,128)}, u32[]{:S(2)}, u32[]{:S(2)}) collective-permute-start(f32[2,48,3072]{2,1,0:T(8,128)} %get-tuple-element.19.sums_ref), channel_id=1, source_target_pairs={{0,128},{128,0},{1,129},{129,1},{2,130},{130,2},{3,131},{131,3},{4... | collective-permute-start | bytes 3538952 | tf_op jit(solution)/shard_map/start/ppermute | solution.py:567
  32.6 17.3 %all-to-all-start = ((f32[32,24,128]{2,1,0:T(8,128)}), f32[32,24,128]{2,1,0:T(8,128)S(1)}, u32[]{:S(2)}, u32[]{:S(2)}) async-start(f32[32,24,128]{2,1,0:T(8,128)} %join.1), calls=%async_computation | async-start | bytes 786432 | tf_op jit(solution)/shard_map/solve/all_to_all | solution.py:586
  74.3 0.8 copy-start.4
  75.1 13.8 %all-to-all-start.2 = ((f32[32,24,128]{2,1,0:T(8,128)}), f32[32,24,128]{2,1,0:T(8,128)S(1)}, u32[]{:S(2)}, u32[]{:S(2)}) async-start(f32[32,24,128]{2,1,0:T(8,128)} %get-tuple-element.23), calls=%async_computation.2 | async-start | bytes 786432 | tf_op jit(solution)/shard_map/solve/all_to_all | solution.py:586
  93.5 53.2 %copy-start.5 = (f32[48,3072]{1,0:T(8,128)S(1)}, f32[48,3072]{1,0:T(8,128)}, u32[]{:S(2)}) copy-start(f32[48,3072]{1,0:T(8,128)} %copy-done.4) | copy-start | bytes 1769476
  93.5 14.0 %all-to-all-start.3 = ((f32[32,24,128]{2,1,0:T(8,128)}), f32[32,24,128]{2,1,0:T(8,128)S(1)}, u32[]{:S(2)}, u32[]{:S(2)}) async-start(f32[32,24,128]{2,1,0:T(8,128)} %get-tuple-element.25), calls=%async_computation.3 | async-start | bytes 786432 | tf_op jit(solution)/shard_map/solve/all_to_all | solution.py:586
  124.4 3.6 %collective-permute-start.2 = (f32[1,128]{1,0:T(1,128)S(1)}, f32[1,128]{1,0:T(1,128)S(1)}, u32[]{:S(2)}, u32[]{:S(2)}) collective-permute-start(f32[1,128]{1,0:T(1,128)S(1)} %bitcast.18), channel_id=1, source_target_pairs={{0,1},{1,0},{2,3},{3,2},{4,5},{5,4},{6,7},{7,6},{8,9},{9,8},{10,11... | collective-permute-start | bytes 1544 | tf_op jit(solution)/shard_map/solve/ppermute | solution.py:606
  128.0 4.4 %collective-permute-start.3 = (f32[1,128]{1,0:T(1,128)S(1)}, f32[1,128]{1,0:T(1,128)S(1)}, u32[]{:S(2)}, u32[]{:S(2)}) collective-permute-start(f32[1,128]{1,0:T(1,128)S(1)} %bitcast_add_fusion), channel_id=1, source_target_pairs={{0,2},{1,3},{2,0},{3,1},{4,6},{5,7},{6,4},{7,5},{8,10},{9,11},{10,... | collective-permute-start | bytes 1544 | tf_op jit(solution)/shard_map/solve/ppermute | solution.py:606
  132.5 7.5 %collective-permute-start.4 = (f32[1,128]{1,0:T(1,128)S(1)}, f32[1,128]{1,0:T(1,128)S(1)}, u32[]{:S(2)}, u32[]{:S(2)}) collective-permute-start(f32[1,128]{1,0:T(1,128)S(1)} %add.20.sums_ref), channel_id=1, source_target_pairs={{0,128},{128,0},{1,129},{129,1},{2,130},{130,2},{3,131},{131,3},{4... | collective-permute-start | bytes 1544 | tf_op jit(solution)/shard_map/finish/ppermute | solution.py:567
  140.6 15.7 %collective-permute-start.5 = (f32[576,128]{1,0:T(8,128)S(1)}, f32[576,128]{1,0:T(8,128)S(1)}, u32[]{:S(2)}, u32[]{:S(2)}) collective-permute-start(f32[576,128]{1,0:T(8,128)S(1)} %get-tuple-element.30), channel_id=1, source_target_pairs={{0,128},{128,0},{1,129},{129,1},{2,130},{130,2},{3,131},{131,3},{4... | collective-permute-start | bytes 884744 | tf_op jit(solution)/shard_map/finish/ppermute | solution.py:567
  146.6 9.7 %copy-start.3 = (f32[2,48,3072]{2,1,0:T(8,128)S(1)}, f32[2,48,3072]{2,1,0:T(8,128)}, u32[]{:S(2)}) copy-start(f32[2,48,3072]{2,1,0:T(8,128)} %get-tuple-element.19.sums_ref) | copy-start | bytes 3538948

commit v6 on v5

--- a/solution.py
+++ b/solution.py
@@ -401,7 +401,7 @@
 
 def grid_kernel(band_ref, count_ref, row_ref, table_ref, *refs):
     field_ref, out_ref, held, semaphores = refs[-4:]
-    table = Loaded(table_ref, held, semaphores, GROUPS)
+    table = Loaded(table_ref, held, semaphores, GROUPS, ahead=len(GROUPS))
     bands, slots, _ = band_ref.shape
     rows, lon = count_ref.shape
     row = row_ref[...]
@@ -414,7 +414,7 @@
 
 def last_kernel(level_ref, band_ref, count_ref, row_ref, table_ref, field_ref, rhs_ref, image_ref, quotient_ref, *refs):
     next_ref, sums_ref, held, semaphores = refs[-4:]
-    table = Loaded(table_ref, held, semaphores, GROUPS)
+    table = Loaded(table_ref, held, semaphores, GROUPS, ahead=len(GROUPS))
     bands, slots, _ = band_ref.shape
     rows, lon = count_ref.shape
     rhs, image, start = rhs_ref[...], image_ref[...], field_ref[...]

time: 163 us -> 162 us (level)
  no operation moved by 1% of the time
where the time goes in v6:
time: 162 us
  waiting for transfers between devices  53.3 us (33%)
  Pallas kernels  43 us (27%)
  starting transfers between devices  33.8 us (21%)
  blocking collectives  24.7 us (15%)
  local copies, waits for them, and re-layouts  5.69 us (4%)
    pallas_call x10, Pallas kernels, run(): pl.pallas_call(kernel, out_shape=outs, in_specs=[pl.BlockSpec(memory_spac...  43 us
    all_to_all x3, waiting for transfers between devices, exchange(): return lax.all_to_all(chunks, 'tile', 0, 0, tiled=True)  28.7 us
    all_to_all x2, blocking collectives, exchange(): return lax.all_to_all(chunks, 'tile', 0, 0, tiled=True)  24.7 us
    ppermute x4, starting transfers between devices, trade(): return lax.ppermute(array, 'grp', swap)  18.5 us
    ppermute x4, waiting for transfers between devices, trade(): return lax.ppermute(array, 'grp', swap)  16.7 us
    all_to_all x3, starting transfers between devices, exchange(): return lax.all_to_all(chunks, 'tile', 0, 0, tiled=True)  15.3 us
    ppermute x2, waiting for transfers between devices, on_device(): lax.ppermute(scalars, 'lev', [(i, i ^ step) for i in range(levels)])  7.96 us
    unnamed x16, local copies, waits for them, and re-layouts  3.58 us
  transfers between devices with their start and end apart: 9, of which 8 were waited for; matrix products, arithmetic and copies ran while one was open for 2% of the time, Pallas kernels for 13%

profile of v6, /device:TPU:32, one launch (start us, length us, event | category | flops | bytes accessed | tf_op | source)
XLA Modules:
  0.0 161.6 jit_solution(6861789333798900467)
XLA Ops:
  2.4 5.5 %other.1 = (f32[576,128]{1,0:T(8,128)S(1)}, f32[48,3072]{1,0:T(8,128)S(1)}) custom-call(s32[1]{0:T(128)} %bitcast.grp_ref, bf16[8,2,48,3072]{3,2,1,0:T(8,128)(2,1)} %members_ref.7, s32[48,3072]{1,0:T(8,128)S(1)} %copy-done.1, s32[768]{0:T(1024)S(1)} %copy-done.6, bf16[4,2,384,896]{3,2,1,0:T(8,128)(2,1)} %constant.33.clone.table_ref), custom_call_target="tpu_custom_call" | custom-call | flops 1 | bytes 1 | tf_op jit(solution)/shard_map/start/other/pallas_call | solution.py:524
  7.9 6.4 %collective-permute-start.1 = (f32[576,128]{1,0:T(8,128)S(1)}, f32[576,128]{1,0:T(8,128)S(1)}, u32[]{:S(2)}, u32[]{:S(2)}) collective-permute-start(f32[576,128]{1,0:T(8,128)S(1)} %get-tuple-element.21), channel_id=1, source_target_pairs={{0,128},{128,0},{1,129},{129,1},{2,130},{130,2},{3,131},{131,3},{4... | collective-permute-start | bytes 884744 | tf_op jit(solution)/shard_map/start/ppermute | solution.py:567
  14.3 6.0 %own.1 = (f32[768,128]{1,0:T(8,128)S(1)}, f32[2,48,3072]{2,1,0:T(8,128)}) custom-call(s32[1]{0:T(128)} %bitcast.grp_ref, bf16[8,2,48,3072]{3,2,1,0:T(8,128)(2,1)} %members_ref.7, f32[2,48,3072]{2,1,0:T(8,128)} %obs_ref.1, s32[48,3072]{1,0:T(8,128)S(1)} %copy-done.1, s32[1,768]{1,0:T(1,128)S(1)} %broadcast_in_dim.13.row_ref, ...), custom_call_target="tpu_custom_call" | custom-call | flops 1 | bytes 1 | tf_op jit(solution)/shard_map/start/own/pallas_call | solution.py:524
  20.4 11.1 %collective-permute-done.1.packed_ref = f32[576,128]{1,0:T(8,128)S(1)} collective-permute-done((f32[576,128]{1,0:T(8,128)S(1)}, f32[576,128]{1,0:T(8,128)S(1)}, u32[]{:S(2)}, u32[]{:S(2)}) %collective-permute-start.1) | collective-permute-done | bytes 294944 | tf_op jit(solution)/shard_map/start/ppermute | solution.py:567
  32.6 7.3 %all-to-all-start = ((f32[32,24,128]{2,1,0:T(8,128)}), f32[32,24,128]{2,1,0:T(8,128)S(1)}, u32[]{:S(2)}, u32[]{:S(2)}) async-start(f32[32,24,128]{2,1,0:T(8,128)} %join.1), calls=%async_computation | async-start | bytes 786432 | tf_op jit(solution)/shard_map/solve/all_to_all | solution.py:586
  41.1 8.8 %all-to-all-done.chunks_ref = f32[32,24,128]{2,1,0:T(8,128)S(1)} async-done(((f32[32,24,128]{2,1,0:T(8,128)}), f32[32,24,128]{2,1,0:T(8,128)S(1)}, u32[]{:S(2)}, u32[]{:S(2)}) %all-to-all-start) | async-done | bytes 393248 | tf_op jit(solution)/shard_map/solve/all_to_all | solution.py:586
  49.9 3.7 %lat1.1 = (f32[48,768]{1,0:T(8,128)S(1)}, f32[32,24,128]{2,1,0:T(8,128)S(1)}) custom-call(f32[32,24,128]{2,1,0:T(8,128)S(1)} %all-to-all-done.chunks_ref, f32[1,768]{1,0:T(1,128)S(1)} %bitcast.13, s32[24,1]{1,0:T(8,128)S(1)} %copy.14.waves_ref, bf16[2,2,384,1024]{3,2,1,0:T(8,128)(2,1)} %constant.34.clone.lat_ref), custom_call_target="tpu_custom_call" | custom-call | flops 1 | bytes 1 | tf_op jit(solution)/shard_map/solve/lat1/pallas_call | solution.py:524
  53.5 13.6 %all_to_all.25.band_ref.first_ref = f32[32,24,128]{2,1,0:T(8,128)S(1)} all-to-all(f32[32,24,128]{2,1,0:T(8,128)S(1)} %get-tuple-element.22), channel_id=1, replica_groups=mesh['grp'=2,'tile'=32,'lev'=4] {'tile'}, dimensions={0} | all-to-all | bytes 786432 | tf_op jit(solution)/shard_map/solve/all_to_all | solution.py:586
  67.2 6.9 %grid.1 = (f32[48,3072]{1,0:T(8,128)S(1)}, f32[32,24,128]{2,1,0:T(8,128)}) custom-call(f32[32,24,128]{2,1,0:T(8,128)S(1)} %all_to_all.25.band_ref.first_ref, s32[48,3072]{1,0:T(8,128)S(1)} %copy-done.2, s32[1,768]{1,0:T(1,128)S(1)} %broadcast_in_dim.13.row_ref, bf16[4,2,384,896]{3,2,1,0:T(8,128)(2,1)} %constant.33.clone.table_ref), custom_call_target="tpu_custom_call" | custom-call | flops 1 | bytes 1 | tf_op jit(solution)/shard_map/solve/grid/pallas_call | solution.py:524
  74.9 3.9 %all-to-all-start.2 = ((f32[32,24,128]{2,1,0:T(8,128)}), f32[32,24,128]{2,1,0:T(8,128)S(1)}, u32[]{:S(2)}, u32[]{:S(2)}) async-start(f32[32,24,128]{2,1,0:T(8,128)} %get-tuple-element.23), calls=%async_computation.2 | async-start | bytes 786432 | tf_op jit(solution)/shard_map/solve/all_to_all | solution.py:586
  78.8 9.9 %all-to-all-done.2.chunks_ref = f32[32,24,128]{2,1,0:T(8,128)S(1)} async-done(((f32[32,24,128]{2,1,0:T(8,128)}), f32[32,24,128]{2,1,0:T(8,128)S(1)}, u32[]{:S(2)}, u32[]{:S(2)}) %all-to-all-start.2) | async-done | bytes 393248 | tf_op jit(solution)/shard_map/solve/all_to_all | solution.py:586
  88.7 4.5 %lat2.1 = (f32[48,768]{1,0:T(8,128)S(1)}, f32[32,24,128]{2,1,0:T(8,128)}, f32[8,128]{1,0:T(8,128)S(1)}) custom-call(f32[32,24,128]{2,1,0:T(8,128)S(1)} %all-to-all-done.2.chunks_ref, f32[1,768]{1,0:T(1,128)S(1)} %bitcast.14, s32[24,1]{1,0:T(8,128)S(1)} %copy.14.waves_ref, f32[48,768]{1,0:T(8,128)S(1)} %get-tuple-element.24.rhs_ref, ...), custom_call_target="tpu_custom_call" | custom-call | flops 1 | bytes 1 | tf_op jit(solution)/shard_map/solve/lat2/pallas_call | solution.py:524
  93.3 4.0 %all-to-all-start.3 = ((f32[32,24,128]{2,1,0:T(8,128)}), f32[32,24,128]{2,1,0:T(8,128)S(1)}, u32[]{:S(2)}, u32[]{:S(2)}) async-start(f32[32,24,128]{2,1,0:T(8,128)} %get-tuple-element.25), calls=%async_computation.3 | async-start | bytes 786432 | tf_op jit(solution)/shard_map/solve/all_to_all | solution.py:586
  97.3 9.9 %all-to-all-done.3.band_ref.second_ref = f32[32,24,128]{2,1,0:T(8,128)S(1)} async-done(((f32[32,24,128]{2,1,0:T(8,128)}), f32[32,24,128]{2,1,0:T(8,128)S(1)}, u32[]{:S(2)}, u32[]{:S(2)}) %all-to-all-start.3) | async-done | bytes 393248 | tf_op jit(solution)/shard_map/solve/all_to_all | solution.py:586
  107.3 5.6 %last.1 = (f32[48,3072]{1,0:T(8,128)S(1)}, f32[32,1,128]{2,1,0:T(1,128)S(1)}) custom-call(s32[1]{0:T(128)} %bitcast.1.level_ref, f32[32,24,128]{2,1,0:T(8,128)S(1)} %all-to-all-done.3.band_ref.second_ref, s32[48,3072]{1,0:T(8,128)S(1)} %copy-done.2, s32[1,768]{1,0:T(1,128)S(1)} %broadcast_in_dim.13.row_ref, ...), custom_call_target="tpu_custom_call" | custom-call | flops 1 | bytes 1 | tf_op jit(solution)/shard_map/solve/last/pallas_call | solution.py:524
  112.8 11.1 %all_to_all.26 = f32[32,1,128]{2,1,0:T(1,128)S(1)} all-to-all(f32[32,1,128]{2,1,0:T(1,128)S(1)} %get-tuple-element.29), channel_id=1, replica_groups=mesh['grp'=2,'tile'=32,'lev'=4] {'tile'}, dimensions={0} | all-to-all | bytes 32768 | tf_op jit(solution)/shard_map/solve/all_to_all | solution.py:586
  124.1 3.5 %collective-permute-done.2 = f32[1,128]{1,0:T(1,128)S(1)} collective-permute-done((f32[1,128]{1,0:T(1,128)S(1)}, f32[1,128]{1,0:T(1,128)S(1)}, u32[]{:S(2)}, u32[]{:S(2)}) %collective-permute-start.2) | collective-permute-done | bytes 544 | tf_op jit(solution)/shard_map/solve/ppermute | solution.py:606
  127.6 4.4 %collective-permute-done.3 = f32[1,128]{1,0:T(1,128)S(1)} collective-permute-done((f32[1,128]{1,0:T(1,128)S(1)}, f32[1,128]{1,0:T(1,128)S(1)}, u32[]{:S(2)}, u32[]{:S(2)}) %collective-permute-start.3) | collective-permute-done | bytes 544 | tf_op jit(solution)/shard_map/solve/ppermute | solution.py:606
  132.0 6.0 %collective-permute-start.4 = (f32[1,128]{1,0:T(1,128)S(1)}, f32[1,128]{1,0:T(1,128)S(1)}, u32[]{:S(2)}, u32[]{:S(2)}) collective-permute-start(f32[1,128]{1,0:T(1,128)S(1)} %add.20.sums_ref), channel_id=1, source_target_pairs={{0,128},{128,0},{1,129},{129,1},{2,130},{130,2},{3,131},{131,3},{4... | collective-permute-start | bytes 1544 | tf_op jit(solution)/shard_map/finish/ppermute | solution.py:567
  138.0 1.5 collective-permute-done.4.sums_in_ref
  140.1 6.0 %collective-permute-start.5 = (f32[576,128]{1,0:T(8,128)S(1)}, f32[576,128]{1,0:T(8,128)S(1)}, u32[]{:S(2)}, u32[]{:S(2)}) collective-permute-start(f32[576,128]{1,0:T(8,128)S(1)} %get-tuple-element.30), channel_id=1, source_target_pairs={{0,128},{128,0},{1,129},{129,1},{2,130},{130,2},{3,131},{131,3},{4... | collective-permute-start | bytes 884744 | tf_op jit(solution)/shard_map/finish/ppermute | solution.py:567
  146.1 3.7 %finish_own.1.half_ref = bf16[8,2,48,3072]{3,2,1,0:T(8,128)(2,1)} custom-call(s32[1]{0:T(128)} %bitcast.grp_ref, bf16[8,2,48,3072]{3,2,1,0:T(8,128)(2,1)} %members_ref.7, f32[2,48,3072]{2,1,0:T(8,128)} %get-tuple-element.19.sums_ref, f32[2,48,3072]{2,1,0:T(8,128)} %collective-permute-done.refs_0_.sums_in_ref, f32[1,128]{1,0:T(1,128)S(1)} %get-tuple-element.31.factors_ref, ...), custom_call_target="tpu_custom_call" | custom-call | flops 1 | bytes 1 | tf_op jit(solution)/shard_map/finish/finish_own/pallas_call | solution.py:524
  151.8 4.0 %collective-permute-done.5.packed_ref = f32[576,128]{1,0:T(8,128)S(1)} collective-permute-done((f32[576,128]{1,0:T(8,128)S(1)}, f32[576,128]{1,0:T(8,128)S(1)}, u32[]{:S(2)}, u32[]{:S(2)}) %collective-permute-start.5) | collective-permute-done | bytes 294944 | tf_op jit(solution)/shard_map/finish/ppermute | solution.py:567
  155.9 5.5 %finish_other.1 = bf16[8,2,48,3072]{3,2,1,0:T(8,128)(2,1)} custom-call(s32[1]{0:T(128)} %bitcast.grp_ref, bf16[8,2,48,3072]{3,2,1,0:T(8,128)(2,1)} %members_ref.7, f32[2,48,3072]{2,1,0:T(8,128)S(1)} %copy-done.3, f32[2,48,3072]{2,1,0:T(8,128)} %collective-permute-done.refs_0_.sums_in_ref, ...), custom_call_target="tpu_custom_call", output_to_operand_aliasing={{}: (7, {})} | custom-call | flops 1 | bytes 1 | tf_op jit(solution)/shard_map/finish/finish_other/pallas_call | solution.py:524
  (34 shorter events, 7.6 us)
Async XLA Ops:
  0.6 40.1 %copy-start = (f32[2,768]{1,0:T(2,128)S(1)}, f32[2,768]{1,0:T(2,128)}, u32[]{:S(2)}) copy-start(f32[2,768]{1,0:T(2,128)} %param.10) | copy-start | bytes 18436
  0.7 1.1 copy-start.1
  1.7 0.7 copy-start.6
  7.9 23.6 %collective-permute-start.1 = (f32[576,128]{1,0:T(8,128)S(1)}, f32[576,128]{1,0:T(8,128)S(1)}, u32[]{:S(2)}, u32[]{:S(2)}) collective-permute-start(f32[576,128]{1,0:T(8,128)S(1)} %get-tuple-element.21), channel_id=1, source_target_pairs={{0,128},{128,0},{1,129},{129,1},{2,130},{130,2},{3,131},{131,3},{4... | collective-permute-start | bytes 884744 | tf_op jit(solution)/shard_map/start/ppermute | solution.py:567
  20.3 46.9 %copy-start.2 = (s32[48,3072]{1,0:T(8,128)S(1)}, s32[48,3072]{1,0:T(8,128)}, u32[]{:S(2)}) copy-start(s32[48,3072]{1,0:T(8,128)} %count_ref.7) | copy-start | bytes 1769476
  20.3 58.5 %collective-permute-start = (f32[2,48,3072]{2,1,0:T(8,128)}, f32[2,48,3072]{2,1,0:T(8,128)}, u32[]{:S(2)}, u32[]{:S(2)}) collective-permute-start(f32[2,48,3072]{2,1,0:T(8,128)} %get-tuple-element.19.sums_ref), channel_id=1, source_target_pairs={{0,128},{128,0},{1,129},{129,1},{2,130},{130,2},{3,131},{131,3},{4... | collective-permute-start | bytes 3538952 | tf_op jit(solution)/shard_map/start/ppermute | solution.py:567
  32.6 17.3 %all-to-all-start = ((f32[32,24,128]{2,1,0:T(8,128)}), f32[32,24,128]{2,1,0:T(8,128)S(1)}, u32[]{:S(2)}, u32[]{:S(2)}) async-start(f32[32,24,128]{2,1,0:T(8,128)} %join.1), calls=%async_computation | async-start | bytes 786432 | tf_op jit(solution)/shard_map/solve/all_to_all | solution.py:586
  74.1 0.8 copy-start.4
  74.9 13.9 %all-to-all-start.2 = ((f32[32,24,128]{2,1,0:T(8,128)}), f32[32,24,128]{2,1,0:T(8,128)S(1)}, u32[]{:S(2)}, u32[]{:S(2)}) async-start(f32[32,24,128]{2,1,0:T(8,128)} %get-tuple-element.23), calls=%async_computation.2 | async-start | bytes 786432 | tf_op jit(solution)/shard_map/solve/all_to_all | solution.py:586
  93.2 52.9 %copy-start.5 = (f32[48,3072]{1,0:T(8,128)S(1)}, f32[48,3072]{1,0:T(8,128)}, u32[]{:S(2)}) copy-start(f32[48,3072]{1,0:T(8,128)} %copy-done.4) | copy-start | bytes 1769476
  93.3 14.0 %all-to-all-start.3 = ((f32[32,24,128]{2,1,0:T(8,128)}), f32[32,24,128]{2,1,0:T(8,128)S(1)}, u32[]{:S(2)}, u32[]{:S(2)}) async-start(f32[32,24,128]{2,1,0:T(8,128)} %get-tuple-element.25), calls=%async_computation.3 | async-start | bytes 786432 | tf_op jit(solution)/shard_map/solve/all_to_all | solution.py:586
  124.0 3.6 %collective-permute-start.2 = (f32[1,128]{1,0:T(1,128)S(1)}, f32[1,128]{1,0:T(1,128)S(1)}, u32[]{:S(2)}, u32[]{:S(2)}) collective-permute-start(f32[1,128]{1,0:T(1,128)S(1)} %bitcast.18), channel_id=1, source_target_pairs={{0,1},{1,0},{2,3},{3,2},{4,5},{5,4},{6,7},{7,6},{8,9},{9,8},{10,11... | collective-permute-start | bytes 1544 | tf_op jit(solution)/shard_map/solve/ppermute | solution.py:606
  127.6 4.4 %collective-permute-start.3 = (f32[1,128]{1,0:T(1,128)S(1)}, f32[1,128]{1,0:T(1,128)S(1)}, u32[]{:S(2)}, u32[]{:S(2)}) collective-permute-start(f32[1,128]{1,0:T(1,128)S(1)} %bitcast_add_fusion), channel_id=1, source_target_pairs={{0,2},{1,3},{2,0},{3,1},{4,6},{5,7},{6,4},{7,5},{8,10},{9,11},{10,... | collective-permute-start | bytes 1544 | tf_op jit(solution)/shard_map/solve/ppermute | solution.py:606
  132.0 7.5 %collective-permute-start.4 = (f32[1,128]{1,0:T(1,128)S(1)}, f32[1,128]{1,0:T(1,128)S(1)}, u32[]{:S(2)}, u32[]{:S(2)}) collective-permute-start(f32[1,128]{1,0:T(1,128)S(1)} %add.20.sums_ref), channel_id=1, source_target_pairs={{0,128},{128,0},{1,129},{129,1},{2,130},{130,2},{3,131},{131,3},{4... | collective-permute-start | bytes 1544 | tf_op jit(solution)/shard_map/finish/ppermute | solution.py:567
  140.1 15.7 %collective-permute-start.5 = (f32[576,128]{1,0:T(8,128)S(1)}, f32[576,128]{1,0:T(8,128)S(1)}, u32[]{:S(2)}, u32[]{:S(2)}) collective-permute-start(f32[576,128]{1,0:T(8,128)S(1)} %get-tuple-element.30), channel_id=1, source_target_pairs={{0,128},{128,0},{1,129},{129,1},{2,130},{130,2},{3,131},{131,3},{4... | collective-permute-start | bytes 884744 | tf_op jit(solution)/shard_map/finish/ppermute | solution.py:567
  146.1 9.7 %copy-start.3 = (f32[2,48,3072]{2,1,0:T(8,128)S(1)}, f32[2,48,3072]{2,1,0:T(8,128)}, u32[]{:S(2)}) copy-start(f32[2,48,3072]{2,1,0:T(8,128)} %get-tuple-element.19.sums_ref) | copy-start | bytes 3538948
